TPU v7x, 32 devices: a whole 2x2x4 slice. The times are simulated.
32 devices in a mesh: groups: 2 (over y), rows: 4 (over z), proj: 4 (over x, core).
Axes of the slice: x: 2, y: 2, z: 4, core: 2. Of those that a mesh axis runs over, the one named last changes fastest.
Arguments:
- targets: bfloat16 [256, 8192], P('proj', 'rows'), may hold values from -6 to 6
- precond: bfloat16 [16384, 8192], P(('groups', 'rows'), 'proj'), parts along dimension 0, may hold values from -0.0625 to 0.0625
- train_grads: bfloat16 [12288, 8192], P(('groups', 'rows'), 'proj'), parts along dimension 0, may hold values from -0.0625 to 0.0625
Outputs:
- scores: float32 [256, 12288], P('proj', ('groups', 'rows')), parts along dimension 1
There are 2 independent parts, one for each index of `groups`. A program takes and returns all parts, laid end to end along the dimension named above; an argument that names none is the same for every part. Nothing has to cross between parts.
All inputs are finite; a program needn't handle non-finite values.
Results may differ from a plain program's by a relative error of at most 0.015.
Values may be sent and summed in bfloat16 or wider, within the bound.
No kernel may reach another device: no remote copies, remote signals or barrier semaphores. Data moves between devices by JAX's collectives and lax.ppermute only.
A program may use at most 64 MiB of HBM per device.

v0:
```python
import jax
import jax.numpy as jnp
from jax import lax
from jax.sharding import PartitionSpec as P


def body(targets, precond, train_grads):
    all_targets = lax.all_gather(targets, "proj", axis=0, tiled=True)
    share = lax.psum_scatter(
        jnp.dot(all_targets, precond, preferred_element_type=jnp.float32).astype(jnp.bfloat16),
        "rows",
        scatter_dimension=0,
        tiled=True,
    )
    conditioned = lax.all_gather(share, "rows", axis=0, tiled=True)
    partial_value = lax.dot_general(
        conditioned, train_grads, (((1,), (1,)), ((), ())), preferred_element_type=jnp.float32
    )
    return lax.psum_scatter(
        partial_value.astype(jnp.bfloat16), "proj", scatter_dimension=0, tiled=True
    ).astype(jnp.float32)


def solution(mesh):
    return jax.shard_map(
        body,
        mesh=mesh,
        in_specs=(P("proj", "rows"), P(("groups", "rows"), "proj"), P(("groups", "rows"), "proj")),
        out_specs=P("proj", ("groups", "rows")),
        check_vma=False,
    )
```

profile of v0, /device:TPU:0, one launch (start us, length us, event | category | flops | bytes accessed | tf_op | source)
XLA Modules:
  0.0 128.0 jit_solution(1492285723351271252)
XLA Ops:
  6.5 0.0 all-gather.3.cloned.1.call-start
  6.5 0.7 all-gather.3.cloned.1.call-update
  7.3 0.0 reduce-scatter.3.cloned.1.call-start
  7.3 21.1 %all-gather.3.cloned.1.call-done = bf16[256,2048]{1,0:T(8,128)(2,1)} async-done(((bf16[64,2048]{1,0:T(8,128)(2,1)}), bf16[256,2048]{1,0:T(8,128)(2,1)}) %all-gather.3.cloned.1.call-update) | async-done | bytes 1048592 | tf_op jit(solution)/shard_map/all_gather | solution.py:8
  28.4 7.0 %convolution_convert_fusion.1 = bf16[256,2048]{1,0:T(8,128)(2,1)} fusion(bf16[256,2048]{1,0:T(8,128)(2,1)} %all-gather.3.cloned.1.call-done, bf16[2048,2048]{1,0:T(8,128)(2,1)} %param.4), kind=kOutput, calls=%fused_computation.1 | convolution fusion | flops 2148007936 | bytes 10485760 | tf_op jit(solution)/shard_map/dot_general | solution.py:10
  35.4 0.0 reduce-scatter.3.cloned.1.call-update
  35.4 0.0 all-gather.5.cloned.1.call-start
  35.5 27.2 %reduce-scatter.3.cloned.1.call-done = bf16[64,2048]{1,0:T(8,128)(2,1)} async-done(((bf16[256,2048]{1,0:T(8,128)(2,1)}), bf16[64,2048]{1,0:T(8,128)(2,1)}) %reduce-scatter.3.cloned.1.call-update) | async-done | bytes 262160 | tf_op jit(solution)/shard_map/reduce_scatter | solution.py:9
  62.7 0.0 all-gather.5.cloned.1.call-update
  62.7 0.0 reduce-scatter.5.cloned.1.call-start
  62.8 28.2 %all-gather.5.cloned.1.call-done = bf16[256,2048]{1,0:T(8,128)(2,1)} async-done(((bf16[64,2048]{1,0:T(8,128)(2,1)}), bf16[256,2048]{1,0:T(8,128)(2,1)}) %all-gather.5.cloned.1.call-update) | async-done | bytes 1048592 | tf_op jit(solution)/shard_map/all_gather | solution.py:15
  91.0 5.9 %convolution_convert_fusion = bf16[256,1536]{1,0:T(8,128)(2,1)} fusion(bf16[256,2048]{1,0:T(8,128)(2,1)} %all-gather.5.cloned.1.call-done, bf16[1536,2048]{1,0:T(8,128)(2,1)} %param.5), kind=kOutput, calls=%fused_computation | convolution fusion | flops 1611005952 | bytes 8126464 | tf_op jit(solution)/shard_map/dot_general | solution.py:16
  96.8 0.0 reduce-scatter.5.cloned.1.call-update
  96.9 22.9 %reduce-scatter.5.cloned.1.call-done = bf16[64,1536]{1,0:T(8,128)(2,1)} async-done(((bf16[256,1536]{1,0:T(8,128)(2,1)}), bf16[64,1536]{1,0:T(8,128)(2,1)}) %reduce-scatter.5.cloned.1.call-update) | async-done | bytes 196624 | tf_op jit(solution)/shard_map/reduce_scatter | solution.py:19
  119.8 1.7 %convert_element_type.11 = f32[64,1536]{1,0:T(8,128)} convert(bf16[64,1536]{1,0:T(8,128)(2,1)} %reduce-scatter.5.cloned.1.call-done) | non-fusion elementwise | flops 98304 | bytes 589824 | tf_op jit(solution)/shard_map/convert_element_type | solution.py:21
Async XLA Ops:
  6.5 21.8 %all-gather.3.cloned.1.call-start = ((), (), s32[]{:S(2)}) async-start(), calls=%async_computation.2 | async-start | bytes 1310720 | tf_op jit(solution)/shard_map/all_gather | solution.py:8
  7.3 55.5 %reduce-scatter.3.cloned.1.call-start = ((), (), s32[]{:S(2)}) async-start(), calls=%async_computation.3 | async-start | bytes 1310720 | tf_op jit(solution)/shard_map/reduce_scatter | solution.py:9
  35.4 55.6 %all-gather.5.cloned.1.call-start = ((), (), s32[]{:S(2)}) async-start(), calls=%async_computation.4 | async-start | bytes 1310720 | tf_op jit(solution)/shard_map/all_gather | solution.py:15
  62.7 57.0 %reduce-scatter.5.cloned.1.call-start = ((), (), s32[]{:S(2)}) async-start(), calls=%async_computation.5 | async-start | bytes 983040 | tf_op jit(solution)/shard_map/reduce_scatter | solution.py:19
Sparse Core Ops, SparseCore 0:
  8.9 19.4 all-gather.2
  35.5 27.1 reduce-scatter.2
  64.4 26.5 all-gather.4
  97.0 22.7 reduce-scatter.4
where the time goes:
time: 128 us
  waiting for transfers between devices  100 us (78%)
  between operations  13.1 us (10%)
  matrix products  12.9 us (10%)
  other arithmetic  1.7 us (1%)
    all_gather x1, waiting for transfers between devices, body(): conditioned = lax.all_gather(share, 'rows', axis=0, tiled=True)  28.2 us
    reduce_scatter x1, waiting for transfers between devices, body(): lax.psum_scatter(jnp.dot(all_targets, precond, preferred_element_type=jnp...  27.2 us
    reduce_scatter x1, waiting for transfers between devices, body(): lax.psum_scatter(partial_value.astype(jnp.bfloat16), 'proj', scatter_dime...  22.9 us
    all_gather x1, waiting for transfers between devices, body(): all_targets = lax.all_gather(targets, 'proj', axis=0, tiled=True)  21.1 us
    dot_general x1, matrix products, body(): jnp.dot(all_targets, precond, preferred_element_type=jnp.float32)  7.02 us
    dot_general x1, matrix products, body(): lax.dot_general(conditioned, train_grads, (((1,), (1,)), ((), ())), prefe...  5.86 us
  transfers between devices with their start and end apart: 4, of which 4 were waited for; matrix products, arithmetic and copies ran while one was open for 0% of the time, Pallas kernels for 0%

commit v1 on v0

v1 whole, which is shorter than its diff:
```python
import jax
import jax.numpy as jnp
from jax import lax
from jax.experimental import pallas as pl
from jax.experimental.pallas import tpu as pltpu
from jax.sharding import PartitionSpec as P

VMEM = pl.BlockSpec(memory_space=pltpu.VMEM)
SMEM = pl.BlockSpec(memory_space=pltpu.SMEM)
LIMIT = pltpu.CompilerParams(vmem_limit_bytes=32 << 20)
BF16, F32 = jnp.bfloat16, jnp.float32


def apply_precond(rows, precond):
    m, n = rows.shape[0], precond.shape[1]
    step = min(n, 512)

    def kernel(rows_ref, precond_ref, out_ref):
        for at in range(0, n, step):
            out_ref[:, at : at + step] = jnp.dot(
                rows_ref[...], precond_ref[:, at : at + step], preferred_element_type=F32
            ).astype(BF16)

    return pl.pallas_call(
        kernel,
        out_shape=jax.ShapeDtypeStruct((m, n), BF16),
        in_specs=[VMEM, VMEM],
        out_specs=VMEM,
        compiler_params=LIMIT,
        cost_estimate=pl.CostEstimate(
            flops=2 * m * precond.size, bytes_accessed=precond.size * 2, transcendentals=0
        ),
    )(rows, precond)


def score(outer, kept, given, train):
    m, n = kept.shape[0], train.shape[0]
    step = n // 3

    def kernel(outer_ref, kept_ref, given_ref, train_ref, out_ref):
        left = jnp.where(outer_ref[0] == 1, given_ref[...], kept_ref[...])
        for at in range(0, n, step):
            out_ref[:, at : at + step] = lax.dot_general(
                left, train_ref[at : at + step, :], (((1,), (1,)), ((), ())), preferred_element_type=F32
            ).astype(BF16)

    return pl.pallas_call(
        kernel,
        out_shape=jax.ShapeDtypeStruct((m, n), BF16),
        in_specs=[SMEM, VMEM, VMEM, VMEM],
        out_specs=VMEM,
        compiler_params=LIMIT,
        cost_estimate=pl.CostEstimate(
            flops=2 * m * train.size, bytes_accessed=train.size * 2, transcendentals=0
        ),
    )(outer, kept, given, train)


def add(a, b):
    def kernel(a_ref, b_ref, out_ref):
        out_ref[...] = (a_ref[...].astype(F32) + b_ref[...].astype(F32)).astype(BF16)

    return pl.pallas_call(
        kernel,
        out_shape=jax.ShapeDtypeStruct(a.shape, BF16),
        in_specs=[VMEM, VMEM],
        out_specs=VMEM,
        compiler_params=LIMIT,
    )(a, b)


def make_body(n_rows, n_proj):
    half = n_rows // 2
    inward = [[(h, h + 1), (n_rows - 1 - h, n_rows - 2 - h)] for h in range(half - 1)]
    middle = [(half - 1, half), (half, half - 1)]
    outward = [[(b, a) for a, b in pairs] for pairs in reversed(inward)]

    def across(x, d):
        return lax.ppermute(x, "proj", [(i, i ^ d) for i in range(n_proj)])

    def body(targets, precond, train):
        z = lax.axis_index("rows")
        m = targets.shape[0]
        rows = {0: targets, 1: across(targets, 1)}
        for d in range(2, n_proj, 2):
            rows[d] = across(targets, d)
            rows[d + 1] = across(rows[d], 1)
        owners = [0, 1] + [d ^ 1 for d in range(2, n_proj)]
        cond = {d: apply_precond(rows[d], precond) for d in owners}
        chunks = [(0, 0, m // 2)] + [(d, 0, m) for d in owners[1:]] + [(0, m // 2, m)]
        parts = {}
        for d, lo, hi in chunks:
            total = cond[d][lo:hi]
            for pairs in inward:
                total = add(total, lax.ppermute(total, "rows", pairs))
            total = add(total, lax.ppermute(total, "rows", middle))
            for hop, pairs in enumerate(outward):
                given = lax.ppermute(total, "rows", pairs)
                edge = half - 2 - hop
                outer = ((z == edge) | (z == n_rows - 1 - edge)).astype(jnp.int32)
                if hop < len(outward) - 1:
                    total = jnp.where(outer == 1, given, total)
            parts[d, lo] = score(outer[None], total, given, train)
        got = jnp.concatenate([parts[0, 0], parts[0, m // 2]]).astype(F32)
        for d in owners[1:]:
            got = got + across(parts[d, 0], d).astype(F32)
        return got

    return body


def solution(mesh):
    return jax.shard_map(
        make_body(mesh.shape["rows"], mesh.shape["proj"]),
        mesh=mesh,
        in_specs=(P("proj", "rows"), P(("groups", "rows"), "proj"), P(("groups", "rows"), "proj")),
        out_specs=P("proj", ("groups", "rows")),
        check_vma=False,
    )
```

time: 128 us -> 88.3 us (0.69)
  waiting for transfers between devices: 100 us -> 28.5 us
  starting transfers between devices: 0.12 us -> 32.4 us
  Pallas kernels: 0 us -> 16.7 us
  matrix products: 12.9 us -> 0 us
  between operations: 13.1 us -> 0.36 us
  local copies, waits for them, and re-layouts: 0 us -> 8.99 us
    reduce_scatter x2 -> x0, waiting for transfers between devices: 50.1 us -> none  [the longest x1 27.2 us: body(): lax.psum_scatter(jnp.dot(all_targets, precond, preferred_element_type=jnp...]
    all_gather x2 -> x0, waiting for transfers between devices: 49.3 us -> none  [the longest x1 28.2 us: body(): conditioned = lax.all_gather(share, 'rows', axis=0, tiled=True)]
    ppermute x0 -> x21, starting transfers between devices: none -> 32.4 us  [the longest x5 17.3 us: body(): total = add(total, lax.ppermute(total, 'rows', pairs))]
    ppermute x0 -> x21, waiting for transfers between devices: none -> 28.5 us  [the longest x5 12.4 us: body(): total = add(total, lax.ppermute(total, 'rows', pairs))]
    pallas_call x0 -> x19, Pallas kernels: none -> 16.7 us  [the longest x5 9.9 us: score(): pl.pallas_call(kernel, out_shape=jax.ShapeDtypeStruct((m, n), BF16), in_s...]
    dot_general x2 -> x0, matrix products: 12.9 us -> none  [the longest x1 7.02 us: body(): jnp.dot(all_targets, precond, preferred_element_type=jnp.float32)]
    unnamed x0 -> x14, local copies, waits for them, and re-layouts: none -> 8.97 us
    convert_element_type x1 -> x0, other arithmetic: 1.7 us -> none  [body(): return lax.psum_scatter(partial_value.astype(jnp.bfloat16), 'proj', scatt...]
  transfers between devices with their start and end apart: 4 -> 21, of which waited for: 4 -> 8; matrix products, arithmetic and copies ran while one was open for 0% -> 0% of each run, Pallas kernels for 0% -> 19%
where the time goes in v1:
time: 88.3 us; the launch traced here: 87.8 us
  starting transfers between devices  32.4 us (37%)
  waiting for transfers between devices  28.5 us (32%)
  Pallas kernels  16.7 us (19%)
  local copies, waits for them, and re-layouts  8.99 us (10%)
    ppermute x5, starting transfers between devices, body(): total = add(total, lax.ppermute(total, 'rows', pairs))  17.3 us
    ppermute x5, waiting for transfers between devices, body(): total = add(total, lax.ppermute(total, 'rows', pairs))  12.4 us
    pallas_call x5, Pallas kernels, score(): pl.pallas_call(kernel, out_shape=jax.ShapeDtypeStruct((m, n), BF16), in_s...  9.9 us
    ppermute x5, waiting for transfers between devices, body(): given = lax.ppermute(total, 'rows', pairs)  9.5 us
    unnamed x14, local copies, waits for them, and re-layouts  8.97 us
    ppermute x6, waiting for transfers between devices, across(): return lax.ppermute(x, 'proj', [(i, i ^ d) for i in range(n_proj)])  6.54 us
    ppermute x5, starting transfers between devices, body(): given = lax.ppermute(total, 'rows', pairs)  6.46 us
    pallas_call x4, Pallas kernels, apply_precond(): pl.pallas_call(kernel, out_shape=jax.ShapeDtypeStruct((m, n), BF16), in_s...  6.28 us
  transfers between devices with their start and end apart: 21, of which 8 were waited for; matrix products, arithmetic and copies ran while one was open for 0% of the time, Pallas kernels for 19%

profile of v1, /device:TPU:0, one launch (start us, length us, event | category | flops | bytes accessed | tf_op | source)
XLA Modules:
  0.0 87.8 jit_solution(2874798947931288867)
XLA Ops:
  0.0 2.9 %collective-permute-start.11 = (bf16[64,2048]{1,0:T(8,128)(2,1)}, bf16[64,2048]{1,0:T(8,128)(2,1)S(1)}, u32[]{:S(2)}, u32[]{:S(2)}) collective-permute-start(bf16[64,2048]{1,0:T(8,128)(2,1)} %rows_ref.1), channel_id=1, source_target_pairs={{0,2},{1,3},{2,0},{3,1},{4,6},{5,7},{6,4},{7,5},{8,10},{9,11},{10,... | collective-permute-start | bytes 786440 | tf_op jit(solution)/shard_map/ppermute | solution.py:79
  2.9 6.5 %collective-permute-done.11.rows_ref = bf16[64,2048]{1,0:T(8,128)(2,1)S(1)} collective-permute-done((bf16[64,2048]{1,0:T(8,128)(2,1)}, bf16[64,2048]{1,0:T(8,128)(2,1)S(1)}, u32[]{:S(2)}, u32[]{:S(2)}) %collective-permute-start.11) | collective-permute-done | bytes 262176 | tf_op jit(solution)/shard_map/ppermute | solution.py:79
  9.5 3.4 %copy-done.2 = bf16[2048,2048]{1,0:T(8,128)(2,1)S(1)} copy-done((bf16[2048,2048]{1,0:T(8,128)(2,1)S(1)}, bf16[2048,2048]{1,0:T(8,128)(2,1)}, u32[]{:S(2)}) %copy-start.2) | copy-done | bytes 8388632
  12.8 1.6 %shard_map.52.a_ref = bf16[64,2048]{1,0:T(8,128)(2,1)S(1)} custom-call(bf16[64,2048]{1,0:T(8,128)(2,1)S(1)} %collective-permute-done.11.rows_ref, bf16[2048,2048]{1,0:T(8,128)(2,1)S(1)} %copy-done.2), custom_call_target="tpu_custom_call" | custom-call | flops 536870912 | bytes 8388608 | tf_op jit(solution)/shard_map/pallas_call | solution.py:24
  14.4 4.0 %collective-permute-start.17 = (bf16[64,2048]{1,0:T(8,128)(2,1)S(1)}, bf16[64,2048]{1,0:T(8,128)(2,1)S(1)}, u32[]{:S(2)}, u32[]{:S(2)}) collective-permute-start(bf16[64,2048]{1,0:T(8,128)(2,1)S(1)} %shard_map.52.a_ref), channel_id=1, source_target_pairs={{0,4},{12,8},{1,5},{13,9},{2,6},{14,10},{3,7},{15,11},{16,20},{28,... | collective-permute-start | bytes 786440 | tf_op jit(solution)/shard_map/ppermute | solution.py:95
  18.5 1.6 %shard_map.44.a_ref = bf16[64,2048]{1,0:T(8,128)(2,1)S(1)} custom-call(bf16[64,2048]{1,0:T(8,128)(2,1)S(1)} %collective-permute-done.6.rows_ref, bf16[2048,2048]{1,0:T(8,128)(2,1)S(1)} %copy-done.3), custom_call_target="tpu_custom_call" | custom-call | flops 536870912 | bytes 8388608 | tf_op jit(solution)/shard_map/pallas_call | solution.py:24
  20.0 1.5 %collective-permute-start.7 = (bf16[64,2048]{1,0:T(8,128)(2,1)S(1)}, bf16[64,2048]{1,0:T(8,128)(2,1)S(1)}, u32[]{:S(2)}, u32[]{:S(2)}) collective-permute-start(bf16[64,2048]{1,0:T(8,128)(2,1)S(1)} %shard_map.44.a_ref), channel_id=1, source_target_pairs={{0,4},{12,8},{1,5},{13,9},{2,6},{14,10},{3,7},{15,11},{16,20},{28,... | collective-permute-start | bytes 786440 | tf_op jit(solution)/shard_map/ppermute | solution.py:95
  21.6 1.6 %shard_map.48.a_ref = bf16[64,2048]{1,0:T(8,128)(2,1)S(1)} custom-call(bf16[64,2048]{1,0:T(8,128)(2,1)S(1)} %collective-permute-done.12.rows_ref, bf16[2048,2048]{1,0:T(8,128)(2,1)S(1)} %copy-done.3), custom_call_target="tpu_custom_call" | custom-call | flops 536870912 | bytes 8388608 | tf_op jit(solution)/shard_map/pallas_call | solution.py:24
  23.1 1.3 %collective-permute-start.13 = (bf16[64,2048]{1,0:T(8,128)(2,1)S(1)}, bf16[64,2048]{1,0:T(8,128)(2,1)S(1)}, u32[]{:S(2)}, u32[]{:S(2)}) collective-permute-start(bf16[64,2048]{1,0:T(8,128)(2,1)S(1)} %shard_map.48.a_ref), channel_id=1, source_target_pairs={{0,4},{12,8},{1,5},{13,9},{2,6},{14,10},{3,7},{15,11},{16,20},{28,... | collective-permute-start | bytes 786440 | tf_op jit(solution)/shard_map/ppermute | solution.py:95
  24.5 0.6 collective-permute-done.17.b_ref
  25.0 0.1 shard_map.53.a_ref
  25.1 0.7 collective-permute-start.18
  25.8 4.9 %collective-permute-done.7.b_ref = bf16[64,2048]{1,0:T(8,128)(2,1)S(1)} collective-permute-done((bf16[64,2048]{1,0:T(8,128)(2,1)S(1)}, bf16[64,2048]{1,0:T(8,128)(2,1)S(1)}, u32[]{:S(2)}, u32[]{:S(2)}) %collective-permute-start.7) | collective-permute-done | bytes 262176 | tf_op jit(solution)/shard_map/ppermute | solution.py:95
  30.7 0.1 shard_map.45.a_ref
  30.7 0.7 collective-permute-start.8
  31.4 4.5 %collective-permute-done.13.b_ref = bf16[64,2048]{1,0:T(8,128)(2,1)S(1)} collective-permute-done((bf16[64,2048]{1,0:T(8,128)(2,1)S(1)}, bf16[64,2048]{1,0:T(8,128)(2,1)S(1)}, u32[]{:S(2)}, u32[]{:S(2)}) %collective-permute-start.13) | collective-permute-done | bytes 262176 | tf_op jit(solution)/shard_map/ppermute | solution.py:95
  35.9 0.1 shard_map.49.a_ref
  36.0 0.7 collective-permute-start.14
  36.6 1.6 %shard_map.37 = bf16[64,2048]{1,0:T(8,128)(2,1)S(1)} custom-call(bf16[64,2048]{1,0:T(8,128)(2,1)S(1)} %copy-done.4, bf16[2048,2048]{1,0:T(8,128)(2,1)S(1)} %copy-done.3), custom_call_target="tpu_custom_call" | custom-call | flops 536870912 | bytes 8388608 | tf_op jit(solution)/shard_map/pallas_call | solution.py:24
  38.2 0.1 shard_map.54.kept_ref
  38.3 1.3 %collective-permute-start.19 = (bf16[64,2048]{1,0:T(8,128)(2,1)S(1)}, bf16[64,2048]{1,0:T(8,128)(2,1)S(1)}, u32[]{:S(2)}, u32[]{:S(2)}) collective-permute-start(bf16[64,2048]{1,0:T(8,128)(2,1)S(1)} %shard_map.54.kept_ref), channel_id=1, source_target_pairs={{4,0},{8,12},{5,1},{9,13},{6,2},{10,14},{7,3},{11,15},{20,16},{24,... | collective-permute-start | bytes 786440 | tf_op jit(solution)/shard_map/ppermute | solution.py:98
  39.6 0.1 shard_map.46.kept_ref
  39.7 1.3 %collective-permute-start.9 = (bf16[64,2048]{1,0:T(8,128)(2,1)S(1)}, bf16[64,2048]{1,0:T(8,128)(2,1)S(1)}, u32[]{:S(2)}, u32[]{:S(2)}) collective-permute-start(bf16[64,2048]{1,0:T(8,128)(2,1)S(1)} %shard_map.46.kept_ref), channel_id=1, source_target_pairs={{4,0},{8,12},{5,1},{9,13},{6,2},{10,14},{7,3},{11,15},{20,16},{24,... | collective-permute-start | bytes 786440 | tf_op jit(solution)/shard_map/ppermute | solution.py:98
  41.0 0.1 shard_map.50.kept_ref
  41.1 1.3 %collective-permute-start.15 = (bf16[64,2048]{1,0:T(8,128)(2,1)S(1)}, bf16[64,2048]{1,0:T(8,128)(2,1)S(1)}, u32[]{:S(2)}, u32[]{:S(2)}) collective-permute-start(bf16[64,2048]{1,0:T(8,128)(2,1)S(1)} %shard_map.50.kept_ref), channel_id=1, source_target_pairs={{4,0},{8,12},{5,1},{9,13},{6,2},{10,14},{7,3},{11,15},{20,16},{24,... | collective-permute-start | bytes 786440 | tf_op jit(solution)/shard_map/ppermute | solution.py:98
  42.4 9.2 %collective-permute-start.3 = (bf16[32,2048]{1,0:T(8,128)(2,1)S(1)}, bf16[32,2048]{1,0:T(8,128)(2,1)S(1)}, u32[]{:S(2)}, u32[]{:S(2)}) collective-permute-start(bf16[32,2048]{1,0:T(8,128)(2,1)S(1)} %get-tuple-element.6.a_ref), channel_id=1, source_target_pairs={{0,4},{12,8},{1,5},{13,9},{2,6},{14,10},{3,7},{15,11},{16,20},{28,... | collective-permute-start | bytes 393224 | tf_op jit(solution)/shard_map/ppermute | solution.py:95
  51.6 1.3 %collective-permute-start = (bf16[32,2048]{1,0:T(8,128)(2,1)S(1)}, bf16[32,2048]{1,0:T(8,128)(2,1)S(1)}, u32[]{:S(2)}, u32[]{:S(2)}) collective-permute-start(bf16[32,2048]{1,0:T(8,128)(2,1)S(1)} %get-tuple-element.5.a_ref), channel_id=1, source_target_pairs={{0,4},{12,8},{1,5},{13,9},{2,6},{14,10},{3,7},{15,11},{16,20},{28,... | collective-permute-start | bytes 393224 | tf_op jit(solution)/shard_map/ppermute | solution.py:95
  52.9 1.8 %collective-permute-done.3.b_ref = bf16[32,2048]{1,0:T(8,128)(2,1)S(1)} collective-permute-done((bf16[32,2048]{1,0:T(8,128)(2,1)S(1)}, bf16[32,2048]{1,0:T(8,128)(2,1)S(1)}, u32[]{:S(2)}, u32[]{:S(2)}) %collective-permute-start.3) | collective-permute-done | bytes 131104 | tf_op jit(solution)/shard_map/ppermute | solution.py:95
  54.8 0.7 collective-permute-start.4
  55.4 0.7 collective-permute-done.b_ref
  56.2 0.7 collective-permute-start.1
  56.9 2.8 %copy-done = bf16[1536,2048]{1,0:T(8,128)(2,1)S(1)} copy-done((bf16[1536,2048]{1,0:T(8,128)(2,1)S(1)}, bf16[1536,2048]{1,0:T(8,128)(2,1)}, u32[]{:S(2)}) %copy-start) | copy-done | bytes 6291480
  59.6 2.0 %shard_map.55 = bf16[64,1536]{1,0:T(8,128)(2,1)S(1)} custom-call(s32[1]{0:T(128)} %bitcast.outer_ref, bf16[64,2048]{1,0:T(8,128)(2,1)S(1)} %shard_map.54.kept_ref, bf16[64,2048]{1,0:T(8,128)(2,1)S(1)} %collective-permute-done.19.given_ref, bf16[1536,2048]{1,0:T(8,128)(2,1)S(1)} %copy-done), custom_call_target="tpu_custom_call" | custom-call | flops 402653184 | bytes 6291456 | tf_op jit(solution)/shard_map/pallas_call | solution.py:47
  61.7 1.6 %collective-permute-start.20 = (bf16[64,1536]{1,0:T(8,128)(2,1)S(1)}, bf16[64,1536]{1,0:T(8,128)(2,1)S(1)}, u32[]{:S(2)}, u32[]{:S(2)}) collective-permute-start(bf16[64,1536]{1,0:T(8,128)(2,1)S(1)} %shard_map.55), channel_id=1, source_target_pairs={{0,2},{1,3},{2,0},{3,1},{4,6},{5,7},{6,4},{7,5},{8,10},{9,11},{10,... | collective-permute-start | bytes 589832 | tf_op jit(solution)/shard_map/ppermute | solution.py:79
  63.2 2.8 %copy-done.1 = bf16[1536,2048]{1,0:T(8,128)(2,1)S(1)} copy-done((bf16[1536,2048]{1,0:T(8,128)(2,1)S(1)}, bf16[1536,2048]{1,0:T(8,128)(2,1)}, u32[]{:S(2)}) %copy-start.1) | copy-done | bytes 6291480
  66.0 2.0 %shard_map.47 = bf16[64,1536]{1,0:T(8,128)(2,1)S(1)} custom-call(s32[1]{0:T(128)} %bitcast.outer_ref, bf16[64,2048]{1,0:T(8,128)(2,1)S(1)} %shard_map.46.kept_ref, bf16[64,2048]{1,0:T(8,128)(2,1)S(1)} %collective-permute-done.9.given_ref, bf16[1536,2048]{1,0:T(8,128)(2,1)S(1)} %copy-done.1), custom_call_target="tpu_custom_call" | custom-call | flops 402653184 | bytes 6291456 | tf_op jit(solution)/shard_map/pallas_call | solution.py:47
  68.0 0.0 slice-start.1
  68.0 0.1 collective-permute-start.10
  68.1 2.0 %shard_map.51 = bf16[64,1536]{1,0:T(8,128)(2,1)S(1)} custom-call(s32[1]{0:T(128)} %bitcast.outer_ref, bf16[64,2048]{1,0:T(8,128)(2,1)S(1)} %shard_map.50.kept_ref, bf16[64,2048]{1,0:T(8,128)(2,1)S(1)} %collective-permute-done.15.given_ref, bf16[1536,2048]{1,0:T(8,128)(2,1)S(1)} %copy-done.1), custom_call_target="tpu_custom_call" | custom-call | flops 402653184 | bytes 6291456 | tf_op jit(solution)/shard_map/pallas_call | solution.py:47
  70.1 0.7 collective-permute-start.16
  70.9 1.3 %collective-permute-start.5 = (bf16[32,2048]{1,0:T(8,128)(2,1)S(1)}, bf16[32,2048]{1,0:T(8,128)(2,1)S(1)}, u32[]{:S(2)}, u32[]{:S(2)}) collective-permute-start(bf16[32,2048]{1,0:T(8,128)(2,1)S(1)} %shard_map.42.kept_ref), channel_id=1, source_target_pairs={{4,0},{8,12},{5,1},{9,13},{6,2},{10,14},{7,3},{11,15},{20,16},{24,... | collective-permute-start | bytes 393224 | tf_op jit(solution)/shard_map/ppermute | solution.py:98
  72.2 1.3 %collective-permute-start.2 = (bf16[32,2048]{1,0:T(8,128)(2,1)S(1)}, bf16[32,2048]{1,0:T(8,128)(2,1)S(1)}, u32[]{:S(2)}, u32[]{:S(2)}) collective-permute-start(bf16[32,2048]{1,0:T(8,128)(2,1)S(1)} %shard_map.39.kept_ref), channel_id=1, source_target_pairs={{4,0},{8,12},{5,1},{9,13},{6,2},{10,14},{7,3},{11,15},{20,16},{24,... | collective-permute-start | bytes 393224 | tf_op jit(solution)/shard_map/ppermute | solution.py:98
  73.5 9.2 %collective-permute-done.5.given_ref = bf16[32,2048]{1,0:T(8,128)(2,1)S(1)} collective-permute-done((bf16[32,2048]{1,0:T(8,128)(2,1)S(1)}, bf16[32,2048]{1,0:T(8,128)(2,1)S(1)}, u32[]{:S(2)}, u32[]{:S(2)}) %collective-permute-start.5) | collective-permute-done | bytes 131104 | tf_op jit(solution)/shard_map/ppermute | solution.py:98
  82.8 1.9 %shard_map.43 = bf16[32,1536]{1,0:T(8,128)(2,1)S(1)} custom-call(s32[1]{0:T(128)} %bitcast.outer_ref, bf16[32,2048]{1,0:T(8,128)(2,1)S(1)} %shard_map.42.kept_ref, bf16[32,2048]{1,0:T(8,128)(2,1)S(1)} %collective-permute-done.5.given_ref, bf16[1536,2048]{1,0:T(8,128)(2,1)S(1)} %bitcast.2), custom_call_target="tpu_custom_call" | custom-call | flops 201326592 | bytes 6291456 | tf_op jit(solution)/shard_map/pallas_call | solution.py:47
  84.7 0.3 collective-permute-done.2.given_ref
  84.9 1.9 %shard_map.40 = bf16[32,1536]{1,0:T(8,128)(2,1)S(1)} custom-call(s32[1]{0:T(128)} %bitcast.outer_ref, bf16[32,2048]{1,0:T(8,128)(2,1)S(1)} %shard_map.39.kept_ref, bf16[32,2048]{1,0:T(8,128)(2,1)S(1)} %collective-permute-done.2.given_ref, bf16[1536,2048]{1,0:T(8,128)(2,1)S(1)} %bitcast.2), custom_call_target="tpu_custom_call" | custom-call | flops 201326592 | bytes 6291456 | tf_op jit(solution)/shard_map/pallas_call | solution.py:47
  86.9 0.0 collective-permute-done.20
  86.9 0.8 convert_add_fusion
  (30 shorter events, 0.2 us)
Async XLA Ops:
  0.0 9.5 %collective-permute-start.11 = (bf16[64,2048]{1,0:T(8,128)(2,1)}, bf16[64,2048]{1,0:T(8,128)(2,1)S(1)}, u32[]{:S(2)}, u32[]{:S(2)}) collective-permute-start(bf16[64,2048]{1,0:T(8,128)(2,1)} %rows_ref.1), channel_id=1, source_target_pairs={{0,2},{1,3},{2,0},{3,1},{4,6},{5,7},{6,4},{7,5},{8,10},{9,11},{10,... | collective-permute-start | bytes 786440 | tf_op jit(solution)/shard_map/ppermute | solution.py:79
  2.9 15.5 %collective-permute-start.6 = (bf16[64,2048]{1,0:T(8,128)(2,1)}, bf16[64,2048]{1,0:T(8,128)(2,1)S(1)}, u32[]{:S(2)}, u32[]{:S(2)}) collective-permute-start(bf16[64,2048]{1,0:T(8,128)(2,1)} %rows_ref.1), channel_id=1, source_target_pairs={{0,1},{1,0},{2,3},{3,2},{4,5},{5,4},{6,7},{7,6},{8,9},{9,8},{10,11... | collective-permute-start | bytes 786440 | tf_op jit(solution)/shard_map/ppermute | solution.py:79
  9.5 12.1 %collective-permute-start.12 = (bf16[64,2048]{1,0:T(8,128)(2,1)S(1)}, bf16[64,2048]{1,0:T(8,128)(2,1)S(1)}, u32[]{:S(2)}, u32[]{:S(2)}) collective-permute-start(bf16[64,2048]{1,0:T(8,128)(2,1)S(1)} %collective-permute-done.11.rows_ref), channel_id=1, source_target_pairs={{0,1},{1,0},{2,3},{3,2},{4,5},{5,4},{6,7},{7,6},{8,9},{9,8},{10,11... | collective-permute-start | bytes 786440 | tf_op jit(solution)/shard_map/ppermute | solution.py:79
  9.5 3.4 %copy-start.2 = (bf16[2048,2048]{1,0:T(8,128)(2,1)S(1)}, bf16[2048,2048]{1,0:T(8,128)(2,1)}, u32[]{:S(2)}) copy-start(bf16[2048,2048]{1,0:T(8,128)(2,1)} %precond_ref.7) | copy-start | bytes 25165828
  12.8 5.6 %copy-start.3 = (bf16[2048,2048]{1,0:T(8,128)(2,1)S(1)}, bf16[2048,2048]{1,0:T(8,128)(2,1)}, u32[]{:S(2)}) copy-start(bf16[2048,2048]{1,0:T(8,128)(2,1)} %precond_ref.7) | copy-start | bytes 25165828
  14.4 22.2 %copy-start.4 = (bf16[64,2048]{1,0:T(8,128)(2,1)S(1)}, bf16[64,2048]{1,0:T(8,128)(2,1)}, u32[]{:S(2)}) copy-start(bf16[64,2048]{1,0:T(8,128)(2,1)} %rows_ref.1) | copy-start | bytes 786436
  14.4 10.6 %collective-permute-start.17 = (bf16[64,2048]{1,0:T(8,128)(2,1)S(1)}, bf16[64,2048]{1,0:T(8,128)(2,1)S(1)}, u32[]{:S(2)}, u32[]{:S(2)}) collective-permute-start(bf16[64,2048]{1,0:T(8,128)(2,1)S(1)} %shard_map.52.a_ref), channel_id=1, source_target_pairs={{0,4},{12,8},{1,5},{13,9},{2,6},{14,10},{3,7},{15,11},{16,20},{28,... | collective-permute-start | bytes 786440 | tf_op jit(solution)/shard_map/ppermute | solution.py:95
  20.0 10.6 %collective-permute-start.7 = (bf16[64,2048]{1,0:T(8,128)(2,1)S(1)}, bf16[64,2048]{1,0:T(8,128)(2,1)S(1)}, u32[]{:S(2)}, u32[]{:S(2)}) collective-permute-start(bf16[64,2048]{1,0:T(8,128)(2,1)S(1)} %shard_map.44.a_ref), channel_id=1, source_target_pairs={{0,4},{12,8},{1,5},{13,9},{2,6},{14,10},{3,7},{15,11},{16,20},{28,... | collective-permute-start | bytes 786440 | tf_op jit(solution)/shard_map/ppermute | solution.py:95
  23.1 12.7 %collective-permute-start.13 = (bf16[64,2048]{1,0:T(8,128)(2,1)S(1)}, bf16[64,2048]{1,0:T(8,128)(2,1)S(1)}, u32[]{:S(2)}, u32[]{:S(2)}) collective-permute-start(bf16[64,2048]{1,0:T(8,128)(2,1)S(1)} %shard_map.48.a_ref), channel_id=1, source_target_pairs={{0,4},{12,8},{1,5},{13,9},{2,6},{14,10},{3,7},{15,11},{16,20},{28,... | collective-permute-start | bytes 786440 | tf_op jit(solution)/shard_map/ppermute | solution.py:95
  25.1 13.1 %collective-permute-start.18 = (bf16[64,2048]{1,0:T(8,128)(2,1)S(1)}, bf16[64,2048]{1,0:T(8,128)(2,1)S(1)}, u32[]{:S(2)}, u32[]{:S(2)}) collective-permute-start(bf16[64,2048]{1,0:T(8,128)(2,1)S(1)} %shard_map.53.a_ref), channel_id=1, source_target_pairs={{4,8},{8,4},{5,9},{9,5},{6,10},{10,6},{7,11},{11,7},{20,24},{24,20... | collective-permute-start | bytes 786440 | tf_op jit(solution)/shard_map/ppermute | solution.py:96
  30.7 8.9 %collective-permute-start.8 = (bf16[64,2048]{1,0:T(8,128)(2,1)S(1)}, bf16[64,2048]{1,0:T(8,128)(2,1)S(1)}, u32[]{:S(2)}, u32[]{:S(2)}) collective-permute-start(bf16[64,2048]{1,0:T(8,128)(2,1)S(1)} %shard_map.45.a_ref), channel_id=1, source_target_pairs={{4,8},{8,4},{5,9},{9,5},{6,10},{10,6},{7,11},{11,7},{20,24},{24,20... | collective-permute-start | bytes 786440 | tf_op jit(solution)/shard_map/ppermute | solution.py:96
  36.0 5.0 %collective-permute-start.14 = (bf16[64,2048]{1,0:T(8,128)(2,1)S(1)}, bf16[64,2048]{1,0:T(8,128)(2,1)S(1)}, u32[]{:S(2)}, u32[]{:S(2)}) collective-permute-start(bf16[64,2048]{1,0:T(8,128)(2,1)S(1)} %shard_map.49.a_ref), channel_id=1, source_target_pairs={{4,8},{8,4},{5,9},{9,5},{6,10},{10,6},{7,11},{11,7},{20,24},{24,20... | collective-permute-start | bytes 786440 | tf_op jit(solution)/shard_map/ppermute | solution.py:96
  38.3 18.5 %collective-permute-start.19 = (bf16[64,2048]{1,0:T(8,128)(2,1)S(1)}, bf16[64,2048]{1,0:T(8,128)(2,1)S(1)}, u32[]{:S(2)}, u32[]{:S(2)}) collective-permute-start(bf16[64,2048]{1,0:T(8,128)(2,1)S(1)} %shard_map.54.kept_ref), channel_id=1, source_target_pairs={{4,0},{8,12},{5,1},{9,13},{6,2},{10,14},{7,3},{11,15},{20,16},{24,... | collective-permute-start | bytes 786440 | tf_op jit(solution)/shard_map/ppermute | solution.py:98
  39.7 23.5 %collective-permute-start.9 = (bf16[64,2048]{1,0:T(8,128)(2,1)S(1)}, bf16[64,2048]{1,0:T(8,128)(2,1)S(1)}, u32[]{:S(2)}, u32[]{:S(2)}) collective-permute-start(bf16[64,2048]{1,0:T(8,128)(2,1)S(1)} %shard_map.46.kept_ref), channel_id=1, source_target_pairs={{4,0},{8,12},{5,1},{9,13},{6,2},{10,14},{7,3},{11,15},{20,16},{24,... | collective-permute-start | bytes 786440 | tf_op jit(solution)/shard_map/ppermute | solution.py:98
  41.1 27.0 %collective-permute-start.15 = (bf16[64,2048]{1,0:T(8,128)(2,1)S(1)}, bf16[64,2048]{1,0:T(8,128)(2,1)S(1)}, u32[]{:S(2)}, u32[]{:S(2)}) collective-permute-start(bf16[64,2048]{1,0:T(8,128)(2,1)S(1)} %shard_map.50.kept_ref), channel_id=1, source_target_pairs={{4,0},{8,12},{5,1},{9,13},{6,2},{10,14},{7,3},{11,15},{20,16},{24,... | collective-permute-start | bytes 786440 | tf_op jit(solution)/shard_map/ppermute | solution.py:98
  42.4 12.3 %collective-permute-start.3 = (bf16[32,2048]{1,0:T(8,128)(2,1)S(1)}, bf16[32,2048]{1,0:T(8,128)(2,1)S(1)}, u32[]{:S(2)}, u32[]{:S(2)}) collective-permute-start(bf16[32,2048]{1,0:T(8,128)(2,1)S(1)} %get-tuple-element.6.a_ref), channel_id=1, source_target_pairs={{0,4},{12,8},{1,5},{13,9},{2,6},{14,10},{3,7},{15,11},{16,20},{28,... | collective-permute-start | bytes 393224 | tf_op jit(solution)/shard_map/ppermute | solution.py:95
  51.6 4.5 %collective-permute-start = (bf16[32,2048]{1,0:T(8,128)(2,1)S(1)}, bf16[32,2048]{1,0:T(8,128)(2,1)S(1)}, u32[]{:S(2)}, u32[]{:S(2)}) collective-permute-start(bf16[32,2048]{1,0:T(8,128)(2,1)S(1)} %get-tuple-element.5.a_ref), channel_id=1, source_target_pairs={{0,4},{12,8},{1,5},{13,9},{2,6},{14,10},{3,7},{15,11},{16,20},{28,... | collective-permute-start | bytes 393224 | tf_op jit(solution)/shard_map/ppermute | solution.py:95
  54.8 16.1 %collective-permute-start.4 = (bf16[32,2048]{1,0:T(8,128)(2,1)S(1)}, bf16[32,2048]{1,0:T(8,128)(2,1)S(1)}, u32[]{:S(2)}, u32[]{:S(2)}) collective-permute-start(bf16[32,2048]{1,0:T(8,128)(2,1)S(1)} %shard_map.41.a_ref), channel_id=1, source_target_pairs={{4,8},{8,4},{5,9},{9,5},{6,10},{10,6},{7,11},{11,7},{20,24},{24,20... | collective-permute-start | bytes 393224 | tf_op jit(solution)/shard_map/ppermute | solution.py:96
  56.2 16.0 %collective-permute-start.1 = (bf16[32,2048]{1,0:T(8,128)(2,1)S(1)}, bf16[32,2048]{1,0:T(8,128)(2,1)S(1)}, u32[]{:S(2)}, u32[]{:S(2)}) collective-permute-start(bf16[32,2048]{1,0:T(8,128)(2,1)S(1)} %shard_map.38.a_ref), channel_id=1, source_target_pairs={{4,8},{8,4},{5,9},{9,5},{6,10},{10,6},{7,11},{11,7},{20,24},{24,20... | collective-permute-start | bytes 393224 | tf_op jit(solution)/shard_map/ppermute | solution.py:96
  56.9 2.8 %copy-start = (bf16[1536,2048]{1,0:T(8,128)(2,1)S(1)}, bf16[1536,2048]{1,0:T(8,128)(2,1)}, u32[]{:S(2)}) copy-start(bf16[1536,2048]{1,0:T(8,128)(2,1)} %train_ref.9) | copy-start | bytes 18874372
  61.7 25.2 %collective-permute-start.20 = (bf16[64,1536]{1,0:T(8,128)(2,1)S(1)}, bf16[64,1536]{1,0:T(8,128)(2,1)S(1)}, u32[]{:S(2)}, u32[]{:S(2)}) collective-permute-start(bf16[64,1536]{1,0:T(8,128)(2,1)S(1)} %shard_map.55), channel_id=1, source_target_pairs={{0,2},{1,3},{2,0},{3,1},{4,6},{5,7},{6,4},{7,5},{8,10},{9,11},{10,... | collective-permute-start | bytes 589832 | tf_op jit(solution)/shard_map/ppermute | solution.py:79
  63.2 2.8 %copy-start.1 = (bf16[1536,2048]{1,0:T(8,128)(2,1)S(1)}, bf16[1536,2048]{1,0:T(8,128)(2,1)}, u32[]{:S(2)}) copy-start(bf16[1536,2048]{1,0:T(8,128)(2,1)} %train_ref.9) | copy-start | bytes 18874372
  66.0 16.8 %slice-start = ((s8[6291456]{0:T(1024)(128)(4,1)}), s8[4194304]{0:T(1024)(128)(4,1)S(1)}, s32[]{:S(2)}) async-start(s8[6291456]{0:T(1024)(128)(4,1)} %bitcast.1), calls=%async_computation | async-start | bytes 8388608
  68.0 14.7 %slice-start.1 = ((s8[6291456]{0:T(1024)(128)(4,1)}), s8[2097152]{0:T(1024)(128)(4,1)S(1)}, s32[]{:S(2)}) async-start(s8[6291456]{0:T(1024)(128)(4,1)} %bitcast.1), calls=%async_computation.1 | async-start | bytes 4194304
  68.0 18.9 %collective-permute-start.10 = (bf16[64,1536]{1,0:T(8,128)(2,1)S(1)}, bf16[64,1536]{1,0:T(8,128)(2,1)S(1)}, u32[]{:S(2)}, u32[]{:S(2)}) collective-permute-start(bf16[64,1536]{1,0:T(8,128)(2,1)S(1)} %shard_map.47), channel_id=1, source_target_pairs={{0,1},{1,0},{2,3},{3,2},{4,5},{5,4},{6,7},{7,6},{8,9},{9,8},{10,11... | collective-permute-start | bytes 589832 | tf_op jit(solution)/shard_map/ppermute | solution.py:79
  70.1 16.8 %collective-permute-start.16 = (bf16[64,1536]{1,0:T(8,128)(2,1)S(1)}, bf16[64,1536]{1,0:T(8,128)(2,1)S(1)}, u32[]{:S(2)}, u32[]{:S(2)}) collective-permute-start(bf16[64,1536]{1,0:T(8,128)(2,1)S(1)} %shard_map.51), channel_id=1, source_target_pairs={{0,3},{1,2},{2,1},{3,0},{4,7},{5,6},{6,5},{7,4},{8,11},{9,10},{10,... | collective-permute-start | bytes 589832 | tf_op jit(solution)/shard_map/ppermute | solution.py:79
  70.9 11.9 %collective-permute-start.5 = (bf16[32,2048]{1,0:T(8,128)(2,1)S(1)}, bf16[32,2048]{1,0:T(8,128)(2,1)S(1)}, u32[]{:S(2)}, u32[]{:S(2)}) collective-permute-start(bf16[32,2048]{1,0:T(8,128)(2,1)S(1)} %shard_map.42.kept_ref), channel_id=1, source_target_pairs={{4,0},{8,12},{5,1},{9,13},{6,2},{10,14},{7,3},{11,15},{20,16},{24,... | collective-permute-start | bytes 393224 | tf_op jit(solution)/shard_map/ppermute | solution.py:98
  72.2 12.7 %collective-permute-start.2 = (bf16[32,2048]{1,0:T(8,128)(2,1)S(1)}, bf16[32,2048]{1,0:T(8,128)(2,1)S(1)}, u32[]{:S(2)}, u32[]{:S(2)}) collective-permute-start(bf16[32,2048]{1,0:T(8,128)(2,1)S(1)} %shard_map.39.kept_ref), channel_id=1, source_target_pairs={{4,0},{8,12},{5,1},{9,13},{6,2},{10,14},{7,3},{11,15},{20,16},{24,... | collective-permute-start | bytes 393224 | tf_op jit(solution)/shard_map/ppermute | solution.py:98

commit v2 on v0

v2 whole, which is shorter than its diff:
```python
import jax
import jax.numpy as jnp
from jax import lax
from jax.experimental import pallas as pl
from jax.experimental.pallas import tpu as pltpu
from jax.sharding import PartitionSpec as P

VMEM = pl.BlockSpec(memory_space=pltpu.VMEM)
LIMIT = pltpu.CompilerParams(vmem_limit_bytes=12 << 20)
BF16, F32 = jnp.bfloat16, jnp.float32


def dot(a, b):
    return jnp.dot(a, b, preferred_element_type=F32)


def dot_t(a, b):
    return lax.dot_general(a, b, (((1,), (1,)), ((), ())), preferred_element_type=F32)


class Order:
    def __init__(self):
        self.last = ()

    def __call__(self, kernel, shapes, *args, cost=0):
        n_args, n_extra = len(args), len(self.last)

        def ordered(*refs):
            kernel(*refs[:n_args], *refs[n_args + n_extra :])

        outs = pl.pallas_call(
            ordered,
            out_shape=tuple(pltpu.VMEM(shape, dtype) for shape, dtype in shapes),
            in_specs=[VMEM] * (n_args + n_extra),
            out_specs=(VMEM,) * len(shapes),
            compiler_params=LIMIT,
            cost_estimate=pl.CostEstimate(flops=0, bytes_accessed=cost, transcendentals=0),
        )(*args, *self.last)
        self.last = (outs[0],)
        return outs


def make_body(n_rows, n_proj):
    half = n_rows // 2
    hops = half - 1
    n_chunks = n_proj

    def both_ways(pairs):
        partner = {i: j for a, b in pairs for i, j in ((a, b), (b, a))}
        swaps = []
        for z in range(n_rows):
            for p in range(n_proj):
                to = (partner[z], p) if z in partner else (z, p ^ 1)
                swaps.append((z * n_proj + p, to[0] * n_proj + to[1]))
        return swaps

    hop_swaps = [both_ways([(h, h + 1), (n_rows - 1 - h, n_rows - 2 - h)]) for h in range(hops)]
    middle_swaps = both_ways([(half - 1, half)])

    def along(x, swaps):
        return lax.ppermute(x, ("rows", "proj"), swaps)

    def across(x, d):
        return lax.ppermute(x, "proj", [(i, i ^ d) for i in range(n_proj)])

    def at(h):
        z = lax.axis_index("rows")
        return (z == h) | (z == n_rows - 1 - h)

    def body(targets, precond, train):
        call = Order()
        m = targets.shape[0]
        n, t = precond.shape[1], train.shape[0]

        def elementwise(function, *args):
            def kernel(*refs):
                *in_refs, out_ref = refs
                out_ref[...] = function(*[r[...] for r in in_refs])

            return call(kernel, [(args[0].shape, BF16)], *args)[0]

        def plus(a, b):
            return (a.astype(F32) + b.astype(F32)).astype(BF16)

        def condition(*rows):
            step = min(n, 512)

            def kernel(*refs):
                row_refs, precond_ref, out_refs = refs[: len(rows)], refs[len(rows)], refs[len(rows) + 1 :]
                left = jnp.concatenate([r[...] for r in row_refs])
                for lo in range(0, n, step):
                    cols = slice(lo, lo + step)
                    value = dot(left, precond_ref[:, cols]).astype(BF16)
                    for i, out_ref in enumerate(out_refs):
                        out_ref[:, cols] = value[i * m : (i + 1) * m]

            return call(kernel, [((m, n), BF16)] * len(rows), *rows, precond)

        def scores(kept, given, dtype):
            step = t // 3

            def kernel(kept_ref, given_ref, train_ref, out_ref):
                left = jnp.where(at(0), given_ref[...], kept_ref[...])
                for lo in range(0, t, step):
                    cols = slice(lo, lo + step)
                    out_ref[:, cols] = dot_t(left, train_ref[cols, :]).astype(dtype)

            return call(kernel, [((m, t), dtype)], kept, given, train)[0]

        (staged,) = call(lambda x_ref, out_ref: out_ref.__setitem__(..., x_ref[...]), [(targets.shape, BF16)], targets, cost=40 << 20)
        rows = {0: staged, 1: across(staged, 1), 2: across(staged, 2)}
        owners = [*range(1, n_proj), 0]
        here, total, parts = {}, {}, {}

        def begin(c):
            here[c] = condition(rows[owners[c]])[0]

        here[0], here[n_chunks - 1] = condition(rows[1], rows[0])
        again = elementwise(lambda x: x, staged)
        for d in range(3, n_proj):
            rows[d] = across(again, d)

        moving = {}

        def valid(c):
            return 0 <= c < n_chunks

        def start_hop(h, step):
            inward, outward = step - h, step - 2 * hops + h
            if valid(inward) and valid(outward):
                value = elementwise(lambda a, b: jnp.where(at(h), a, b), here[inward], total[outward])
            elif valid(inward):
                value = here[inward]
            elif valid(outward):
                value = total[outward]
            else:
                return
            moving[h, step] = along(value, hop_swaps[h])

        def end_hop_inward(h, step):
            c = step - h
            if valid(c):
                here[c] = elementwise(
                    lambda a, b: jnp.where(at(h + 1), plus(a, b), a), here[c], moving[h, step]
                )

        def end_hop_outward(h, step):
            c = step - 2 * hops + h
            if valid(c) and h > 0:
                total[c] = elementwise(lambda a, b: jnp.where(at(h), b, a), total[c], moving[h, step])

        def finish(c):
            d = owners[c]
            value = scores(total[c], moving[0, c + 2 * hops], BF16 if d else F32)
            parts[d] = across(value, d) if d else value

        start_hop(0, 0)
        begun = 1
        for step in range(1, n_chunks + 2 * hops + 2):
            if begun < n_chunks - 1:
                begin(begun)
                begun += 1
            if step < 2 * hops:
                start_hop(0, step)
            for h in reversed(range(hops)):
                end_hop_inward(h, step - 1)
            if valid(step - hops):
                moving["middle", step] = along(here[step - hops], middle_swaps)
            if valid(step - 1 - hops):
                c = step - 1 - hops
                total[c] = elementwise(plus, here[c], moving["middle", step - 1])
            for h in range(hops):
                end_hop_outward(h, step - 1)
            for h in reversed(range(hops)):
                if h > 0 or step >= 2 * hops:
                    start_hop(h, step)
            if valid(step - 1 - 2 * hops):
                finish(step - 1 - 2 * hops)

        def close(own_ref, *refs):
            *got_refs, out_ref = refs
            value = own_ref[...]
            for ref in got_refs:
                value = value + ref[...].astype(F32)
            out_ref[...] = value

        return call(close, [((m, t), F32)], *[parts[d] for d in range(n_proj)])[0]

    return body


def solution(mesh):
    return jax.shard_map(
        make_body(mesh.shape["rows"], mesh.shape["proj"]),
        mesh=mesh,
        in_specs=(P("proj", "rows"), P(("groups", "rows"), "proj"), P(("groups", "rows"), "proj")),
        out_specs=P("proj", ("groups", "rows")),
        check_vma=False,
    )
```

time: 128 us -> 59.3 us (0.46)
  waiting for transfers between devices: 100 us -> 19.6 us
  starting transfers between devices: 0.12 us -> 21.1 us
  Pallas kernels: 0 us -> 13.2 us
  matrix products: 12.9 us -> 0 us
  between operations: 13.1 us -> 0.21 us
  local copies, waits for them, and re-layouts: 0 us -> 5.1 us
  other arithmetic: 1.7 us -> 0.01 us
    reduce_scatter x2 -> x0, waiting for transfers between devices: 50.1 us -> none  [the longest x1 27.2 us: body(): lax.psum_scatter(jnp.dot(all_targets, precond, preferred_element_type=jnp...]
    all_gather x2 -> x0, waiting for transfers between devices: 49.3 us -> none  [the longest x1 28.2 us: body(): conditioned = lax.all_gather(share, 'rows', axis=0, tiled=True)]
    ppermute x0 -> x16, starting transfers between devices: none -> 21.1 us  [the longest x10 15.6 us: along(): return lax.ppermute(x, ('rows', 'proj'), swaps)]
    ppermute x0 -> x16, waiting for transfers between devices: none -> 19.6 us  [the longest x10 14.8 us: along(): return lax.ppermute(x, ('rows', 'proj'), swaps)]
    pallas_call x0 -> x20, Pallas kernels: none -> 13.2 us  [__call__(): pl.pallas_call(ordered, out_shape=tuple((pltpu.VMEM(shape, dtype) for sha...]
    dot_general x2 -> x0, matrix products: 12.9 us -> none  [the longest x1 7.02 us: body(): jnp.dot(all_targets, precond, preferred_element_type=jnp.float32)]
    unnamed x0 -> x11, local copies, waits for them, and re-layouts: none -> 5.1 us
    convert_element_type x1 -> x0, other arithmetic: 1.7 us -> none  [body(): return lax.psum_scatter(partial_value.astype(jnp.bfloat16), 'proj', scatt...]
  transfers between devices with their start and end apart: 4 -> 16, of which waited for: 4 -> 8; matrix products, arithmetic and copies ran while one was open for 0% -> 0% of each run, Pallas kernels for 0% -> 22%
where the time goes in v2:
time: 59.3 us; the launch traced here: 59.2 us
  starting transfers between devices  21.1 us (36%)
  waiting for transfers between devices  19.6 us (33%)
  Pallas kernels  13.2 us (22%)
  local copies, waits for them, and re-layouts  5.1 us (9%)
    ppermute x10, starting transfers between devices, along(): return lax.ppermute(x, ('rows', 'proj'), swaps)  15.6 us
    ppermute x10, waiting for transfers between devices, along(): return lax.ppermute(x, ('rows', 'proj'), swaps)  14.8 us
    pallas_call x20, Pallas kernels, __call__(): pl.pallas_call(ordered, out_shape=tuple((pltpu.VMEM(shape, dtype) for sha...  13.2 us
    ppermute x6, starting transfers between devices, across(): return lax.ppermute(x, 'proj', [(i, i ^ d) for i in range(n_proj)])  5.52 us
    unnamed x11, local copies, waits for them, and re-layouts  5.1 us
    ppermute x6, waiting for transfers between devices, across(): return lax.ppermute(x, 'proj', [(i, i ^ d) for i in range(n_proj)])  4.72 us
  transfers between devices with their start and end apart: 16, of which 8 were waited for; matrix products, arithmetic and copies ran while one was open for 0% of the time, Pallas kernels for 22%

profile of v2, /device:TPU:0, one launch (start us, length us, event | category | flops | bytes accessed | tf_op | source)
XLA Modules:
  0.0 59.2 jit_solution(1586703082499676674)
XLA Ops:
  0.0 0.9 %copy-done.2 = bf16[64,2048]{1,0:T(8,128)(2,1)S(1)} copy-done((bf16[64,2048]{1,0:T(8,128)(2,1)S(1)}, bf16[64,2048]{1,0:T(8,128)(2,1)}, u32[]{:S(2)}) %copy-start.2) | copy-done | bytes 262168
  1.0 0.5 collective-permute-start
  1.5 2.6 %collective-permute-start.1 = (bf16[64,2048]{1,0:T(8,128)(2,1)S(1)}, bf16[64,2048]{1,0:T(8,128)(2,1)S(1)}, u32[]{:S(2)}, u32[]{:S(2)}) collective-permute-start(bf16[64,2048]{1,0:T(8,128)(2,1)S(1)} %shard_map.37.refs_1_.refs_3_.refs_0_), channel_id=1, source_target_pairs={{0,2},{1,3},{2,0},{3,1},{4,6},{5,7},{6,4},{7,5},{8,10},{9,11},{10,... | collective-permute-start | bytes 786440 | tf_op jit(solution)/shard_map/ppermute | solution.py:64
  4.1 3.4 %copy-done = bf16[2048,2048]{1,0:T(8,128)(2,1)S(1)} copy-done((bf16[2048,2048]{1,0:T(8,128)(2,1)S(1)}, bf16[2048,2048]{1,0:T(8,128)(2,1)}, u32[]{:S(2)}) %copy-start) | copy-done | bytes 8388632
  7.4 1.3 %shard_map.38 = (bf16[64,2048]{1,0:T(8,128)(2,1)S(1)}, bf16[64,2048]{1,0:T(8,128)(2,1)S(1)}) custom-call(bf16[64,2048]{1,0:T(8,128)(2,1)S(1)} %collective-permute-done.refs_0_, bf16[64,2048]{1,0:T(8,128)(2,1)S(1)} %shard_map.37.refs_1_.refs_3_.refs_0_, bf16[2048,2048]{1,0:T(8,128)(2,1)S(1)} %copy-done, bf16[64,2048]{1,0:T(8,128)(2,1)S(1)} %shard_map.37.refs_1_.refs_3_.refs_0_), custom_call_target="tpu_custom_call" | custom-call | tf_op jit(solution)/shard_map/pallas_call | solution.py:31
  8.7 1.6 %collective-permute-start.4 = (bf16[64,2048]{1,0:T(8,128)(2,1)S(1)}, bf16[64,2048]{1,0:T(8,128)(2,1)S(1)}, u32[]{:S(2)}, u32[]{:S(2)}) collective-permute-start(bf16[64,2048]{1,0:T(8,128)(2,1)S(1)} %get-tuple-element.8.refs_1_.refs_0_), channel_id=1, source_target_pairs={{0,4},{1,5},{2,6},{3,7},{4,0},{5,1},{6,2},{7,3},{8,12},{9,13},{10,... | collective-permute-start | bytes 786440 | tf_op jit(solution)/shard_map/ppermute | solution.py:61
  10.4 1.0 %collective-permute-start.3 = (bf16[64,2048]{1,0:T(8,128)(2,1)S(1)}, bf16[64,2048]{1,0:T(8,128)(2,1)S(1)}, u32[]{:S(2)}, u32[]{:S(2)}) collective-permute-start(bf16[64,2048]{1,0:T(8,128)(2,1)S(1)} %shard_map.39.refs_2_), channel_id=1, source_target_pairs={{0,3},{1,2},{2,1},{3,0},{4,7},{5,6},{6,5},{7,4},{8,11},{9,10},{10,... | collective-permute-start | bytes 786440 | tf_op jit(solution)/shard_map/ppermute | solution.py:64
  11.4 0.0 collective-permute-done.1.refs_0_
  11.4 1.6 %shard_map.40.refs_2_.refs_0_ = bf16[64,2048]{1,0:T(8,128)(2,1)S(1)} custom-call(bf16[64,2048]{1,0:T(8,128)(2,1)S(1)} %collective-permute-done.1.refs_0_, bf16[2048,2048]{1,0:T(8,128)(2,1)S(1)} %copy-done.1, bf16[64,2048]{1,0:T(8,128)(2,1)S(1)} %shard_map.39.refs_2_), custom_call_target="tpu_custom_call" | custom-call | tf_op jit(solution)/shard_map/pallas_call | solution.py:31
  12.9 0.0 slice-start
  12.9 1.5 %collective-permute-start.2 = (bf16[64,2048]{1,0:T(8,128)(2,1)S(1)}, bf16[64,2048]{1,0:T(8,128)(2,1)S(1)}, u32[]{:S(2)}, u32[]{:S(2)}) collective-permute-start(bf16[64,2048]{1,0:T(8,128)(2,1)S(1)} %shard_map.40.refs_2_.refs_0_), channel_id=1, source_target_pairs={{0,4},{1,5},{2,6},{3,7},{4,0},{5,1},{6,2},{7,3},{8,12},{9,13},{10,... | collective-permute-start | bytes 786440 | tf_op jit(solution)/shard_map/ppermute | solution.py:61
  14.5 3.5 %collective-permute-done.4.refs_1_ = bf16[64,2048]{1,0:T(8,128)(2,1)S(1)} collective-permute-done((bf16[64,2048]{1,0:T(8,128)(2,1)S(1)}, bf16[64,2048]{1,0:T(8,128)(2,1)S(1)}, u32[]{:S(2)}, u32[]{:S(2)}) %collective-permute-start.4) | collective-permute-done | bytes 262176 | tf_op jit(solution)/shard_map/ppermute | solution.py:61
  17.9 0.1 shard_map.41.refs_2_.refs_0_
  18.0 0.0 slice-start.1
  18.0 0.1 collective-permute-start.6
  18.1 0.9 %collective-permute-done.3.refs_0_ = bf16[64,2048]{1,0:T(8,128)(2,1)S(1)} collective-permute-done((bf16[64,2048]{1,0:T(8,128)(2,1)S(1)}, bf16[64,2048]{1,0:T(8,128)(2,1)S(1)}, u32[]{:S(2)}, u32[]{:S(2)}) %collective-permute-start.3) | collective-permute-done | bytes 262176 | tf_op jit(solution)/shard_map/ppermute | solution.py:64
  19.0 1.6 %shard_map.42.refs_2_.refs_0_ = bf16[64,2048]{1,0:T(8,128)(2,1)S(1)} custom-call(bf16[64,2048]{1,0:T(8,128)(2,1)S(1)} %collective-permute-done.3.refs_0_, bf16[2048,2048]{1,0:T(8,128)(2,1)S(1)} %copy-done.1, bf16[64,2048]{1,0:T(8,128)(2,1)S(1)} %shard_map.41.refs_2_.refs_0_), custom_call_target="tpu_custom_call" | custom-call | tf_op jit(solution)/shard_map/pallas_call | solution.py:31
  20.6 2.2 %collective-permute-done.2.refs_1_ = bf16[64,2048]{1,0:T(8,128)(2,1)S(1)} collective-permute-done((bf16[64,2048]{1,0:T(8,128)(2,1)S(1)}, bf16[64,2048]{1,0:T(8,128)(2,1)S(1)}, u32[]{:S(2)}, u32[]{:S(2)}) %collective-permute-start.2) | collective-permute-done | bytes 262176 | tf_op jit(solution)/shard_map/ppermute | solution.py:61
  22.8 0.1 shard_map.43.refs_2_.refs_0_
  22.9 0.0 collective-permute-done.6.refs_1_
  22.9 0.1 shard_map.44.refs_1_.refs_2_.refs_0_
  23.0 3.6 %collective-permute-start.7 = (bf16[64,2048]{1,0:T(8,128)(2,1)S(1)}, bf16[64,2048]{1,0:T(8,128)(2,1)S(1)}, u32[]{:S(2)}, u32[]{:S(2)}) collective-permute-start(bf16[64,2048]{1,0:T(8,128)(2,1)S(1)} %shard_map.45.refs_2_), channel_id=1, source_target_pairs={{0,4},{1,5},{2,6},{3,7},{4,0},{5,1},{6,2},{7,3},{8,12},{9,13},{10,... | collective-permute-start | bytes 786440 | tf_op jit(solution)/shard_map/ppermute | solution.py:61
  26.6 4.3 %collective-permute-done.7.refs_1_ = bf16[64,2048]{1,0:T(8,128)(2,1)S(1)} collective-permute-done((bf16[64,2048]{1,0:T(8,128)(2,1)S(1)}, bf16[64,2048]{1,0:T(8,128)(2,1)S(1)}, u32[]{:S(2)}, u32[]{:S(2)}) %collective-permute-start.7) | collective-permute-done | bytes 262176 | tf_op jit(solution)/shard_map/ppermute | solution.py:61
  31.0 0.1 shard_map.46.refs_2_.refs_0_
  31.1 0.0 collective-permute-done.5.refs_1_
  31.1 0.1 shard_map.47.refs_1_.refs_2_.refs_0_
  31.2 2.3 %collective-permute-start.8 = (bf16[64,2048]{1,0:T(8,128)(2,1)S(1)}, bf16[64,2048]{1,0:T(8,128)(2,1)S(1)}, u32[]{:S(2)}, u32[]{:S(2)}) collective-permute-start(bf16[64,2048]{1,0:T(8,128)(2,1)S(1)} %shard_map.48.refs_3_), channel_id=1, source_target_pairs={{0,4},{1,5},{2,6},{3,7},{4,0},{5,1},{6,2},{7,3},{8,12},{9,13},{10,... | collective-permute-start | bytes 786440 | tf_op jit(solution)/shard_map/ppermute | solution.py:61
  33.5 0.0 collective-permute-start.10
  33.5 2.0 %shard_map.49.refs_2_ = bf16[64,1536]{1,0:T(8,128)(2,1)S(1)} custom-call(bf16[64,2048]{1,0:T(8,128)(2,1)S(1)} %shard_map.44.refs_1_.refs_2_.refs_0_, bf16[64,2048]{1,0:T(8,128)(2,1)S(1)} %collective-permute-done.7.refs_1_, bf16[1536,2048]{1,0:T(8,128)(2,1)S(1)} %bitcast.1, bf16[64,2048]{1,0:T(8,128)(2,1)S(1)} %shard_map.48.refs_3_), custom_call_target="tpu_custom_call" | custom-call | tf_op jit(solution)/shard_map/pallas_call | solution.py:31
  35.5 2.3 %collective-permute-done.8.refs_1_ = bf16[64,2048]{1,0:T(8,128)(2,1)S(1)} collective-permute-done((bf16[64,2048]{1,0:T(8,128)(2,1)S(1)}, bf16[64,2048]{1,0:T(8,128)(2,1)S(1)}, u32[]{:S(2)}, u32[]{:S(2)}) %collective-permute-start.8) | collective-permute-done | bytes 262176 | tf_op jit(solution)/shard_map/ppermute | solution.py:61
  37.8 0.1 shard_map.50.refs_2_.refs_0_
  37.9 0.1 collective-permute-start.9
  38.0 0.0 collective-permute-done.10.refs_1_
  38.0 0.1 shard_map.51.refs_3_.refs_0_
  38.1 3.8 %collective-permute-start.12 = (bf16[64,2048]{1,0:T(8,128)(2,1)S(1)}, bf16[64,2048]{1,0:T(8,128)(2,1)S(1)}, u32[]{:S(2)}, u32[]{:S(2)}) collective-permute-start(bf16[64,2048]{1,0:T(8,128)(2,1)S(1)} %shard_map.51.refs_3_.refs_0_), channel_id=1, source_target_pairs={{0,4},{1,5},{2,6},{3,7},{4,0},{5,1},{6,2},{7,3},{8,12},{9,13},{10,... | collective-permute-start | bytes 786440 | tf_op jit(solution)/shard_map/ppermute | solution.py:61
  41.9 2.0 %shard_map.52.refs_2_ = bf16[64,1536]{1,0:T(8,128)(2,1)S(1)} custom-call(bf16[64,2048]{1,0:T(8,128)(2,1)S(1)} %shard_map.47.refs_1_.refs_2_.refs_0_, bf16[64,2048]{1,0:T(8,128)(2,1)S(1)} %collective-permute-done.8.refs_1_, bf16[1536,2048]{1,0:T(8,128)(2,1)S(1)} %bitcast.1, bf16[64,2048]{1,0:T(8,128)(2,1)S(1)} %shard_map.51.refs_3_.refs_0_), custom_call_target="tpu_custom_call" | custom-call | tf_op jit(solution)/shard_map/pallas_call | solution.py:31
  43.9 0.0 collective-permute-done.9.refs_1_
  43.9 0.1 shard_map.53.refs_3_.refs_0_
  44.0 2.5 %collective-permute-start.11 = (bf16[64,2048]{1,0:T(8,128)(2,1)S(1)}, bf16[64,2048]{1,0:T(8,128)(2,1)S(1)}, u32[]{:S(2)}, u32[]{:S(2)}) collective-permute-start(bf16[64,2048]{1,0:T(8,128)(2,1)S(1)} %shard_map.53.refs_3_.refs_0_), channel_id=1, source_target_pairs={{0,4},{1,5},{2,6},{3,7},{4,0},{5,1},{6,2},{7,3},{8,12},{9,13},{10,... | collective-permute-start | bytes 786440 | tf_op jit(solution)/shard_map/ppermute | solution.py:61
  46.5 1.4 %collective-permute-start.14 = (bf16[64,1536]{1,0:T(8,128)(2,1)S(1)}, bf16[64,1536]{1,0:T(8,128)(2,1)S(1)}, u32[]{:S(2)}, u32[]{:S(2)}) collective-permute-start(bf16[64,1536]{1,0:T(8,128)(2,1)S(1)} %shard_map.52.refs_2_), channel_id=1, source_target_pairs={{0,2},{1,3},{2,0},{3,1},{4,6},{5,7},{6,4},{7,5},{8,10},{9,11},{10,... | collective-permute-start | bytes 589832 | tf_op jit(solution)/shard_map/ppermute | solution.py:64
  47.9 1.2 %collective-permute-done.12.refs_1_ = bf16[64,2048]{1,0:T(8,128)(2,1)S(1)} collective-permute-done((bf16[64,2048]{1,0:T(8,128)(2,1)S(1)}, bf16[64,2048]{1,0:T(8,128)(2,1)S(1)}, u32[]{:S(2)}, u32[]{:S(2)}) %collective-permute-start.12) | collective-permute-done | bytes 262176 | tf_op jit(solution)/shard_map/ppermute | solution.py:61
  49.1 2.0 %shard_map.54.refs_3_ = bf16[64,1536]{1,0:T(8,128)(2,1)S(1)} custom-call(bf16[64,2048]{1,0:T(8,128)(2,1)S(1)} %shard_map.51.refs_3_.refs_0_, bf16[64,2048]{1,0:T(8,128)(2,1)S(1)} %collective-permute-done.12.refs_1_, bf16[1536,2048]{1,0:T(8,128)(2,1)S(1)} %bitcast.1, bf16[64,2048]{1,0:T(8,128)(2,1)S(1)} %shard_map.53.refs_3_.refs_0_), custom_call_target="tpu_custom_call" | custom-call | tf_op jit(solution)/shard_map/pallas_call | solution.py:31
  51.1 0.1 collective-permute-start.15
  51.2 1.3 %collective-permute-done.11.refs_1_ = bf16[64,2048]{1,0:T(8,128)(2,1)S(1)} collective-permute-done((bf16[64,2048]{1,0:T(8,128)(2,1)S(1)}, bf16[64,2048]{1,0:T(8,128)(2,1)S(1)}, u32[]{:S(2)}, u32[]{:S(2)}) %collective-permute-start.11) | collective-permute-done | bytes 262176 | tf_op jit(solution)/shard_map/ppermute | solution.py:61
  52.5 2.0 %shard_map.55.refs_0_.refs_4_ = f32[64,1536]{1,0:T(8,128)S(1)} custom-call(bf16[64,2048]{1,0:T(8,128)(2,1)S(1)} %shard_map.53.refs_3_.refs_0_, bf16[64,2048]{1,0:T(8,128)(2,1)S(1)} %collective-permute-done.11.refs_1_, bf16[1536,2048]{1,0:T(8,128)(2,1)S(1)} %bitcast.1, bf16[64,1536]{1,0:T(8,128)(2,1)S(1)} %shard_map.54.refs_3_), custom_call_target="tpu_custom_call" | custom-call | tf_op jit(solution)/shard_map/pallas_call | solution.py:31
  54.5 3.8 %collective-permute-done.15.refs_3_ = bf16[64,1536]{1,0:T(8,128)(2,1)S(1)} collective-permute-done((bf16[64,1536]{1,0:T(8,128)(2,1)S(1)}, bf16[64,1536]{1,0:T(8,128)(2,1)S(1)}, u32[]{:S(2)}, u32[]{:S(2)}) %collective-permute-start.15) | collective-permute-done | bytes 196640 | tf_op jit(solution)/shard_map/ppermute | solution.py:64
  58.3 0.1 shard_map.56
  58.4 0.7 %copy.4 = f32[64,1536]{1,0:T(8,128)} copy(f32[64,1536]{1,0:T(8,128)S(1)} %shard_map.56) | data formatting | bytes 786432
  (16 shorter events, 0.1 us)
Async XLA Ops:
  0.0 0.9 %copy-start.2 = (bf16[64,2048]{1,0:T(8,128)(2,1)S(1)}, bf16[64,2048]{1,0:T(8,128)(2,1)}, u32[]{:S(2)}) copy-start(bf16[64,2048]{1,0:T(8,128)(2,1)} %refs_0_.1) | copy-start | bytes 786436
  1.0 3.1 %collective-permute-start = (bf16[64,2048]{1,0:T(8,128)(2,1)S(1)}, bf16[64,2048]{1,0:T(8,128)(2,1)S(1)}, u32[]{:S(2)}, u32[]{:S(2)}) collective-permute-start(bf16[64,2048]{1,0:T(8,128)(2,1)S(1)} %shard_map.37.refs_1_.refs_3_.refs_0_), channel_id=1, source_target_pairs={{0,1},{1,0},{2,3},{3,2},{4,5},{5,4},{6,7},{7,6},{8,9},{9,8},{10,11... | collective-permute-start | bytes 786440 | tf_op jit(solution)/shard_map/ppermute | solution.py:64
  1.5 9.9 %collective-permute-start.1 = (bf16[64,2048]{1,0:T(8,128)(2,1)S(1)}, bf16[64,2048]{1,0:T(8,128)(2,1)S(1)}, u32[]{:S(2)}, u32[]{:S(2)}) collective-permute-start(bf16[64,2048]{1,0:T(8,128)(2,1)S(1)} %shard_map.37.refs_1_.refs_3_.refs_0_), channel_id=1, source_target_pairs={{0,2},{1,3},{2,0},{3,1},{4,6},{5,7},{6,4},{7,5},{8,10},{9,11},{10,... | collective-permute-start | bytes 786440 | tf_op jit(solution)/shard_map/ppermute | solution.py:64
  4.1 3.4 %copy-start = (bf16[2048,2048]{1,0:T(8,128)(2,1)S(1)}, bf16[2048,2048]{1,0:T(8,128)(2,1)}, u32[]{:S(2)}) copy-start(bf16[2048,2048]{1,0:T(8,128)(2,1)} %refs_1_.3) | copy-start | bytes 25165828
  7.4 3.9 %copy-start.1 = (bf16[2048,2048]{1,0:T(8,128)(2,1)S(1)}, bf16[2048,2048]{1,0:T(8,128)(2,1)}, u32[]{:S(2)}) copy-start(bf16[2048,2048]{1,0:T(8,128)(2,1)} %refs_1_.3) | copy-start | bytes 25165828
  8.7 9.2 %collective-permute-start.4 = (bf16[64,2048]{1,0:T(8,128)(2,1)S(1)}, bf16[64,2048]{1,0:T(8,128)(2,1)S(1)}, u32[]{:S(2)}, u32[]{:S(2)}) collective-permute-start(bf16[64,2048]{1,0:T(8,128)(2,1)S(1)} %get-tuple-element.8.refs_1_.refs_0_), channel_id=1, source_target_pairs={{0,4},{1,5},{2,6},{3,7},{4,0},{5,1},{6,2},{7,3},{8,12},{9,13},{10,... | collective-permute-start | bytes 786440 | tf_op jit(solution)/shard_map/ppermute | solution.py:61
  10.4 8.6 %collective-permute-start.3 = (bf16[64,2048]{1,0:T(8,128)(2,1)S(1)}, bf16[64,2048]{1,0:T(8,128)(2,1)S(1)}, u32[]{:S(2)}, u32[]{:S(2)}) collective-permute-start(bf16[64,2048]{1,0:T(8,128)(2,1)S(1)} %shard_map.39.refs_2_), channel_id=1, source_target_pairs={{0,3},{1,2},{2,1},{3,0},{4,7},{5,6},{6,5},{7,4},{8,11},{9,10},{10,... | collective-permute-start | bytes 786440 | tf_op jit(solution)/shard_map/ppermute | solution.py:64
  12.9 20.6 %slice-start = ((s8[6291456]{0:T(1024)(128)(4,1)}), s8[4194304]{0:T(1024)(128)(4,1)S(1)}, s32[]{:S(2)}) async-start(s8[6291456]{0:T(1024)(128)(4,1)} %bitcast), calls=%async_computation | async-start | bytes 8388608
  12.9 9.8 %collective-permute-start.2 = (bf16[64,2048]{1,0:T(8,128)(2,1)S(1)}, bf16[64,2048]{1,0:T(8,128)(2,1)S(1)}, u32[]{:S(2)}, u32[]{:S(2)}) collective-permute-start(bf16[64,2048]{1,0:T(8,128)(2,1)S(1)} %shard_map.40.refs_2_.refs_0_), channel_id=1, source_target_pairs={{0,4},{1,5},{2,6},{3,7},{4,0},{5,1},{6,2},{7,3},{8,12},{9,13},{10,... | collective-permute-start | bytes 786440 | tf_op jit(solution)/shard_map/ppermute | solution.py:61
  18.0 15.5 %slice-start.1 = ((s8[6291456]{0:T(1024)(128)(4,1)}), s8[2097152]{0:T(1024)(128)(4,1)S(1)}, s32[]{:S(2)}) async-start(s8[6291456]{0:T(1024)(128)(4,1)} %bitcast), calls=%async_computation.1 | async-start | bytes 4194304
  18.0 4.8 %collective-permute-start.6 = (bf16[64,2048]{1,0:T(8,128)(2,1)S(1)}, bf16[64,2048]{1,0:T(8,128)(2,1)S(1)}, u32[]{:S(2)}, u32[]{:S(2)}) collective-permute-start(bf16[64,2048]{1,0:T(8,128)(2,1)S(1)} %shard_map.41.refs_2_.refs_0_), channel_id=1, source_target_pairs={{0,1},{1,0},{2,3},{3,2},{4,8},{5,9},{6,10},{7,11},{8,4},{9,5},{10,... | collective-permute-start | bytes 786440 | tf_op jit(solution)/shard_map/ppermute | solution.py:61
  23.0 8.0 %collective-permute-start.7 = (bf16[64,2048]{1,0:T(8,128)(2,1)S(1)}, bf16[64,2048]{1,0:T(8,128)(2,1)S(1)}, u32[]{:S(2)}, u32[]{:S(2)}) collective-permute-start(bf16[64,2048]{1,0:T(8,128)(2,1)S(1)} %shard_map.45.refs_2_), channel_id=1, source_target_pairs={{0,4},{1,5},{2,6},{3,7},{4,0},{5,1},{6,2},{7,3},{8,12},{9,13},{10,... | collective-permute-start | bytes 786440 | tf_op jit(solution)/shard_map/ppermute | solution.py:61
  26.6 4.4 %collective-permute-start.5 = (bf16[64,2048]{1,0:T(8,128)(2,1)S(1)}, bf16[64,2048]{1,0:T(8,128)(2,1)S(1)}, u32[]{:S(2)}, u32[]{:S(2)}) collective-permute-start(bf16[64,2048]{1,0:T(8,128)(2,1)S(1)} %shard_map.43.refs_2_.refs_0_), channel_id=1, source_target_pairs={{0,1},{1,0},{2,3},{3,2},{4,8},{5,9},{6,10},{7,11},{8,4},{9,5},{10,... | collective-permute-start | bytes 786440 | tf_op jit(solution)/shard_map/ppermute | solution.py:61
  31.2 6.6 %collective-permute-start.8 = (bf16[64,2048]{1,0:T(8,128)(2,1)S(1)}, bf16[64,2048]{1,0:T(8,128)(2,1)S(1)}, u32[]{:S(2)}, u32[]{:S(2)}) collective-permute-start(bf16[64,2048]{1,0:T(8,128)(2,1)S(1)} %shard_map.48.refs_3_), channel_id=1, source_target_pairs={{0,4},{1,5},{2,6},{3,7},{4,0},{5,1},{6,2},{7,3},{8,12},{9,13},{10,... | collective-permute-start | bytes 786440 | tf_op jit(solution)/shard_map/ppermute | solution.py:61
  33.5 4.5 %collective-permute-start.10 = (bf16[64,2048]{1,0:T(8,128)(2,1)S(1)}, bf16[64,2048]{1,0:T(8,128)(2,1)S(1)}, u32[]{:S(2)}, u32[]{:S(2)}) collective-permute-start(bf16[64,2048]{1,0:T(8,128)(2,1)S(1)} %shard_map.46.refs_2_.refs_0_), channel_id=1, source_target_pairs={{0,1},{1,0},{2,3},{3,2},{4,8},{5,9},{6,10},{7,11},{8,4},{9,5},{10,... | collective-permute-start | bytes 786440 | tf_op jit(solution)/shard_map/ppermute | solution.py:61
  37.9 6.0 %collective-permute-start.9 = (bf16[64,2048]{1,0:T(8,128)(2,1)S(1)}, bf16[64,2048]{1,0:T(8,128)(2,1)S(1)}, u32[]{:S(2)}, u32[]{:S(2)}) collective-permute-start(bf16[64,2048]{1,0:T(8,128)(2,1)S(1)} %shard_map.50.refs_2_.refs_0_), channel_id=1, source_target_pairs={{0,1},{1,0},{2,3},{3,2},{4,8},{5,9},{6,10},{7,11},{8,4},{9,5},{10,... | collective-permute-start | bytes 786440 | tf_op jit(solution)/shard_map/ppermute | solution.py:61
  38.1 11.0 %collective-permute-start.12 = (bf16[64,2048]{1,0:T(8,128)(2,1)S(1)}, bf16[64,2048]{1,0:T(8,128)(2,1)S(1)}, u32[]{:S(2)}, u32[]{:S(2)}) collective-permute-start(bf16[64,2048]{1,0:T(8,128)(2,1)S(1)} %shard_map.51.refs_3_.refs_0_), channel_id=1, source_target_pairs={{0,4},{1,5},{2,6},{3,7},{4,0},{5,1},{6,2},{7,3},{8,12},{9,13},{10,... | collective-permute-start | bytes 786440 | tf_op jit(solution)/shard_map/ppermute | solution.py:61
  44.0 8.5 %collective-permute-start.11 = (bf16[64,2048]{1,0:T(8,128)(2,1)S(1)}, bf16[64,2048]{1,0:T(8,128)(2,1)S(1)}, u32[]{:S(2)}, u32[]{:S(2)}) collective-permute-start(bf16[64,2048]{1,0:T(8,128)(2,1)S(1)} %shard_map.53.refs_3_.refs_0_), channel_id=1, source_target_pairs={{0,4},{1,5},{2,6},{3,7},{4,0},{5,1},{6,2},{7,3},{8,12},{9,13},{10,... | collective-permute-start | bytes 786440 | tf_op jit(solution)/shard_map/ppermute | solution.py:61
  46.5 8.0 %collective-permute-start.13 = (bf16[64,1536]{1,0:T(8,128)(2,1)S(1)}, bf16[64,1536]{1,0:T(8,128)(2,1)S(1)}, u32[]{:S(2)}, u32[]{:S(2)}) collective-permute-start(bf16[64,1536]{1,0:T(8,128)(2,1)S(1)} %shard_map.49.refs_2_), channel_id=1, source_target_pairs={{0,1},{1,0},{2,3},{3,2},{4,5},{5,4},{6,7},{7,6},{8,9},{9,8},{10,11... | collective-permute-start | bytes 589832 | tf_op jit(solution)/shard_map/ppermute | solution.py:64
  46.5 8.0 %collective-permute-start.14 = (bf16[64,1536]{1,0:T(8,128)(2,1)S(1)}, bf16[64,1536]{1,0:T(8,128)(2,1)S(1)}, u32[]{:S(2)}, u32[]{:S(2)}) collective-permute-start(bf16[64,1536]{1,0:T(8,128)(2,1)S(1)} %shard_map.52.refs_2_), channel_id=1, source_target_pairs={{0,2},{1,3},{2,0},{3,1},{4,6},{5,7},{6,4},{7,5},{8,10},{9,11},{10,... | collective-permute-start | bytes 589832 | tf_op jit(solution)/shard_map/ppermute | solution.py:64
  51.1 7.2 %collective-permute-start.15 = (bf16[64,1536]{1,0:T(8,128)(2,1)S(1)}, bf16[64,1536]{1,0:T(8,128)(2,1)S(1)}, u32[]{:S(2)}, u32[]{:S(2)}) collective-permute-start(bf16[64,1536]{1,0:T(8,128)(2,1)S(1)} %shard_map.54.refs_3_), channel_id=1, source_target_pairs={{0,3},{1,2},{2,1},{3,0},{4,7},{5,6},{6,5},{7,4},{8,11},{9,10},{10,... | collective-permute-start | bytes 589832 | tf_op jit(solution)/shard_map/ppermute | solution.py:64

commit v3 on v2

v3 whole, which is shorter than its diff:
```python
import jax
import jax.numpy as jnp
from jax import lax
from jax.experimental import pallas as pl
from jax.experimental.pallas import tpu as pltpu
from jax.sharding import PartitionSpec as P

VMEM = pl.BlockSpec(memory_space=pltpu.VMEM)
ANY = pl.BlockSpec(memory_space=pl.ANY)
BF16, F32 = jnp.bfloat16, jnp.float32
SPLIT = 1
LAG = 1


def dot(a, b):
    return jnp.dot(a, b, preferred_element_type=F32)


def dot_t(a, b):
    return lax.dot_general(a, b, (((1,), (1,)), ((), ())), preferred_element_type=F32)


class Order:
    def __init__(self):
        self.last = ()

    def __call__(self, kernel, shapes, *args, in_place=(), scratch=(), limit=12 << 20):
        n_args, n_extra = len(args), len(self.last)

        def ordered(*refs):
            kernel(*refs[:n_args], *refs[n_args + n_extra :])

        outs = pl.pallas_call(
            ordered,
            out_shape=tuple(pltpu.VMEM(shape, dtype) for shape, dtype in shapes),
            in_specs=[ANY if i in in_place else VMEM for i in range(n_args)] + [VMEM] * n_extra,
            out_specs=(VMEM,) * len(shapes),
            scratch_shapes=scratch,
            compiler_params=pltpu.CompilerParams(vmem_limit_bytes=limit),
            cost_estimate=pl.CostEstimate(flops=0, bytes_accessed=0, transcendentals=0),
        )(*args, *self.last)
        self.last = (outs[0],)
        return outs


def make_body(n_rows, n_proj):
    half = n_rows // 2
    hops = half - 1

    def both_ways(pairs):
        partner = {i: j for a, b in pairs for i, j in ((a, b), (b, a))}
        swaps = []
        for z in range(n_rows):
            for p in range(n_proj):
                to = (partner[z], p) if z in partner else (z, p ^ 1)
                swaps.append((z * n_proj + p, to[0] * n_proj + to[1]))
        return swaps

    hop_swaps = [both_ways([(h, h + 1), (n_rows - 1 - h, n_rows - 2 - h)]) for h in range(hops)]
    middle_swaps = both_ways([(half - 1, half)])

    def along(x, swaps):
        return lax.ppermute(x, ("rows", "proj"), swaps)

    def across(x, d):
        return lax.ppermute(x, "proj", [(i, i ^ d) for i in range(n_proj)])

    def at(h):
        z = lax.axis_index("rows")
        return (z == h) | (z == n_rows - 1 - h)

    def body(targets, precond, train):
        call = Order()
        m, k = targets.shape
        n, t = precond.shape[1], train.shape[0]
        size = m // SPLIT

        def elementwise(function, *args):
            small = min(x.shape[0] for x in args)
            longest = max(range(len(args)), key=lambda i: args[i].shape[0])
            large = args[longest].shape[0]

            def kernel(*refs):
                *in_refs, out_ref = refs
                out_ref[:small] = function(*[r[:small] for r in in_refs])
                if large > small:
                    out_ref[small:] = in_refs[longest][small:]

            return call(kernel, [((large, *args[0].shape[1:]), BF16)], *args)[0]

        def update(function, kept, got):
            def kernel(kept_ref, got_ref, out_ref):
                out_ref[...] = function(kept_ref[...], got_ref[: kept.shape[0]])

            return call(kernel, [(kept.shape, BF16)], kept, got)[0]

        def plus(a, b):
            return (a.astype(F32) + b.astype(F32)).astype(BF16)

        def first_condition(left):
            blocks = 8 if k % (8 * 256) == 0 else 1
            step, width = k // blocks, min(n, 512)

            def kernel(left_ref, precond_hbm, *refs):
                *out_refs, precond_ref, sum_ref, sems = refs
                copies = []
                for i in range(blocks):
                    part = pl.ds(i * step, step)
                    copies.append(pltpu.make_async_copy(precond_hbm.at[part], precond_ref.at[part], sems.at[i]))
                    copies[i].start()
                for i in range(blocks):
                    copies[i].wait()
                    part = slice(i * step, (i + 1) * step)
                    for lo in range(0, n, width):
                        cols = slice(lo, lo + width)
                        value = dot(left_ref[:, part], precond_ref[part, cols])
                        if i > 0:
                            value = value + sum_ref[:, cols]
                        if i < blocks - 1:
                            sum_ref[:, cols] = value
                        else:
                            for j, out_ref in enumerate(out_refs):
                                out_ref[:, cols] = value[j * size : (j + 1) * size].astype(BF16)

            *out, kept = call(
                kernel,
                [((size, n), BF16)] * SPLIT + [(precond.shape, BF16)],
                left,
                pltpu.with_memory_space_constraint(precond, pltpu.HBM),
                in_place=(1,),
                scratch=(pltpu.VMEM((m, n), F32), pltpu.SemaphoreType.DMA((blocks,))),
            )
            return out, kept

        def condition(*lefts):
            step = min(n, 512)
            count = len(lefts) * SPLIT

            def kernel(*refs):
                left_refs, precond_ref, out_refs = refs[: len(lefts)], refs[len(lefts)], refs[len(lefts) + 1 :]
                left = jnp.concatenate([r[...] for r in left_refs])
                for lo in range(0, n, step):
                    cols = slice(lo, lo + step)
                    value = dot(left, precond_ref[:, cols]).astype(BF16)
                    for j, out_ref in enumerate(out_refs):
                        out_ref[:, cols] = value[j * size : (j + 1) * size]

            return call(kernel, [((size, n), BF16)] * count, *lefts, weights)

        def scores(groups, dtype):
            step = t // 3

            def kernel(*refs):
                total_refs, train_ref, out_refs = refs[: -1 - len(groups)], refs[-1 - len(groups)], refs[-len(groups) :]
                left = jnp.concatenate([r[...] for r in total_refs])
                for lo in range(0, t, step):
                    cols = slice(lo, lo + step)
                    value = dot_t(left, train_ref[cols, :]).astype(dtype)
                    for j, out_ref in enumerate(out_refs):
                        out_ref[:, cols] = value[j * m : (j + 1) * m]

            return call(kernel, [((m, t), dtype)] * len(groups), *sum(groups, []), train)

        owners = [1, *[d ^ 1 for d in range(2, n_proj)], 0]
        n_chunks = n_proj * SPLIT
        rows = {0: targets}
        here, total, parts, moving = {}, {}, {}, {}

        def same(x):
            return elementwise(lambda v: v, x)

        def fetch(i, value):
            rows[owners[i]] = across(value, owners[i])

        def begin(*group):
            new = condition(*[rows[owners[i]] for i in group])
            here.update(zip([c for i in group for c in range(i * SPLIT, (i + 1) * SPLIT)], new, strict=True))

        def valid(c):
            return 0 <= c < n_chunks

        def outward(h, step):
            return step - 2 * hops + h - LAG

        def start_hop(h, step):
            c, back = step - h, outward(h, step)
            if valid(c) and valid(back):
                value = elementwise(lambda a, b: jnp.where(at(h), a, b), here[c], total[back])
            elif valid(c):
                value = same(here[c]) if step > 0 else here[c]
            elif valid(back):
                value = same(total[back])
            else:
                return
            moving[h, step] = along(value, hop_swaps[h])

        def end_hop(h, step):
            c, back = step - h, outward(h, step)
            if valid(c):
                here[c] = update(lambda a, b: jnp.where(at(h + 1), plus(a, b), a), here[c], moving[h, step])
            if valid(back):
                total[back] = update(lambda a, b: jnp.where(at(h), b, a), total[back], moving[h, step])

        def gather(i):
            def kernel(*refs):
                *in_refs, out_ref = refs
                value = in_refs[0][...].astype(F32)
                for ref in in_refs[1:]:
                    value = value + ref[...].astype(F32)
                out_ref[...] = value

            terms = ([parts["sum"]] if "sum" in parts else []) + [parts[i]]
            parts["sum"] = call(kernel, [((m, t), F32)], *terms)[0]

        def finish(*group):
            values = scores([[total[c] for c in range(i * SPLIT, (i + 1) * SPLIT)] for i in group], F32 if owners[group[0]] == 0 else BF16)
            for i, value in zip(group, values):
                parts[i] = across(value, owners[i]) if owners[i] else value

        rows[1] = across(targets, 1)
        fetch(1, targets)
        first, weights = first_condition(rows[1])
        here.update(enumerate(first))
        start_hop(0, 0)
        if n_proj > 3:
            fetch(2, same(targets))
        begin(1)
        start_hop(0, 1)
        finished = 0
        for step in range(1, n_chunks + 2 * hops + LAG + 1):
            for h in reversed(range(hops)):
                end_hop(h, step - 1)
            c = step - hops
            if valid(c):
                moving["middle", step] = along(here[c], middle_swaps)
            for h in range(1, hops):
                start_hop(h, step)
            i = step // SPLIT + 1
            if step % SPLIT == 0 and 1 < i < n_proj - 1:
                if i + 1 < n_proj - 1:
                    fetch(i + 1, same(targets))
                begin(*([i] if i < n_proj - 2 else [i, i + 1]))
            c = step - 1 - 2 * hops - LAG
            if valid(c) and c % SPLIT == SPLIT - 1:
                i = c // SPLIT
                if i > 0:
                    finish(*([i] if i > 1 else [0, 1]))
                if 1 < i < n_proj - 1:
                    gather(i - 2)
                    gather(i - 1) if i == n_proj - 2 else None
            c = step - 1 - hops
            if valid(c):
                total[c] = update(plus, here[c], moving["middle", step - 1])
            start_hop(0, step + 1)

        gather(n_proj - 2)
        gather(n_proj - 1)
        return parts["sum"]

    return body


def solution(mesh):
    return jax.shard_map(
        make_body(mesh.shape["rows"], mesh.shape["proj"]),
        mesh=mesh,
        in_specs=(P("proj", "rows"), P(("groups", "rows"), "proj"), P(("groups", "rows"), "proj")),
        out_specs=P("proj", ("groups", "rows")),
        check_vma=False,
    )
```

time: 59.3 us -> 56 us (0.944)
  starting transfers between devices: 21.1 us -> 26.8 us
  waiting for transfers between devices: 19.6 us -> 14.2 us
  local copies, waits for them, and re-layouts: 5.1 us -> 0.77 us
  Pallas kernels: 13.2 us -> 13.8 us
    ppermute x10 -> x11, waiting for transfers between devices: 14.8 us -> 8.3 us  [along(): return lax.ppermute(x, ('rows', 'proj'), swaps)]
    unnamed x11 -> x7, local copies, waits for them, and re-layouts: 5.1 us -> 0.77 us
    ppermute x10 -> x11, starting transfers between devices: 15.6 us -> 19.4 us  [along(): return lax.ppermute(x, ('rows', 'proj'), swaps)]
    ppermute x6, starting transfers between devices: 5.52 us -> 7.4 us  [across(): return lax.ppermute(x, 'proj', [(i, i ^ d) for i in range(n_proj)])]
    ppermute x6, waiting for transfers between devices: 4.72 us -> 5.9 us  [across(): return lax.ppermute(x, 'proj', [(i, i ^ d) for i in range(n_proj)])]
    pallas_call x20 -> x29, Pallas kernels: 13.2 us -> 13.8 us  [__call__(): pl.pallas_call(ordered, out_shape=tuple((pltpu.VMEM(shape, dtype) for sha...]
  transfers between devices with their start and end apart: 16 -> 17, of which waited for: 8 -> 8; matrix products, arithmetic and copies ran while one was open for 0% -> 0% of each run, Pallas kernels for 22% -> 25%
where the time goes in v3:
time: 56 us; the launch traced here: 55.9 us
  starting transfers between devices  26.8 us (48%)
  waiting for transfers between devices  14.2 us (25%)
  Pallas kernels  13.8 us (25%)
  local copies, waits for them, and re-layouts  0.77 us (1%)
    ppermute x11, starting transfers between devices, along(): return lax.ppermute(x, ('rows', 'proj'), swaps)  19.4 us
    pallas_call x29, Pallas kernels, __call__(): pl.pallas_call(ordered, out_shape=tuple((pltpu.VMEM(shape, dtype) for sha...  13.8 us
    ppermute x11, waiting for transfers between devices, along(): return lax.ppermute(x, ('rows', 'proj'), swaps)  8.3 us
    ppermute x6, starting transfers between devices, across(): return lax.ppermute(x, 'proj', [(i, i ^ d) for i in range(n_proj)])  7.4 us
    ppermute x6, waiting for transfers between devices, across(): return lax.ppermute(x, 'proj', [(i, i ^ d) for i in range(n_proj)])  5.9 us
  transfers between devices with their start and end apart: 17, of which 8 were waited for; matrix products, arithmetic and copies ran while one was open for 0% of the time, Pallas kernels for 25%

profile of v3, /device:TPU:0, one launch (start us, length us, event | category | flops | bytes accessed | tf_op | source)
XLA Modules:
  0.0 55.9 jit_solution(17487911237122523554)
XLA Ops:
  0.0 0.5 collective-permute-start
  0.5 2.6 %collective-permute-start.2 = (bf16[64,2048]{1,0:T(8,128)(2,1)}, bf16[64,2048]{1,0:T(8,128)(2,1)S(1)}, u32[]{:S(2)}, u32[]{:S(2)}) collective-permute-start(bf16[64,2048]{1,0:T(8,128)(2,1)} %refs_1_.5), channel_id=1, source_target_pairs={{0,3},{1,2},{2,1},{3,0},{4,7},{5,6},{6,5},{7,4},{8,11},{9,10},{10,... | collective-permute-start | bytes 786440 | tf_op jit(solution)/shard_map/ppermute | solution.py:66
  3.1 0.0 collective-permute-done.refs_0_
  3.1 3.8 %shard_map.37 = (bf16[64,2048]{1,0:T(8,128)(2,1)S(1)}, bf16[2048,2048]{1,0:T(8,128)(2,1)S(1)}) custom-call(bf16[64,2048]{1,0:T(8,128)(2,1)S(1)} %collective-permute-done.refs_0_, bf16[2048,2048]{1,0:T(8,128)(2,1)} %refs_1_.4), custom_call_target="tpu_custom_call" | custom-call | tf_op jit(solution)/shard_map/pallas_call | solution.py:33
  6.8 1.8 %collective-permute-start.1 = (bf16[64,2048]{1,0:T(8,128)(2,1)S(1)}, bf16[64,2048]{1,0:T(8,128)(2,1)S(1)}, u32[]{:S(2)}, u32[]{:S(2)}) collective-permute-start(bf16[64,2048]{1,0:T(8,128)(2,1)S(1)} %get-tuple-element.11.refs_1_.refs_0_), channel_id=1, source_target_pairs={{0,4},{1,5},{2,6},{3,7},{4,0},{5,1},{6,2},{7,3},{8,12},{9,13},{10,... | collective-permute-start | bytes 786440 | tf_op jit(solution)/shard_map/ppermute | solution.py:63
  8.6 1.6 %collective-permute-start.5 = (bf16[64,2048]{1,0:T(8,128)(2,1)S(1)}, bf16[64,2048]{1,0:T(8,128)(2,1)S(1)}, u32[]{:S(2)}, u32[]{:S(2)}) collective-permute-start(bf16[64,2048]{1,0:T(8,128)(2,1)S(1)} %shard_map.38.refs_2_), channel_id=1, source_target_pairs={{0,2},{1,3},{2,0},{3,1},{4,6},{5,7},{6,4},{7,5},{8,10},{9,11},{10,... | collective-permute-start | bytes 786440 | tf_op jit(solution)/shard_map/ppermute | solution.py:66
  10.2 1.6 %shard_map.39.refs_0_.refs_1_ = bf16[64,2048]{1,0:T(8,128)(2,1)S(1)} custom-call(bf16[64,2048]{1,0:T(8,128)(2,1)S(1)} %collective-permute-done.2.refs_0_, bf16[2048,2048]{1,0:T(8,128)(2,1)S(1)} %get-tuple-element.12.refs_1_.refs_2_, bf16[64,2048]{1,0:T(8,128)(2,1)S(1)} %shard_map.38.refs_2_), custom_call_target="tpu_custom_call" | custom-call | tf_op jit(solution)/shard_map/pallas_call | solution.py:33
  11.8 1.2 %collective-permute-start.4 = (bf16[64,2048]{1,0:T(8,128)(2,1)S(1)}, bf16[64,2048]{1,0:T(8,128)(2,1)S(1)}, u32[]{:S(2)}, u32[]{:S(2)}) collective-permute-start(bf16[64,2048]{1,0:T(8,128)(2,1)S(1)} %shard_map.40.refs_2_), channel_id=1, source_target_pairs={{0,4},{1,5},{2,6},{3,7},{4,0},{5,1},{6,2},{7,3},{8,12},{9,13},{10,... | collective-permute-start | bytes 786440 | tf_op jit(solution)/shard_map/ppermute | solution.py:63
  13.0 2.5 %collective-permute-done.1.refs_1_ = bf16[64,2048]{1,0:T(8,128)(2,1)S(1)} collective-permute-done((bf16[64,2048]{1,0:T(8,128)(2,1)S(1)}, bf16[64,2048]{1,0:T(8,128)(2,1)S(1)}, u32[]{:S(2)}, u32[]{:S(2)}) %collective-permute-start.1) | collective-permute-done | bytes 262176 | tf_op jit(solution)/shard_map/ppermute | solution.py:63
  15.5 0.1 shard_map.41.refs_3_.refs_0_
  15.6 0.0 slice-start
  15.6 0.1 collective-permute-start.3
  15.7 1.1 %collective-permute-done.5.refs_0_ = bf16[64,2048]{1,0:T(8,128)(2,1)S(1)} collective-permute-done((bf16[64,2048]{1,0:T(8,128)(2,1)S(1)}, bf16[64,2048]{1,0:T(8,128)(2,1)S(1)}, u32[]{:S(2)}, u32[]{:S(2)}) %collective-permute-start.5) | collective-permute-done | bytes 262176 | tf_op jit(solution)/shard_map/ppermute | solution.py:66
  16.8 1.3 %shard_map.42 = (bf16[64,2048]{1,0:T(8,128)(2,1)S(1)}, bf16[64,2048]{1,0:T(8,128)(2,1)S(1)}) custom-call(bf16[64,2048]{1,0:T(8,128)(2,1)S(1)} %collective-permute-done.5.refs_0_, bf16[64,2048]{1,0:T(8,128)(2,1)S(1)} %copy-done, bf16[2048,2048]{1,0:T(8,128)(2,1)S(1)} %get-tuple-element.12.refs_1_.refs_2_, bf16[64,2048]{1,0:T(8,128)(2,1)S(1)} %shard_map.41.refs_3_.refs_0_), custom_call_target="tpu_custom_call" | custom-call | tf_op jit(solution)/shard_map/pallas_call | solution.py:33
  18.1 0.0 slice-start.1
  18.1 2.8 %collective-permute-start.8 = (bf16[64,2048]{1,0:T(8,128)(2,1)S(1)}, bf16[64,2048]{1,0:T(8,128)(2,1)S(1)}, u32[]{:S(2)}, u32[]{:S(2)}) collective-permute-start(bf16[64,2048]{1,0:T(8,128)(2,1)S(1)} %shard_map.43.refs_2_), channel_id=1, source_target_pairs={{0,4},{1,5},{2,6},{3,7},{4,0},{5,1},{6,2},{7,3},{8,12},{9,13},{10,... | collective-permute-start | bytes 786440 | tf_op jit(solution)/shard_map/ppermute | solution.py:63
  20.9 0.2 collective-permute-done.4.refs_1_
  21.1 0.1 shard_map.44.refs_2_.refs_0_
  21.2 0.1 collective-permute-start.7
  21.3 0.0 collective-permute-done.3.refs_1_
  21.3 0.1 shard_map.45.refs_1_.refs_2_.refs_0_
  21.4 3.5 %collective-permute-start.6 = (bf16[64,2048]{1,0:T(8,128)(2,1)S(1)}, bf16[64,2048]{1,0:T(8,128)(2,1)S(1)}, u32[]{:S(2)}, u32[]{:S(2)}) collective-permute-start(bf16[64,2048]{1,0:T(8,128)(2,1)S(1)} %shard_map.46.refs_2_), channel_id=1, source_target_pairs={{0,4},{1,5},{2,6},{3,7},{4,0},{5,1},{6,2},{7,3},{8,12},{9,13},{10,... | collective-permute-start | bytes 786440 | tf_op jit(solution)/shard_map/ppermute | solution.py:63
  24.9 3.2 %collective-permute-done.8.refs_1_ = bf16[64,2048]{1,0:T(8,128)(2,1)S(1)} collective-permute-done((bf16[64,2048]{1,0:T(8,128)(2,1)S(1)}, bf16[64,2048]{1,0:T(8,128)(2,1)S(1)}, u32[]{:S(2)}, u32[]{:S(2)}) %collective-permute-start.8) | collective-permute-done | bytes 262176 | tf_op jit(solution)/shard_map/ppermute | solution.py:63
  28.1 0.1 shard_map.47.refs_2_.refs_0_
  28.2 0.1 collective-permute-start.10
  28.3 0.0 collective-permute-done.7.refs_1_
  28.3 0.1 shard_map.48.refs_0_.refs_1_
  28.4 3.2 %collective-permute-start.9 = (bf16[64,2048]{1,0:T(8,128)(2,1)S(1)}, bf16[64,2048]{1,0:T(8,128)(2,1)S(1)}, u32[]{:S(2)}, u32[]{:S(2)}) collective-permute-start(bf16[64,2048]{1,0:T(8,128)(2,1)S(1)} %shard_map.49.refs_2_), channel_id=1, source_target_pairs={{0,4},{1,5},{2,6},{3,7},{4,0},{5,1},{6,2},{7,3},{8,12},{9,13},{10,... | collective-permute-start | bytes 786440 | tf_op jit(solution)/shard_map/ppermute | solution.py:63
  31.6 1.2 %collective-permute-done.6.refs_1_ = bf16[64,2048]{1,0:T(8,128)(2,1)S(1)} collective-permute-done((bf16[64,2048]{1,0:T(8,128)(2,1)S(1)}, bf16[64,2048]{1,0:T(8,128)(2,1)S(1)}, u32[]{:S(2)}, u32[]{:S(2)}) %collective-permute-start.6) | collective-permute-done | bytes 262176 | tf_op jit(solution)/shard_map/ppermute | solution.py:63
  32.8 0.1 shard_map.50.refs_2_.refs_0_
  32.9 0.1 collective-permute-start.13
  33.0 0.0 collective-permute-done.10.refs_1_
  33.0 0.1 shard_map.52.refs_0_.refs_1_
  33.1 4.5 %collective-permute-start.12 = (bf16[64,2048]{1,0:T(8,128)(2,1)S(1)}, bf16[64,2048]{1,0:T(8,128)(2,1)S(1)}, u32[]{:S(2)}, u32[]{:S(2)}) collective-permute-start(bf16[64,2048]{1,0:T(8,128)(2,1)S(1)} %shard_map.53.refs_2_), channel_id=1, source_target_pairs={{0,4},{1,5},{2,6},{3,7},{4,0},{5,1},{6,2},{7,3},{8,12},{9,13},{10,... | collective-permute-start | bytes 786440 | tf_op jit(solution)/shard_map/ppermute | solution.py:63
  37.6 1.1 %collective-permute-done.9.refs_1_ = bf16[64,2048]{1,0:T(8,128)(2,1)S(1)} collective-permute-done((bf16[64,2048]{1,0:T(8,128)(2,1)S(1)}, bf16[64,2048]{1,0:T(8,128)(2,1)S(1)}, u32[]{:S(2)}, u32[]{:S(2)}) %collective-permute-start.9) | collective-permute-done | bytes 262176 | tf_op jit(solution)/shard_map/ppermute | solution.py:63
  38.8 2.2 %shard_map.55 = (bf16[64,1536]{1,0:T(8,128)(2,1)S(1)}, bf16[64,1536]{1,0:T(8,128)(2,1)S(1)}) custom-call(bf16[64,2048]{1,0:T(8,128)(2,1)S(1)} %shard_map.51.refs_2_.refs_0_, bf16[64,2048]{1,0:T(8,128)(2,1)S(1)} %shard_map.54.refs_1_.refs_3_, bf16[1536,2048]{1,0:T(8,128)(2,1)S(1)} %bitcast.1, bf16[64,2048]{1,0:T(8,128)(2,1)S(1)} %shard_map.54.refs_1_.refs_3_), custom_call_target="tpu_custom_call" | custom-call | tf_op jit(solution)/shard_map/pallas_call | solution.py:33
  41.0 0.0 collective-permute-done.13.refs_1_
  41.0 0.1 shard_map.56.refs_0_.refs_1_
  41.1 2.2 %collective-permute-start.16 = (bf16[64,2048]{1,0:T(8,128)(2,1)S(1)}, bf16[64,2048]{1,0:T(8,128)(2,1)S(1)}, u32[]{:S(2)}, u32[]{:S(2)}) collective-permute-start(bf16[64,2048]{1,0:T(8,128)(2,1)S(1)} %shard_map.57.refs_2_), channel_id=1, source_target_pairs={{0,4},{1,5},{2,6},{3,7},{4,0},{5,1},{6,2},{7,3},{8,12},{9,13},{10,... | collective-permute-start | bytes 786440 | tf_op jit(solution)/shard_map/ppermute | solution.py:63
  43.3 0.0 collective-permute-start.11
  43.3 2.1 %collective-permute-start.14 = (bf16[64,1536]{1,0:T(8,128)(2,1)S(1)}, bf16[64,1536]{1,0:T(8,128)(2,1)S(1)}, u32[]{:S(2)}, u32[]{:S(2)}) collective-permute-start(bf16[64,1536]{1,0:T(8,128)(2,1)S(1)} %get-tuple-element.16), channel_id=1, source_target_pairs={{0,3},{1,2},{2,1},{3,0},{4,7},{5,6},{6,5},{7,4},{8,11},{9,10},{10,... | collective-permute-start | bytes 589832 | tf_op jit(solution)/shard_map/ppermute | solution.py:66
  45.4 0.0 collective-permute-done.12.refs_1_
  45.4 2.0 %shard_map.59.refs_1_ = bf16[64,1536]{1,0:T(8,128)(2,1)S(1)} custom-call(bf16[64,2048]{1,0:T(8,128)(2,1)S(1)} %shard_map.58.refs_0_.refs_2_, bf16[1536,2048]{1,0:T(8,128)(2,1)S(1)} %bitcast.1, bf16[64,2048]{1,0:T(8,128)(2,1)S(1)} %shard_map.58.refs_0_.refs_2_), custom_call_target="tpu_custom_call" | custom-call | tf_op jit(solution)/shard_map/pallas_call | solution.py:33
  47.4 0.7 %collective-permute-start.15 = (bf16[64,1536]{1,0:T(8,128)(2,1)S(1)}, bf16[64,1536]{1,0:T(8,128)(2,1)S(1)}, u32[]{:S(2)}, u32[]{:S(2)}) collective-permute-start(bf16[64,1536]{1,0:T(8,128)(2,1)S(1)} %shard_map.59.refs_1_), channel_id=1, source_target_pairs={{0,2},{1,3},{2,0},{3,1},{4,6},{5,7},{6,4},{7,5},{8,10},{9,11},{10,... | collective-permute-start | bytes 589832 | tf_op jit(solution)/shard_map/ppermute | solution.py:66
  48.2 2.5 %collective-permute-done.14.refs_1_ = bf16[64,1536]{1,0:T(8,128)(2,1)S(1)} collective-permute-done((bf16[64,1536]{1,0:T(8,128)(2,1)S(1)}, bf16[64,1536]{1,0:T(8,128)(2,1)S(1)}, u32[]{:S(2)}, u32[]{:S(2)}) %collective-permute-start.14) | collective-permute-done | bytes 196640 | tf_op jit(solution)/shard_map/ppermute | solution.py:66
  50.7 2.0 %shard_map.63.refs_2_.refs_1_ = f32[64,1536]{1,0:T(8,128)S(1)} custom-call(bf16[64,2048]{1,0:T(8,128)(2,1)S(1)} %shard_map.62.refs_0_.refs_2_, bf16[1536,2048]{1,0:T(8,128)(2,1)S(1)} %bitcast.1, bf16[64,2048]{1,0:T(8,128)(2,1)S(1)} %shard_map.62.refs_0_.refs_2_), custom_call_target="tpu_custom_call" | custom-call | tf_op jit(solution)/shard_map/pallas_call | solution.py:33
  52.7 2.3 %collective-permute-done.15.refs_1_ = bf16[64,1536]{1,0:T(8,128)(2,1)S(1)} collective-permute-done((bf16[64,1536]{1,0:T(8,128)(2,1)S(1)}, bf16[64,1536]{1,0:T(8,128)(2,1)S(1)}, u32[]{:S(2)}, u32[]{:S(2)}) %collective-permute-start.15) | collective-permute-done | bytes 196640 | tf_op jit(solution)/shard_map/ppermute | solution.py:66
  55.2 0.7 %copy.4 = f32[64,1536]{1,0:T(8,128)} copy(f32[64,1536]{1,0:T(8,128)S(1)} %shard_map.65) | data formatting | bytes 786432
  (23 shorter events, 0.4 us)
Async XLA Ops:
  0.0 8.6 %copy-start = (bf16[64,2048]{1,0:T(8,128)(2,1)S(1)}, bf16[64,2048]{1,0:T(8,128)(2,1)}, u32[]{:S(2)}) copy-start(bf16[64,2048]{1,0:T(8,128)(2,1)} %refs_1_.5) | copy-start | bytes 786436
  0.0 3.1 %collective-permute-start = (bf16[64,2048]{1,0:T(8,128)(2,1)}, bf16[64,2048]{1,0:T(8,128)(2,1)S(1)}, u32[]{:S(2)}, u32[]{:S(2)}) collective-permute-start(bf16[64,2048]{1,0:T(8,128)(2,1)} %refs_1_.5), channel_id=1, source_target_pairs={{0,1},{1,0},{2,3},{3,2},{4,5},{5,4},{6,7},{7,6},{8,9},{9,8},{10,11... | collective-permute-start | bytes 786440 | tf_op jit(solution)/shard_map/ppermute | solution.py:66
  0.5 9.7 %collective-permute-start.2 = (bf16[64,2048]{1,0:T(8,128)(2,1)}, bf16[64,2048]{1,0:T(8,128)(2,1)S(1)}, u32[]{:S(2)}, u32[]{:S(2)}) collective-permute-start(bf16[64,2048]{1,0:T(8,128)(2,1)} %refs_1_.5), channel_id=1, source_target_pairs={{0,3},{1,2},{2,1},{3,0},{4,7},{5,6},{6,5},{7,4},{8,11},{9,10},{10,... | collective-permute-start | bytes 786440 | tf_op jit(solution)/shard_map/ppermute | solution.py:66
  6.8 8.6 %collective-permute-start.1 = (bf16[64,2048]{1,0:T(8,128)(2,1)S(1)}, bf16[64,2048]{1,0:T(8,128)(2,1)S(1)}, u32[]{:S(2)}, u32[]{:S(2)}) collective-permute-start(bf16[64,2048]{1,0:T(8,128)(2,1)S(1)} %get-tuple-element.11.refs_1_.refs_0_), channel_id=1, source_target_pairs={{0,4},{1,5},{2,6},{3,7},{4,0},{5,1},{6,2},{7,3},{8,12},{9,13},{10,... | collective-permute-start | bytes 786440 | tf_op jit(solution)/shard_map/ppermute | solution.py:63
  8.6 8.1 %collective-permute-start.5 = (bf16[64,2048]{1,0:T(8,128)(2,1)S(1)}, bf16[64,2048]{1,0:T(8,128)(2,1)S(1)}, u32[]{:S(2)}, u32[]{:S(2)}) collective-permute-start(bf16[64,2048]{1,0:T(8,128)(2,1)S(1)} %shard_map.38.refs_2_), channel_id=1, source_target_pairs={{0,2},{1,3},{2,0},{3,1},{4,6},{5,7},{6,4},{7,5},{8,10},{9,11},{10,... | collective-permute-start | bytes 786440 | tf_op jit(solution)/shard_map/ppermute | solution.py:66
  11.8 9.3 %collective-permute-start.4 = (bf16[64,2048]{1,0:T(8,128)(2,1)S(1)}, bf16[64,2048]{1,0:T(8,128)(2,1)S(1)}, u32[]{:S(2)}, u32[]{:S(2)}) collective-permute-start(bf16[64,2048]{1,0:T(8,128)(2,1)S(1)} %shard_map.40.refs_2_), channel_id=1, source_target_pairs={{0,4},{1,5},{2,6},{3,7},{4,0},{5,1},{6,2},{7,3},{8,12},{9,13},{10,... | collective-permute-start | bytes 786440 | tf_op jit(solution)/shard_map/ppermute | solution.py:63
  15.6 23.3 %slice-start = ((s8[6291456]{0:T(1024)(128)(4,1)}), s8[2097152]{0:T(1024)(128)(4,1)S(1)}, s32[]{:S(2)}) async-start(s8[6291456]{0:T(1024)(128)(4,1)} %bitcast), calls=%async_computation | async-start | bytes 4194304
  15.6 5.7 %collective-permute-start.3 = (bf16[64,2048]{1,0:T(8,128)(2,1)S(1)}, bf16[64,2048]{1,0:T(8,128)(2,1)S(1)}, u32[]{:S(2)}, u32[]{:S(2)}) collective-permute-start(bf16[64,2048]{1,0:T(8,128)(2,1)S(1)} %shard_map.41.refs_3_.refs_0_), channel_id=1, source_target_pairs={{0,1},{1,0},{2,3},{3,2},{4,8},{5,9},{6,10},{7,11},{8,4},{9,5},{10,... | collective-permute-start | bytes 786440 | tf_op jit(solution)/shard_map/ppermute | solution.py:63
  18.1 20.8 %slice-start.1 = ((s8[6291456]{0:T(1024)(128)(4,1)}), s8[4194304]{0:T(1024)(128)(4,1)S(1)}, s32[]{:S(2)}) async-start(s8[6291456]{0:T(1024)(128)(4,1)} %bitcast), calls=%async_computation.1 | async-start | bytes 8388608
  18.1 10.0 %collective-permute-start.8 = (bf16[64,2048]{1,0:T(8,128)(2,1)S(1)}, bf16[64,2048]{1,0:T(8,128)(2,1)S(1)}, u32[]{:S(2)}, u32[]{:S(2)}) collective-permute-start(bf16[64,2048]{1,0:T(8,128)(2,1)S(1)} %shard_map.43.refs_2_), channel_id=1, source_target_pairs={{0,4},{1,5},{2,6},{3,7},{4,0},{5,1},{6,2},{7,3},{8,12},{9,13},{10,... | collective-permute-start | bytes 786440 | tf_op jit(solution)/shard_map/ppermute | solution.py:63
  21.2 7.1 %collective-permute-start.7 = (bf16[64,2048]{1,0:T(8,128)(2,1)S(1)}, bf16[64,2048]{1,0:T(8,128)(2,1)S(1)}, u32[]{:S(2)}, u32[]{:S(2)}) collective-permute-start(bf16[64,2048]{1,0:T(8,128)(2,1)S(1)} %shard_map.44.refs_2_.refs_0_), channel_id=1, source_target_pairs={{0,1},{1,0},{2,3},{3,2},{4,8},{5,9},{6,10},{7,11},{8,4},{9,5},{10,... | collective-permute-start | bytes 786440 | tf_op jit(solution)/shard_map/ppermute | solution.py:63
  21.4 11.4 %collective-permute-start.6 = (bf16[64,2048]{1,0:T(8,128)(2,1)S(1)}, bf16[64,2048]{1,0:T(8,128)(2,1)S(1)}, u32[]{:S(2)}, u32[]{:S(2)}) collective-permute-start(bf16[64,2048]{1,0:T(8,128)(2,1)S(1)} %shard_map.46.refs_2_), channel_id=1, source_target_pairs={{0,4},{1,5},{2,6},{3,7},{4,0},{5,1},{6,2},{7,3},{8,12},{9,13},{10,... | collective-permute-start | bytes 786440 | tf_op jit(solution)/shard_map/ppermute | solution.py:63
  28.2 4.8 %collective-permute-start.10 = (bf16[64,2048]{1,0:T(8,128)(2,1)S(1)}, bf16[64,2048]{1,0:T(8,128)(2,1)S(1)}, u32[]{:S(2)}, u32[]{:S(2)}) collective-permute-start(bf16[64,2048]{1,0:T(8,128)(2,1)S(1)} %shard_map.47.refs_2_.refs_0_), channel_id=1, source_target_pairs={{0,1},{1,0},{2,3},{3,2},{4,8},{5,9},{6,10},{7,11},{8,4},{9,5},{10,... | collective-permute-start | bytes 786440 | tf_op jit(solution)/shard_map/ppermute | solution.py:63
  28.4 10.4 %collective-permute-start.9 = (bf16[64,2048]{1,0:T(8,128)(2,1)S(1)}, bf16[64,2048]{1,0:T(8,128)(2,1)S(1)}, u32[]{:S(2)}, u32[]{:S(2)}) collective-permute-start(bf16[64,2048]{1,0:T(8,128)(2,1)S(1)} %shard_map.49.refs_2_), channel_id=1, source_target_pairs={{0,4},{1,5},{2,6},{3,7},{4,0},{5,1},{6,2},{7,3},{8,12},{9,13},{10,... | collective-permute-start | bytes 786440 | tf_op jit(solution)/shard_map/ppermute | solution.py:63
  32.9 8.1 %collective-permute-start.13 = (bf16[64,2048]{1,0:T(8,128)(2,1)S(1)}, bf16[64,2048]{1,0:T(8,128)(2,1)S(1)}, u32[]{:S(2)}, u32[]{:S(2)}) collective-permute-start(bf16[64,2048]{1,0:T(8,128)(2,1)S(1)} %shard_map.50.refs_2_.refs_0_), channel_id=1, source_target_pairs={{0,1},{1,0},{2,3},{3,2},{4,8},{5,9},{6,10},{7,11},{8,4},{9,5},{10,... | collective-permute-start | bytes 786440 | tf_op jit(solution)/shard_map/ppermute | solution.py:63
  33.1 12.3 %collective-permute-start.12 = (bf16[64,2048]{1,0:T(8,128)(2,1)S(1)}, bf16[64,2048]{1,0:T(8,128)(2,1)S(1)}, u32[]{:S(2)}, u32[]{:S(2)}) collective-permute-start(bf16[64,2048]{1,0:T(8,128)(2,1)S(1)} %shard_map.53.refs_2_), channel_id=1, source_target_pairs={{0,4},{1,5},{2,6},{3,7},{4,0},{5,1},{6,2},{7,3},{8,12},{9,13},{10,... | collective-permute-start | bytes 786440 | tf_op jit(solution)/shard_map/ppermute | solution.py:63
  41.1 9.6 %collective-permute-start.16 = (bf16[64,2048]{1,0:T(8,128)(2,1)S(1)}, bf16[64,2048]{1,0:T(8,128)(2,1)S(1)}, u32[]{:S(2)}, u32[]{:S(2)}) collective-permute-start(bf16[64,2048]{1,0:T(8,128)(2,1)S(1)} %shard_map.57.refs_2_), channel_id=1, source_target_pairs={{0,4},{1,5},{2,6},{3,7},{4,0},{5,1},{6,2},{7,3},{8,12},{9,13},{10,... | collective-permute-start | bytes 786440 | tf_op jit(solution)/shard_map/ppermute | solution.py:63
  43.3 4.9 %collective-permute-start.11 = (bf16[64,1536]{1,0:T(8,128)(2,1)S(1)}, bf16[64,1536]{1,0:T(8,128)(2,1)S(1)}, u32[]{:S(2)}, u32[]{:S(2)}) collective-permute-start(bf16[64,1536]{1,0:T(8,128)(2,1)S(1)} %get-tuple-element.15.refs_2_), channel_id=1, source_target_pairs={{0,1},{1,0},{2,3},{3,2},{4,5},{5,4},{6,7},{7,6},{8,9},{9,8},{10,11... | collective-permute-start | bytes 589832 | tf_op jit(solution)/shard_map/ppermute | solution.py:66
  43.3 7.3 %collective-permute-start.14 = (bf16[64,1536]{1,0:T(8,128)(2,1)S(1)}, bf16[64,1536]{1,0:T(8,128)(2,1)S(1)}, u32[]{:S(2)}, u32[]{:S(2)}) collective-permute-start(bf16[64,1536]{1,0:T(8,128)(2,1)S(1)} %get-tuple-element.16), channel_id=1, source_target_pairs={{0,3},{1,2},{2,1},{3,0},{4,7},{5,6},{6,5},{7,4},{8,11},{9,10},{10,... | collective-permute-start | bytes 589832 | tf_op jit(solution)/shard_map/ppermute | solution.py:66
  47.4 7.6 %collective-permute-start.15 = (bf16[64,1536]{1,0:T(8,128)(2,1)S(1)}, bf16[64,1536]{1,0:T(8,128)(2,1)S(1)}, u32[]{:S(2)}, u32[]{:S(2)}) collective-permute-start(bf16[64,1536]{1,0:T(8,128)(2,1)S(1)} %shard_map.59.refs_1_), channel_id=1, source_target_pairs={{0,2},{1,3},{2,0},{3,1},{4,6},{5,7},{6,4},{7,5},{8,10},{9,11},{10,... | collective-permute-start | bytes 589832 | tf_op jit(solution)/shard_map/ppermute | solution.py:66

commit v4 on v3

v4 whole, which is shorter than its diff:
```python
import jax
import jax.numpy as jnp
from jax import lax
from jax.experimental import pallas as pl
from jax.experimental.pallas import tpu as pltpu
from jax.sharding import PartitionSpec as P

VMEM = pl.BlockSpec(memory_space=pltpu.VMEM)
ANY = pl.BlockSpec(memory_space=pl.ANY)
BF16, F32 = jnp.bfloat16, jnp.float32
WORK = 2 * 10**9
LAG = 1


def dot(a, b):
    return jnp.dot(a, b, preferred_element_type=F32)


def dot_t(a, b):
    return lax.dot_general(a, b, (((1,), (1,)), ((), ())), preferred_element_type=F32)


class Order:
    def __init__(self):
        self.last = ()

    def __call__(self, name, kernel, shapes, *args, in_place=(), scratch=(), work=0):
        n_args, n_extra = len(args), len(self.last)

        def ordered(*refs):
            kernel(*refs[:n_args], *refs[n_args + n_extra :])

        outs = pl.pallas_call(
            ordered,
            name=name,
            out_shape=tuple(pltpu.VMEM(shape, dtype) for shape, dtype in shapes),
            in_specs=[ANY if i in in_place else VMEM for i in range(n_args)] + [VMEM] * n_extra,
            out_specs=(VMEM,) * len(shapes),
            scratch_shapes=scratch,
            compiler_params=pltpu.CompilerParams(vmem_limit_bytes=12 << 20),
            cost_estimate=pl.CostEstimate(flops=work, bytes_accessed=0, transcendentals=0),
        )(*args, *self.last)
        self.last = (outs[0],)
        return outs


def make_body(n_rows, n_proj):
    half = n_rows // 2
    hops = half - 1

    def both_ways(pairs):
        partner = {i: j for a, b in pairs for i, j in ((a, b), (b, a))}
        swaps = []
        for z in range(n_rows):
            for p in range(n_proj):
                to = (partner[z], p) if z in partner else (z, p ^ 1)
                swaps.append((z * n_proj + p, to[0] * n_proj + to[1]))
        return swaps

    hop_swaps = [both_ways([(h, h + 1), (n_rows - 1 - h, n_rows - 2 - h)]) for h in range(hops)]
    middle_swaps = both_ways([(half - 1, half)])

    def along(x, swaps):
        return lax.ppermute(x, ("rows", "proj"), swaps)

    def across(x, d):
        return lax.ppermute(x, "proj", [(i, i ^ d) for i in range(n_proj)])

    def at(h):
        z = lax.axis_index("rows")
        return (z == h) | (z == n_rows - 1 - h)

    def body(targets, precond, train):
        call = Order()
        m, k = targets.shape
        n, t = precond.shape[1], train.shape[0]

        half_n = n // 2
        halves = (slice(0, half_n), slice(half_n, n))

        def elementwise(name, function, *args):
            small = min(x.shape[0] for x in args)
            longest = max(range(len(args)), key=lambda i: args[i].shape[0])
            large = args[longest].shape[0]

            def kernel(*refs):
                *in_refs, out_ref = refs
                out_ref[:small] = function(*[r[:small] for r in in_refs])
                if large > small:
                    out_ref[small:] = in_refs[longest][small:]

            return call(name, kernel, [((large, args[0].shape[1]), BF16)], *args, work=WORK)[0]

        def update(name, function, kept, got):
            def kernel(kept_ref, got_ref, out_ref):
                out_ref[...] = function(kept_ref[...], got_ref[: kept.shape[0]])

            return call(name, kernel, [(kept.shape, BF16)], kept, got, work=WORK)[0]

        def plus(a, b):
            return (a.astype(F32) + b.astype(F32)).astype(BF16)

        def read_condition(left, side):
            blocks = 4 if k % (4 * 256) == 0 else 1
            step, width = k // blocks, min(half_n, 512)

            def kernel(left_ref, precond_hbm, out_ref, precond_ref, sum_ref, sems):
                copies = []
                for i in range(blocks):
                    part = pl.ds(i * step, step)
                    source = precond_hbm.at[part, pl.ds(side * half_n, half_n)]
                    copies.append(pltpu.make_async_copy(source, precond_ref.at[part], sems.at[i]))
                    copies[i].start()
                for i in range(blocks):
                    copies[i].wait()
                    part = slice(i * step, (i + 1) * step)
                    for lo in range(0, half_n, width):
                        cols = slice(lo, lo + width)
                        value = dot(left_ref[:, part], precond_ref[part, cols])
                        if i > 0:
                            value = value + sum_ref[:, cols]
                        if i < blocks - 1:
                            sum_ref[:, cols] = value
                        else:
                            out_ref[:, cols] = value.astype(BF16)

            return call(
                f"read_condition_{side}",
                kernel,
                [((m, half_n), BF16), ((k, half_n), BF16)],
                left,
                pltpu.with_memory_space_constraint(precond, pltpu.HBM),
                in_place=(1,),
                scratch=(pltpu.VMEM((m, half_n), F32), pltpu.SemaphoreType.DMA((blocks,))),
            )

        def condition(name, left, ranges):
            step = min(half_n, 512)

            def kernel(left_ref, low_ref, high_ref, *out_refs):
                for side, ref in zip(halves, (low_ref, high_ref)):
                    for lo in range(0, half_n, step):
                        value = dot(left_ref[...], ref[:, lo : lo + step]).astype(BF16)
                        cols = slice(side.start + lo, side.start + lo + step)
                        for (top, end), out_ref in zip(ranges, out_refs):
                            out_ref[:, cols] = value[top:end]

            return call(name, kernel, [((end - top, n), BF16) for top, end in ranges], left, *weights, work=WORK)

        def transposed(x):
            step = min(512, x.shape[1])
            wide = t // 3 if t % 384 == 0 else t

            def kernel(x_ref, out_ref):
                for top in range(0, t, wide):
                    for lo in range(0, x.shape[1], step):
                        out_ref[lo : lo + step, top : top + wide] = x_ref[top : top + wide, lo : lo + step].T

            return call("transposed_train", kernel, [((x.shape[1], t), BF16)], x, work=WORK)[0]

        def scores(name, chunk, left, cols):
            def kernel(left_ref, train_ref, out_ref):
                out_ref[...] = dot(left_ref[...], train_ref[:, cols]).astype(BF16)

            return call(name, kernel, [((left.shape[0], cols.stop - cols.start), BF16)], left, trained[0], work=WORK if chunk < last - 1 else 0)[0]

        def last_scores(side, kept, given, *before):
            step = t // 3

            def kernel(kept_ref, given_ref, train_ref, *refs):
                *before_refs, out_ref = refs
                left = jnp.where(at(0), given_ref[...], kept_ref[...])
                for lo in range(0, t, step):
                    cols = slice(lo, lo + step)
                    value = dot(left, train_ref[halves[side], cols])
                    for ref in before_refs:
                        value = value + ref[:, cols]
                    out_ref[:, cols] = value

            return call(f"last_scores_{side}", kernel, [((m, t), F32)], kept, given, trained[0], *before)[0]

        owners = [1, *[d ^ 1 for d in range(2, n_proj)], 0]
        ranges = {d: [(0, m)] for d in owners}
        chunks = [(d, *r) for d in owners for r in ranges[d]]
        n_chunks = len(chunks)
        last = n_chunks - 1
        rows = {0: targets}
        here, total, parts, moving = {}, {}, {}, {}

        def same(name, x):
            return elementwise(name, lambda v: v, x)

        def fetch(i, value):
            rows[owners[i]] = across(value, owners[i])

        def begin(i):
            d = owners[i]
            first = chunks.index((d, *ranges[d][0]))
            here.update(enumerate(condition(f"condition_{i}", rows[d], ranges[d]), first))

        def valid(c):
            return 0 <= c < n_chunks

        back_at = 2 * hops + LAG + (hops > 1)

        def outward(h, step):
            return step - back_at if h == 0 else step - 2 * hops + h - LAG

        def start_hop(h, step):
            c, back = step - h, outward(h, step)
            if h == 0 and c == 0:
                moving[h, step] = [along(x, hop_swaps[h]) for x in here[c]]
                return
            if h == 0 and back == last:
                if hops > 1:

                    def kernel(x_ref, *out_refs):
                        for side, out_ref in zip(halves, out_refs):
                            out_ref[...] = x_ref[:, side]

                    total[back] = call("halves", kernel, [((m, half_n), BF16)] * 2, total[back])
                moving[h, step] = [along(x, hop_swaps[h]) for x in total[back]]
                return
            if valid(c) and valid(back):
                value = elementwise(f"merge_{step}", lambda a, b: jnp.where(at(h), a, b), here[c], total[back])
            elif valid(c):
                value = same(f"pass_{step}", here[c])
            elif valid(back):
                value = same(f"back_{step}", total[back])
            else:
                return
            moving[h, step] = along(value, hop_swaps[h])

        def end_hop(h, step):
            c, back = step - h, outward(h, step)

            def absorb(a, b):
                return jnp.where(at(h + 1), plus(a, b), a)

            if h == 0 and c == 0:
                low = update("absorb_0a", absorb, here[c][0], moving[h, step][0])

                def kernel(low_ref, a_ref, b_ref, out_ref):
                    out_ref[:, halves[0]] = low_ref[...]
                    out_ref[:, halves[1]] = absorb(a_ref[...], b_ref[...])

                here[c] = call("absorb_0b", kernel, [((m, n), BF16)], low, here[c][1], moving[h, step][1], work=WORK)[0]
            elif valid(c):
                here[c] = update(f"absorb_{step}", absorb, here[c], moving[h, step])
            if valid(back) and not (h == 0 and back == last):
                total[back] = update(f"adopt_{back}", lambda a, b: jnp.where(at(h), b, a), total[back], moving[h, step])

        def end_middle(c, step):
            if c == last and hops == 1:

                def kernel(a_ref, b_ref, *out_refs):
                    for side, out_ref in zip(halves, out_refs):
                        out_ref[...] = plus(a_ref[:, side], b_ref[:, side])

                total[c] = call("total_last", kernel, [((m, half_n), BF16)] * 2, here[c], moving["middle", step])
            else:
                total[c] = update(f"total_{c}", plus, here[c], moving["middle", step])

        def gather(c):
            for i, (cols, got) in enumerate(zip(pieces(c), parts[c])):
                first = c == 0 and i == 0

                def kernel(*refs):
                    *in_refs, out_ref = refs
                    if first:
                        out_ref[...] = jnp.zeros_like(out_ref)
                    else:
                        out_ref[...] = in_refs[0][...]
                    out_ref[:, cols] += in_refs[-1][...].astype(F32)

                before = [] if first else [parts["sum"]]
                parts["sum"] = call(f"gather_{c}_{i}", kernel, [((m, t), F32)], *before, got, work=WORK if c == last - 1 and i == 0 else 0)[0]

        def pieces(c):
            if c == last - 1 and t % 256 == 0:
                return [slice(0, t // 2), slice(t // 2, t)]
            return [slice(0, t)]

        def finish(c):
            parts[c] = []
            for i, cols in enumerate(pieces(c)):
                parts[c].append(across(scores(f"scores_{c}_{i}", c, total[c], cols), chunks[c][0]))

        for i in range(min(3, n_proj - 1)):
            fetch(i, targets)
        weights = []
        here[0] = []
        for side in (0, 1):
            out, half_weights = read_condition(rows[1], side)
            here[0].append(out)
            weights.append(half_weights)
        start_hop(0, 0)
        begin(1)
        start_hop(0, 1)
        trained = []
        for step in range(1, n_chunks + back_at):
            for h in reversed(range(hops)):
                end_hop(h, step - 1)
            c = step - hops
            if valid(c):
                moving["middle", step] = along(here[c], middle_swaps)
            for h in range(1, hops):
                start_hop(h, step)
            if step == 1:
                begin(n_proj - 1)
            if step + 1 < n_proj - 1:
                if step + 2 < n_proj - 1:
                    fetch(step + 2, same(f"own_rows_{step}", targets))
                begin(step + 1)
            c = step - 1 - back_at
            if valid(c):
                finish(c)
            if step == 2:
                trained.append(transposed(train))
            c = step - 1 - hops
            if valid(c):
                end_middle(c, step - 1)
            start_hop(0, step + 1)
        for c in range(last - 1):
            gather(c)
        value = None
        for side in (0, 1):
            before = [] if value is None else [value]
            value = last_scores(side, total[last][side], moving[0, last + back_at][side], *before)
        gather(last - 1)

        def close(sum_ref, value_ref, out_ref):
            out_ref[...] = sum_ref[...] + value_ref[...]

        return call("close", close, [((m, t), F32)], parts["sum"], value)[0]

    return body


def solution(mesh):
    return jax.shard_map(
        make_body(mesh.shape["rows"], mesh.shape["proj"]),
        mesh=mesh,
        in_specs=(P("proj", "rows"), P(("groups", "rows"), "proj"), P(("groups", "rows"), "proj")),
        out_specs=P("proj", ("groups", "rows")),
        check_vma=False,
    )
```

time: 56 us -> 53.4 us (0.954)
  starting transfers between devices: 26.8 us -> 23 us
  Pallas kernels: 13.8 us -> 17.4 us
  waiting for transfers between devices: 14.2 us -> 11.7 us
    ppermute x6 -> x7, waiting for transfers between devices: 5.9 us -> 1.06 us  [across(): return lax.ppermute(x, 'proj', [(i, i ^ d) for i in range(n_proj)])]
    pallas_call x29 -> x34, Pallas kernels: 13.8 us -> 17.4 us  [__call__(): pl.pallas_call(ordered, name=name, out_shape=tuple((pltpu.VMEM(shape, dty...]
    ppermute x11 -> x13, starting transfers between devices: 19.4 us -> 16.7 us  [along(): return lax.ppermute(x, ('rows', 'proj'), swaps)]
    ppermute x11 -> x13, waiting for transfers between devices: 8.3 us -> 10.6 us  [along(): return lax.ppermute(x, ('rows', 'proj'), swaps)]
    ppermute x6 -> x7, starting transfers between devices: 7.4 us -> 6.35 us  [across(): return lax.ppermute(x, 'proj', [(i, i ^ d) for i in range(n_proj)])]
  transfers between devices with their start and end apart: 17 -> 20, of which waited for: 8 -> 7; matrix products, arithmetic and copies ran while one was open for 0% -> 0% of each run, Pallas kernels for 25% -> 33%
where the time goes in v4:
time: 53.4 us; the launch traced here: 53.3 us
  starting transfers between devices  23 us (43%)
  Pallas kernels  17.4 us (33%)
  waiting for transfers between devices  11.7 us (22%)
  local copies, waits for them, and re-layouts  0.77 us (1%)
    pallas_call x34, Pallas kernels, __call__(): pl.pallas_call(ordered, name=name, out_shape=tuple((pltpu.VMEM(shape, dty...  17.4 us
    ppermute x13, starting transfers between devices, along(): return lax.ppermute(x, ('rows', 'proj'), swaps)  16.7 us
    ppermute x13, waiting for transfers between devices, along(): return lax.ppermute(x, ('rows', 'proj'), swaps)  10.6 us
    ppermute x7, starting transfers between devices, across(): return lax.ppermute(x, 'proj', [(i, i ^ d) for i in range(n_proj)])  6.35 us
  transfers between devices with their start and end apart: 20, of which 7 were waited for; matrix products, arithmetic and copies ran while one was open for 0% of the time, Pallas kernels for 33%

profile of v4, /device:TPU:0, one launch (start us, length us, event | category | flops | bytes accessed | tf_op | source)
XLA Modules:
  0.0 53.3 jit_solution(3230901442804642318)
XLA Ops:
  0.0 0.5 collective-permute-start
  0.5 2.6 %collective-permute-start.2 = (bf16[64,2048]{1,0:T(8,128)(2,1)}, bf16[64,2048]{1,0:T(8,128)(2,1)S(1)}, u32[]{:S(2)}, u32[]{:S(2)}) collective-permute-start(bf16[64,2048]{1,0:T(8,128)(2,1)} %refs_0_.2), channel_id=1, source_target_pairs={{0,3},{1,2},{2,1},{3,0},{4,7},{5,6},{6,5},{7,4},{8,11},{9,10},{10,... | collective-permute-start | bytes 786440 | tf_op jit(solution)/shard_map/ppermute | solution.py:67
  3.1 2.5 %read_condition_0.1 = (bf16[64,1024]{1,0:T(8,128)(2,1)S(1)}, bf16[2048,1024]{1,0:T(8,128)(2,1)S(1)}) custom-call(bf16[64,2048]{1,0:T(8,128)(2,1)S(1)} %collective-permute-done.refs_0_, bf16[2048,2048]{1,0:T(8,128)(2,1)} %refs_1_.3), custom_call_target="tpu_custom_call" | custom-call | tf_op jit(solution)/shard_map/read_condition_0/pallas_call | solution.py:33
  5.6 2.2 %collective-permute-start.1 = (bf16[64,1024]{1,0:T(8,128)(2,1)S(1)}, bf16[64,1024]{1,0:T(8,128)(2,1)S(1)}, u32[]{:S(2)}, u32[]{:S(2)}) collective-permute-start(bf16[64,1024]{1,0:T(8,128)(2,1)S(1)} %get-tuple-element.11.refs_2_.refs_0_), channel_id=1, source_target_pairs={{0,4},{1,5},{2,6},{3,7},{4,0},{5,1},{6,2},{7,3},{8,12},{9,13},{10,... | collective-permute-start | bytes 393224 | tf_op jit(solution)/shard_map/ppermute | solution.py:64
  7.8 2.5 %read_condition_1.1 = (bf16[64,1024]{1,0:T(8,128)(2,1)S(1)}, bf16[2048,1024]{1,0:T(8,128)(2,1)S(1)}) custom-call(bf16[64,2048]{1,0:T(8,128)(2,1)S(1)} %collective-permute-done.refs_0_, bf16[2048,2048]{1,0:T(8,128)(2,1)} %refs_1_.3, bf16[64,1024]{1,0:T(8,128)(2,1)S(1)} %get-tuple-element.11.refs_2_.refs_0_), custom_call_target="tpu_custom_call" | custom-call | tf_op jit(solution)/shard_map/read_condition_1/pallas_call | solution.py:33
  10.3 0.1 collective-permute-start.3
  10.4 1.6 %condition_1.1.refs_0_.refs_1_ = bf16[64,2048]{1,0:T(8,128)(2,1)S(1)} custom-call(bf16[64,2048]{1,0:T(8,128)(2,1)S(1)} %collective-permute-done.2.refs_0_, bf16[2048,1024]{1,0:T(8,128)(2,1)S(1)} %get-tuple-element.12.refs_1_, bf16[2048,1024]{1,0:T(8,128)(2,1)S(1)} %get-tuple-element.13.refs_2_, bf16[64,1024]{1,0:T(8,128)(2,1)S(1)} %get-tuple-element.14.refs_3_.refs_1_), custom_call_target="tpu_custom_call" | custom-call | flops 2000000000 | tf_op jit(solution)/shard_map/condition_1/pallas_call | solution.py:33
  12.0 2.1 %collective-permute-start.5 = (bf16[64,2048]{1,0:T(8,128)(2,1)S(1)}, bf16[64,2048]{1,0:T(8,128)(2,1)S(1)}, u32[]{:S(2)}, u32[]{:S(2)}) collective-permute-start(bf16[64,2048]{1,0:T(8,128)(2,1)S(1)} %pass_1.1.refs_2_), channel_id=1, source_target_pairs={{0,4},{1,5},{2,6},{3,7},{4,0},{5,1},{6,2},{7,3},{8,12},{9,13},{10,... | collective-permute-start | bytes 786440 | tf_op jit(solution)/shard_map/ppermute | solution.py:64
  14.1 1.3 %collective-permute-done.3.refs_2_ = bf16[64,1024]{1,0:T(8,128)(2,1)S(1)} collective-permute-done((bf16[64,1024]{1,0:T(8,128)(2,1)S(1)}, bf16[64,1024]{1,0:T(8,128)(2,1)S(1)}, u32[]{:S(2)}, u32[]{:S(2)}) %collective-permute-start.3) | collective-permute-done | bytes 131104 | tf_op jit(solution)/shard_map/ppermute | solution.py:64
  15.4 0.1 absorb_0b.1.refs_3_.refs_0_
  15.5 0.1 collective-permute-start.4
  15.6 1.6 %condition_3.1.refs_3_.refs_0_ = bf16[64,2048]{1,0:T(8,128)(2,1)S(1)} custom-call(bf16[64,2048]{1,0:T(8,128)(2,1)S(1)} %copy-done, bf16[2048,1024]{1,0:T(8,128)(2,1)S(1)} %get-tuple-element.12.refs_1_, bf16[2048,1024]{1,0:T(8,128)(2,1)S(1)} %get-tuple-element.13.refs_2_, bf16[64,2048]{1,0:T(8,128)(2,1)S(1)} %absorb_0b.1.refs_3_.refs_0_), custom_call_target="tpu_custom_call" | custom-call | flops 2000000000 | tf_op jit(solution)/shard_map/condition_3/pallas_call | solution.py:33
  17.2 1.6 %condition_2.1.refs_0_.refs_1_ = bf16[64,2048]{1,0:T(8,128)(2,1)S(1)} custom-call(bf16[64,2048]{1,0:T(8,128)(2,1)S(1)} %collective-permute-done.6.refs_0_, bf16[2048,1024]{1,0:T(8,128)(2,1)S(1)} %get-tuple-element.12.refs_1_, bf16[2048,1024]{1,0:T(8,128)(2,1)S(1)} %get-tuple-element.13.refs_2_, bf16[64,2048]{1,0:T(8,128)(2,1)S(1)} %condition_3.1.refs_3_.refs_0_), custom_call_target="tpu_custom_call" | custom-call | flops 2000000000 | tf_op jit(solution)/shard_map/condition_2/pallas_call | solution.py:33
  18.7 0.0 slice-start.1
  18.8 3.1 %collective-permute-start.9 = (bf16[64,2048]{1,0:T(8,128)(2,1)S(1)}, bf16[64,2048]{1,0:T(8,128)(2,1)S(1)}, u32[]{:S(2)}, u32[]{:S(2)}) collective-permute-start(bf16[64,2048]{1,0:T(8,128)(2,1)S(1)} %pass_2.1.refs_2_), channel_id=1, source_target_pairs={{0,4},{1,5},{2,6},{3,7},{4,0},{5,1},{6,2},{7,3},{8,12},{9,13},{10,... | collective-permute-start | bytes 786440 | tf_op jit(solution)/shard_map/ppermute | solution.py:64
  21.9 0.1 absorb_1.1.refs_1_.refs_0_
  22.0 0.1 collective-permute-start.8
  22.1 1.7 %transposed_train.1.refs_2_.refs_1_ = bf16[2048,1536]{1,0:T(8,128)(2,1)S(1)} custom-call(bf16[1536,2048]{1,0:T(8,128)(2,1)S(1)} %bitcast.1, bf16[64,2048]{1,0:T(8,128)(2,1)S(1)} %absorb_1.1.refs_1_.refs_0_), custom_call_target="tpu_custom_call" | custom-call | flops 2000000000 | tf_op jit(solution)/shard_map/transposed_train/pallas_call | solution.py:33
  23.8 0.1 total_0.1.refs_1_.refs_2_.refs_0_
  23.9 2.6 %collective-permute-start.7 = (bf16[64,2048]{1,0:T(8,128)(2,1)S(1)}, bf16[64,2048]{1,0:T(8,128)(2,1)S(1)}, u32[]{:S(2)}, u32[]{:S(2)}) collective-permute-start(bf16[64,2048]{1,0:T(8,128)(2,1)S(1)} %merge_3.1.refs_2_), channel_id=1, source_target_pairs={{0,4},{1,5},{2,6},{3,7},{4,0},{5,1},{6,2},{7,3},{8,12},{9,13},{10,... | collective-permute-start | bytes 786440 | tf_op jit(solution)/shard_map/ppermute | solution.py:64
  26.4 1.6 %collective-permute-done.9.refs_1_ = bf16[64,2048]{1,0:T(8,128)(2,1)S(1)} collective-permute-done((bf16[64,2048]{1,0:T(8,128)(2,1)S(1)}, bf16[64,2048]{1,0:T(8,128)(2,1)S(1)}, u32[]{:S(2)}, u32[]{:S(2)}) %collective-permute-start.9) | collective-permute-done | bytes 262176 | tf_op jit(solution)/shard_map/ppermute | solution.py:64
  28.0 0.1 absorb_2.1.refs_2_.refs_0_
  28.1 0.1 collective-permute-start.11
  28.2 0.1 total_1.1.refs_0_.refs_1_
  28.3 2.7 %collective-permute-start.14 = (bf16[64,2048]{1,0:T(8,128)(2,1)S(1)}, bf16[64,2048]{1,0:T(8,128)(2,1)S(1)}, u32[]{:S(2)}, u32[]{:S(2)}) collective-permute-start(bf16[64,2048]{1,0:T(8,128)(2,1)S(1)} %back_4.1.refs_2_), channel_id=1, source_target_pairs={{0,4},{1,5},{2,6},{3,7},{4,0},{5,1},{6,2},{7,3},{8,12},{9,13},{10,... | collective-permute-start | bytes 786440 | tf_op jit(solution)/shard_map/ppermute | solution.py:64
  31.0 2.6 %collective-permute-done.7.refs_1_ = bf16[64,2048]{1,0:T(8,128)(2,1)S(1)} collective-permute-done((bf16[64,2048]{1,0:T(8,128)(2,1)S(1)}, bf16[64,2048]{1,0:T(8,128)(2,1)S(1)}, u32[]{:S(2)}, u32[]{:S(2)}) %collective-permute-start.7) | collective-permute-done | bytes 262176 | tf_op jit(solution)/shard_map/ppermute | solution.py:64
  33.7 0.1 absorb_3.1.refs_2_.refs_0_
  33.7 0.1 collective-permute-start.13
  33.9 1.2 %scores_0_0.1.refs_2_ = bf16[64,1536]{1,0:T(8,128)(2,1)S(1)} custom-call(bf16[64,2048]{1,0:T(8,128)(2,1)S(1)} %adopt_0.1.refs_0_.refs_2_, bf16[2048,1536]{1,0:T(8,128)(2,1)S(1)} %transposed_train.1.refs_2_.refs_1_, bf16[64,2048]{1,0:T(8,128)(2,1)S(1)} %adopt_0.1.refs_0_.refs_2_), custom_call_target="tpu_custom_call" | custom-call | flops 2000000000 | tf_op jit(solution)/shard_map/scores_0_0/pallas_call | solution.py:33
  35.1 0.6 %collective-permute-start.10 = (bf16[64,1536]{1,0:T(8,128)(2,1)S(1)}, bf16[64,1536]{1,0:T(8,128)(2,1)S(1)}, u32[]{:S(2)}, u32[]{:S(2)}) collective-permute-start(bf16[64,1536]{1,0:T(8,128)(2,1)S(1)} %scores_0_0.1.refs_2_), channel_id=1, source_target_pairs={{0,1},{1,0},{2,3},{3,2},{4,5},{5,4},{6,7},{7,6},{8,9},{9,8},{10,11... | collective-permute-start | bytes 589832 | tf_op jit(solution)/shard_map/ppermute | solution.py:67
  35.6 0.1 total_2.1.refs_0_.refs_1_
  35.7 1.6 %collective-permute-start.12 = (bf16[64,2048]{1,0:T(8,128)(2,1)S(1)}, bf16[64,2048]{1,0:T(8,128)(2,1)S(1)}, u32[]{:S(2)}, u32[]{:S(2)}) collective-permute-start(bf16[64,2048]{1,0:T(8,128)(2,1)S(1)} %back_5.1.refs_2_), channel_id=1, source_target_pairs={{0,4},{1,5},{2,6},{3,7},{4,0},{5,1},{6,2},{7,3},{8,12},{9,13},{10,... | collective-permute-start | bytes 786440 | tf_op jit(solution)/shard_map/ppermute | solution.py:64
  37.4 1.5 %collective-permute-done.14.refs_1_ = bf16[64,2048]{1,0:T(8,128)(2,1)S(1)} collective-permute-done((bf16[64,2048]{1,0:T(8,128)(2,1)S(1)}, bf16[64,2048]{1,0:T(8,128)(2,1)S(1)}, u32[]{:S(2)}, u32[]{:S(2)}) %collective-permute-start.14) | collective-permute-done | bytes 262176 | tf_op jit(solution)/shard_map/ppermute | solution.py:64
  38.8 1.2 %scores_1_0.1.refs_2_ = bf16[64,1536]{1,0:T(8,128)(2,1)S(1)} custom-call(bf16[64,2048]{1,0:T(8,128)(2,1)S(1)} %adopt_1.1.refs_0_.refs_2_, bf16[2048,1536]{1,0:T(8,128)(2,1)S(1)} %transposed_train.1.refs_2_.refs_1_, bf16[64,2048]{1,0:T(8,128)(2,1)S(1)} %adopt_1.1.refs_0_.refs_2_), custom_call_target="tpu_custom_call" | custom-call | flops 2000000000 | tf_op jit(solution)/shard_map/scores_1_0/pallas_call | solution.py:33
  40.0 0.6 %collective-permute-start.15 = (bf16[64,1536]{1,0:T(8,128)(2,1)S(1)}, bf16[64,1536]{1,0:T(8,128)(2,1)S(1)}, u32[]{:S(2)}, u32[]{:S(2)}) collective-permute-start(bf16[64,1536]{1,0:T(8,128)(2,1)S(1)} %scores_1_0.1.refs_2_), channel_id=1, source_target_pairs={{0,3},{1,2},{2,1},{3,0},{4,7},{5,6},{6,5},{7,4},{8,11},{9,10},{10,... | collective-permute-start | bytes 589832 | tf_op jit(solution)/shard_map/ppermute | solution.py:67
  40.6 0.1 total_last.1
  40.7 1.6 %collective-permute-start.17 = (bf16[64,1024]{1,0:T(8,128)(2,1)S(1)}, bf16[64,1024]{1,0:T(8,128)(2,1)S(1)}, u32[]{:S(2)}, u32[]{:S(2)}) collective-permute-start(bf16[64,1024]{1,0:T(8,128)(2,1)S(1)} %get-tuple-element.16.refs_0_), channel_id=1, source_target_pairs={{0,4},{1,5},{2,6},{3,7},{4,0},{5,1},{6,2},{7,3},{8,12},{9,13},{10,... | collective-permute-start | bytes 393224 | tf_op jit(solution)/shard_map/ppermute | solution.py:64
  42.3 0.5 collective-permute-start.18
  42.8 1.6 %collective-permute-done.12.refs_1_ = bf16[64,2048]{1,0:T(8,128)(2,1)S(1)} collective-permute-done((bf16[64,2048]{1,0:T(8,128)(2,1)S(1)}, bf16[64,2048]{1,0:T(8,128)(2,1)S(1)}, u32[]{:S(2)}, u32[]{:S(2)}) %collective-permute-start.12) | collective-permute-done | bytes 262176 | tf_op jit(solution)/shard_map/ppermute | solution.py:64
  44.5 0.7 %scores_2_0.1.refs_2_ = bf16[64,768]{1,0:T(8,128)(2,1)S(1)} custom-call(bf16[64,2048]{1,0:T(8,128)(2,1)S(1)} %adopt_2.1.refs_0_.refs_2_, bf16[2048,1536]{1,0:T(8,128)(2,1)S(1)} %transposed_train.1.refs_2_.refs_1_, bf16[64,2048]{1,0:T(8,128)(2,1)S(1)} %adopt_2.1.refs_0_.refs_2_), custom_call_target="tpu_custom_call" | custom-call | tf_op jit(solution)/shard_map/scores_2_0/pallas_call | solution.py:33
  45.1 2.0 %collective-permute-start.16 = (bf16[64,768]{1,0:T(8,128)(2,1)S(1)}, bf16[64,768]{1,0:T(8,128)(2,1)S(1)}, u32[]{:S(2)}, u32[]{:S(2)}) collective-permute-start(bf16[64,768]{1,0:T(8,128)(2,1)S(1)} %scores_2_0.1.refs_2_), channel_id=1, source_target_pairs={{0,2},{1,3},{2,0},{3,1},{4,6},{5,7},{6,4},{7,5},{8,10},{9,11},{10,... | collective-permute-start | bytes 294920 | tf_op jit(solution)/shard_map/ppermute | solution.py:67
  47.1 0.7 %scores_2_1.1.refs_1_ = bf16[64,768]{1,0:T(8,128)(2,1)S(1)} custom-call(bf16[64,2048]{1,0:T(8,128)(2,1)S(1)} %adopt_2.1.refs_0_.refs_2_, bf16[2048,1536]{1,0:T(8,128)(2,1)S(1)} %transposed_train.1.refs_2_.refs_1_, bf16[64,768]{1,0:T(8,128)(2,1)S(1)} %scores_2_0.1.refs_2_), custom_call_target="tpu_custom_call" | custom-call | tf_op jit(solution)/shard_map/scores_2_1/pallas_call | solution.py:33
  47.8 0.2 collective-permute-start.19
  48.1 2.0 %collective-permute-done.18.refs_1_ = bf16[64,1024]{1,0:T(8,128)(2,1)S(1)} collective-permute-done((bf16[64,1024]{1,0:T(8,128)(2,1)S(1)}, bf16[64,1024]{1,0:T(8,128)(2,1)S(1)}, u32[]{:S(2)}, u32[]{:S(2)}) %collective-permute-start.18) | collective-permute-done | bytes 131104 | tf_op jit(solution)/shard_map/ppermute | solution.py:64
  50.0 0.6 %last_scores_0.1.refs_3_.refs_4_ = f32[64,1536]{1,0:T(8,128)S(1)} custom-call(bf16[64,1024]{1,0:T(8,128)(2,1)S(1)} %get-tuple-element.15.refs_2_.refs_0_, bf16[64,1024]{1,0:T(8,128)(2,1)S(1)} %collective-permute-done.18.refs_1_, bf16[2048,1536]{1,0:T(8,128)(2,1)S(1)} %transposed_train.1.refs_2_.refs_1_, f32[64,1536]{1,0:T(8,128)S(1)} %gather_1_0.1.refs_3_.refs_0_), custom_call_target="tpu_custom_call" | custom-call | tf_op jit(solution)/shard_map/last_scores_0/pallas_call | solution.py:33
  50.7 0.7 %last_scores_1.1.refs_2_.refs_1_ = f32[64,1536]{1,0:T(8,128)S(1)} custom-call(bf16[64,1024]{1,0:T(8,128)(2,1)S(1)} %get-tuple-element.16.refs_0_, bf16[64,1024]{1,0:T(8,128)(2,1)S(1)} %collective-permute-done.17.refs_1_, bf16[2048,1536]{1,0:T(8,128)(2,1)S(1)} %transposed_train.1.refs_2_.refs_1_, f32[64,1536]{1,0:T(8,128)S(1)} %last_scores_0.1.refs_3_.refs_4_, ...), custom_call_target="tpu_custom_call" | custom-call | tf_op jit(solution)/shard_map/last_scores_1/pallas_call | solution.py:33
  51.4 1.0 %collective-permute-done.19.refs_1_ = bf16[64,768]{1,0:T(8,128)(2,1)S(1)} collective-permute-done((bf16[64,768]{1,0:T(8,128)(2,1)S(1)}, bf16[64,768]{1,0:T(8,128)(2,1)S(1)}, u32[]{:S(2)}, u32[]{:S(2)}) %collective-permute-start.19) | collective-permute-done | bytes 98336 | tf_op jit(solution)/shard_map/ppermute | solution.py:67
  52.5 0.7 %copy.4 = f32[64,1536]{1,0:T(8,128)} copy(f32[64,1536]{1,0:T(8,128)S(1)} %close.1) | data formatting | bytes 786432
  (34 shorter events, 0.5 us)
Async XLA Ops:
  0.0 3.1 %collective-permute-start = (bf16[64,2048]{1,0:T(8,128)(2,1)}, bf16[64,2048]{1,0:T(8,128)(2,1)S(1)}, u32[]{:S(2)}, u32[]{:S(2)}) collective-permute-start(bf16[64,2048]{1,0:T(8,128)(2,1)} %refs_0_.2), channel_id=1, source_target_pairs={{0,1},{1,0},{2,3},{3,2},{4,5},{5,4},{6,7},{7,6},{8,9},{9,8},{10,11... | collective-permute-start | bytes 786440 | tf_op jit(solution)/shard_map/ppermute | solution.py:67
  0.5 9.9 %collective-permute-start.2 = (bf16[64,2048]{1,0:T(8,128)(2,1)}, bf16[64,2048]{1,0:T(8,128)(2,1)S(1)}, u32[]{:S(2)}, u32[]{:S(2)}) collective-permute-start(bf16[64,2048]{1,0:T(8,128)(2,1)} %refs_0_.2), channel_id=1, source_target_pairs={{0,3},{1,2},{2,1},{3,0},{4,7},{5,6},{6,5},{7,4},{8,11},{9,10},{10,... | collective-permute-start | bytes 786440 | tf_op jit(solution)/shard_map/ppermute | solution.py:67
  3.1 14.1 %collective-permute-start.6 = (bf16[64,2048]{1,0:T(8,128)(2,1)}, bf16[64,2048]{1,0:T(8,128)(2,1)S(1)}, u32[]{:S(2)}, u32[]{:S(2)}) collective-permute-start(bf16[64,2048]{1,0:T(8,128)(2,1)} %refs_0_.2), channel_id=1, source_target_pairs={{0,2},{1,3},{2,0},{3,1},{4,6},{5,7},{6,4},{7,5},{8,10},{9,11},{10,... | collective-permute-start | bytes 786440 | tf_op jit(solution)/shard_map/ppermute | solution.py:67
  5.6 8.5 %collective-permute-start.1 = (bf16[64,1024]{1,0:T(8,128)(2,1)S(1)}, bf16[64,1024]{1,0:T(8,128)(2,1)S(1)}, u32[]{:S(2)}, u32[]{:S(2)}) collective-permute-start(bf16[64,1024]{1,0:T(8,128)(2,1)S(1)} %get-tuple-element.11.refs_2_.refs_0_), channel_id=1, source_target_pairs={{0,4},{1,5},{2,6},{3,7},{4,0},{5,1},{6,2},{7,3},{8,12},{9,13},{10,... | collective-permute-start | bytes 393224 | tf_op jit(solution)/shard_map/ppermute | solution.py:64
  10.3 5.2 %collective-permute-start.3 = (bf16[64,1024]{1,0:T(8,128)(2,1)S(1)}, bf16[64,1024]{1,0:T(8,128)(2,1)S(1)}, u32[]{:S(2)}, u32[]{:S(2)}) collective-permute-start(bf16[64,1024]{1,0:T(8,128)(2,1)S(1)} %get-tuple-element.14.refs_3_.refs_1_), channel_id=1, source_target_pairs={{0,4},{1,5},{2,6},{3,7},{4,0},{5,1},{6,2},{7,3},{8,12},{9,13},{10,... | collective-permute-start | bytes 393224 | tf_op jit(solution)/shard_map/ppermute | solution.py:64
  12.0 3.6 %copy-start = (bf16[64,2048]{1,0:T(8,128)(2,1)S(1)}, bf16[64,2048]{1,0:T(8,128)(2,1)}, u32[]{:S(2)}) copy-start(bf16[64,2048]{1,0:T(8,128)(2,1)} %refs_0_.2) | copy-start | bytes 786436
  12.0 9.9 %collective-permute-start.5 = (bf16[64,2048]{1,0:T(8,128)(2,1)S(1)}, bf16[64,2048]{1,0:T(8,128)(2,1)S(1)}, u32[]{:S(2)}, u32[]{:S(2)}) collective-permute-start(bf16[64,2048]{1,0:T(8,128)(2,1)S(1)} %pass_1.1.refs_2_), channel_id=1, source_target_pairs={{0,4},{1,5},{2,6},{3,7},{4,0},{5,1},{6,2},{7,3},{8,12},{9,13},{10,... | collective-permute-start | bytes 786440 | tf_op jit(solution)/shard_map/ppermute | solution.py:64
  15.5 8.3 %collective-permute-start.4 = (bf16[64,2048]{1,0:T(8,128)(2,1)S(1)}, bf16[64,2048]{1,0:T(8,128)(2,1)S(1)}, u32[]{:S(2)}, u32[]{:S(2)}) collective-permute-start(bf16[64,2048]{1,0:T(8,128)(2,1)S(1)} %absorb_0b.1.refs_3_.refs_0_), channel_id=1, source_target_pairs={{0,1},{1,0},{2,3},{3,2},{4,8},{5,9},{6,10},{7,11},{8,4},{9,5},{10,... | collective-permute-start | bytes 786440 | tf_op jit(solution)/shard_map/ppermute | solution.py:64
  17.2 4.9 %slice-start = ((s8[6291456]{0:T(1024)(128)(4,1)}), s8[4194304]{0:T(1024)(128)(4,1)S(1)}, s32[]{:S(2)}) async-start(s8[6291456]{0:T(1024)(128)(4,1)} %bitcast), calls=%async_computation | async-start | bytes 8388608
  18.7 3.3 %slice-start.1 = ((s8[6291456]{0:T(1024)(128)(4,1)}), s8[2097152]{0:T(1024)(128)(4,1)S(1)}, s32[]{:S(2)}) async-start(s8[6291456]{0:T(1024)(128)(4,1)} %bitcast), calls=%async_computation.1 | async-start | bytes 4194304
  18.8 9.2 %collective-permute-start.9 = (bf16[64,2048]{1,0:T(8,128)(2,1)S(1)}, bf16[64,2048]{1,0:T(8,128)(2,1)S(1)}, u32[]{:S(2)}, u32[]{:S(2)}) collective-permute-start(bf16[64,2048]{1,0:T(8,128)(2,1)S(1)} %pass_2.1.refs_2_), channel_id=1, source_target_pairs={{0,4},{1,5},{2,6},{3,7},{4,0},{5,1},{6,2},{7,3},{8,12},{9,13},{10,... | collective-permute-start | bytes 786440 | tf_op jit(solution)/shard_map/ppermute | solution.py:64
  22.0 6.2 %collective-permute-start.8 = (bf16[64,2048]{1,0:T(8,128)(2,1)S(1)}, bf16[64,2048]{1,0:T(8,128)(2,1)S(1)}, u32[]{:S(2)}, u32[]{:S(2)}) collective-permute-start(bf16[64,2048]{1,0:T(8,128)(2,1)S(1)} %absorb_1.1.refs_1_.refs_0_), channel_id=1, source_target_pairs={{0,1},{1,0},{2,3},{3,2},{4,8},{5,9},{6,10},{7,11},{8,4},{9,5},{10,... | collective-permute-start | bytes 786440 | tf_op jit(solution)/shard_map/ppermute | solution.py:64
  23.9 9.8 %collective-permute-start.7 = (bf16[64,2048]{1,0:T(8,128)(2,1)S(1)}, bf16[64,2048]{1,0:T(8,128)(2,1)S(1)}, u32[]{:S(2)}, u32[]{:S(2)}) collective-permute-start(bf16[64,2048]{1,0:T(8,128)(2,1)S(1)} %merge_3.1.refs_2_), channel_id=1, source_target_pairs={{0,4},{1,5},{2,6},{3,7},{4,0},{5,1},{6,2},{7,3},{8,12},{9,13},{10,... | collective-permute-start | bytes 786440 | tf_op jit(solution)/shard_map/ppermute | solution.py:64
  28.1 7.5 %collective-permute-start.11 = (bf16[64,2048]{1,0:T(8,128)(2,1)S(1)}, bf16[64,2048]{1,0:T(8,128)(2,1)S(1)}, u32[]{:S(2)}, u32[]{:S(2)}) collective-permute-start(bf16[64,2048]{1,0:T(8,128)(2,1)S(1)} %absorb_2.1.refs_2_.refs_0_), channel_id=1, source_target_pairs={{0,1},{1,0},{2,3},{3,2},{4,8},{5,9},{6,10},{7,11},{8,4},{9,5},{10,... | collective-permute-start | bytes 786440 | tf_op jit(solution)/shard_map/ppermute | solution.py:64
  28.3 10.5 %collective-permute-start.14 = (bf16[64,2048]{1,0:T(8,128)(2,1)S(1)}, bf16[64,2048]{1,0:T(8,128)(2,1)S(1)}, u32[]{:S(2)}, u32[]{:S(2)}) collective-permute-start(bf16[64,2048]{1,0:T(8,128)(2,1)S(1)} %back_4.1.refs_2_), channel_id=1, source_target_pairs={{0,4},{1,5},{2,6},{3,7},{4,0},{5,1},{6,2},{7,3},{8,12},{9,13},{10,... | collective-permute-start | bytes 786440 | tf_op jit(solution)/shard_map/ppermute | solution.py:64
  33.7 6.9 %collective-permute-start.13 = (bf16[64,2048]{1,0:T(8,128)(2,1)S(1)}, bf16[64,2048]{1,0:T(8,128)(2,1)S(1)}, u32[]{:S(2)}, u32[]{:S(2)}) collective-permute-start(bf16[64,2048]{1,0:T(8,128)(2,1)S(1)} %absorb_3.1.refs_2_.refs_0_), channel_id=1, source_target_pairs={{0,1},{1,0},{2,3},{3,2},{4,8},{5,9},{6,10},{7,11},{8,4},{9,5},{10,... | collective-permute-start | bytes 786440 | tf_op jit(solution)/shard_map/ppermute | solution.py:64
  35.1 12.7 %collective-permute-start.10 = (bf16[64,1536]{1,0:T(8,128)(2,1)S(1)}, bf16[64,1536]{1,0:T(8,128)(2,1)S(1)}, u32[]{:S(2)}, u32[]{:S(2)}) collective-permute-start(bf16[64,1536]{1,0:T(8,128)(2,1)S(1)} %scores_0_0.1.refs_2_), channel_id=1, source_target_pairs={{0,1},{1,0},{2,3},{3,2},{4,5},{5,4},{6,7},{7,6},{8,9},{9,8},{10,11... | collective-permute-start | bytes 589832 | tf_op jit(solution)/shard_map/ppermute | solution.py:67
  35.7 8.7 %collective-permute-start.12 = (bf16[64,2048]{1,0:T(8,128)(2,1)S(1)}, bf16[64,2048]{1,0:T(8,128)(2,1)S(1)}, u32[]{:S(2)}, u32[]{:S(2)}) collective-permute-start(bf16[64,2048]{1,0:T(8,128)(2,1)S(1)} %back_5.1.refs_2_), channel_id=1, source_target_pairs={{0,4},{1,5},{2,6},{3,7},{4,0},{5,1},{6,2},{7,3},{8,12},{9,13},{10,... | collective-permute-start | bytes 786440 | tf_op jit(solution)/shard_map/ppermute | solution.py:64
  40.0 8.0 %collective-permute-start.15 = (bf16[64,1536]{1,0:T(8,128)(2,1)S(1)}, bf16[64,1536]{1,0:T(8,128)(2,1)S(1)}, u32[]{:S(2)}, u32[]{:S(2)}) collective-permute-start(bf16[64,1536]{1,0:T(8,128)(2,1)S(1)} %scores_1_0.1.refs_2_), channel_id=1, source_target_pairs={{0,3},{1,2},{2,1},{3,0},{4,7},{5,6},{6,5},{7,4},{8,11},{9,10},{10,... | collective-permute-start | bytes 589832 | tf_op jit(solution)/shard_map/ppermute | solution.py:67
  40.7 10.0 %collective-permute-start.17 = (bf16[64,1024]{1,0:T(8,128)(2,1)S(1)}, bf16[64,1024]{1,0:T(8,128)(2,1)S(1)}, u32[]{:S(2)}, u32[]{:S(2)}) collective-permute-start(bf16[64,1024]{1,0:T(8,128)(2,1)S(1)} %get-tuple-element.16.refs_0_), channel_id=1, source_target_pairs={{0,4},{1,5},{2,6},{3,7},{4,0},{5,1},{6,2},{7,3},{8,12},{9,13},{10,... | collective-permute-start | bytes 393224 | tf_op jit(solution)/shard_map/ppermute | solution.py:64
  42.3 7.7 %collective-permute-start.18 = (bf16[64,1024]{1,0:T(8,128)(2,1)S(1)}, bf16[64,1024]{1,0:T(8,128)(2,1)S(1)}, u32[]{:S(2)}, u32[]{:S(2)}) collective-permute-start(bf16[64,1024]{1,0:T(8,128)(2,1)S(1)} %get-tuple-element.15.refs_2_.refs_0_), channel_id=1, source_target_pairs={{0,4},{1,5},{2,6},{3,7},{4,0},{5,1},{6,2},{7,3},{8,12},{9,13},{10,... | collective-permute-start | bytes 393224 | tf_op jit(solution)/shard_map/ppermute | solution.py:64
  45.1 6.2 %collective-permute-start.16 = (bf16[64,768]{1,0:T(8,128)(2,1)S(1)}, bf16[64,768]{1,0:T(8,128)(2,1)S(1)}, u32[]{:S(2)}, u32[]{:S(2)}) collective-permute-start(bf16[64,768]{1,0:T(8,128)(2,1)S(1)} %scores_2_0.1.refs_2_), channel_id=1, source_target_pairs={{0,2},{1,3},{2,0},{3,1},{4,6},{5,7},{6,4},{7,5},{8,10},{9,11},{10,... | collective-permute-start | bytes 294920 | tf_op jit(solution)/shard_map/ppermute | solution.py:67
  47.8 4.7 %collective-permute-start.19 = (bf16[64,768]{1,0:T(8,128)(2,1)S(1)}, bf16[64,768]{1,0:T(8,128)(2,1)S(1)}, u32[]{:S(2)}, u32[]{:S(2)}) collective-permute-start(bf16[64,768]{1,0:T(8,128)(2,1)S(1)} %scores_2_1.1.refs_1_), channel_id=1, source_target_pairs={{0,2},{1,3},{2,0},{3,1},{4,6},{5,7},{6,4},{7,5},{8,10},{9,11},{10,... | collective-permute-start | bytes 294920 | tf_op jit(solution)/shard_map/ppermute | solution.py:67

commit v5 on v4

--- a/solution.py
+++ b/solution.py
@@ -158,26 +158,22 @@
 
             return call("transposed_train", kernel, [((x.shape[1], t), BF16)], x, work=WORK)[0]
 
-        def scores(name, chunk, left, cols):
+        def scores(name, left, cols):
             def kernel(left_ref, train_ref, out_ref):
                 out_ref[...] = dot(left_ref[...], train_ref[:, cols]).astype(BF16)
 
-            return call(name, kernel, [((left.shape[0], cols.stop - cols.start), BF16)], left, trained[0], work=WORK if chunk < last - 1 else 0)[0]
-
-        def last_scores(side, kept, given, *before):
+            return call(name, kernel, [((left.shape[0], cols.stop - cols.start), BF16)], left, trained[0])[0]
+
+        def last_scores(kept, given):
             step = t // 3
 
-            def kernel(kept_ref, given_ref, train_ref, *refs):
-                *before_refs, out_ref = refs
+            def kernel(kept_ref, given_ref, train_ref, out_ref):
                 left = jnp.where(at(0), given_ref[...], kept_ref[...])
                 for lo in range(0, t, step):
                     cols = slice(lo, lo + step)
-                    value = dot(left, train_ref[halves[side], cols])
-                    for ref in before_refs:
-                        value = value + ref[:, cols]
-                    out_ref[:, cols] = value
-
-            return call(f"last_scores_{side}", kernel, [((m, t), F32)], kept, given, trained[0], *before)[0]
+                    out_ref[:, cols] = dot(left, train_ref[:, cols])
+
+            return call("last_scores", kernel, [((m, t), F32)], kept, given, trained[0])[0]
 
         owners = [1, *[d ^ 1 for d in range(2, n_proj)], 0]
         ranges = {d: [(0, m)] for d in owners}
@@ -210,16 +206,6 @@
             c, back = step - h, outward(h, step)
             if h == 0 and c == 0:
                 moving[h, step] = [along(x, hop_swaps[h]) for x in here[c]]
-                return
-            if h == 0 and back == last:
-                if hops > 1:
-
-                    def kernel(x_ref, *out_refs):
-                        for side, out_ref in zip(halves, out_refs):
-                            out_ref[...] = x_ref[:, side]
-
-                    total[back] = call("halves", kernel, [((m, half_n), BF16)] * 2, total[back])
-                moving[h, step] = [along(x, hop_swaps[h]) for x in total[back]]
                 return
             if valid(c) and valid(back):
                 value = elementwise(f"merge_{step}", lambda a, b: jnp.where(at(h), a, b), here[c], total[back])
@@ -251,15 +237,7 @@
                 total[back] = update(f"adopt_{back}", lambda a, b: jnp.where(at(h), b, a), total[back], moving[h, step])
 
         def end_middle(c, step):
-            if c == last and hops == 1:
-
-                def kernel(a_ref, b_ref, *out_refs):
-                    for side, out_ref in zip(halves, out_refs):
-                        out_ref[...] = plus(a_ref[:, side], b_ref[:, side])
-
-                total[c] = call("total_last", kernel, [((m, half_n), BF16)] * 2, here[c], moving["middle", step])
-            else:
-                total[c] = update(f"total_{c}", plus, here[c], moving["middle", step])
+            total[c] = update(f"total_{c}", plus, here[c], moving["middle", step])
 
         def gather(c):
             for i, (cols, got) in enumerate(zip(pieces(c), parts[c])):
@@ -274,17 +252,15 @@
                     out_ref[:, cols] += in_refs[-1][...].astype(F32)
 
                 before = [] if first else [parts["sum"]]
-                parts["sum"] = call(f"gather_{c}_{i}", kernel, [((m, t), F32)], *before, got, work=WORK if c == last - 1 and i == 0 else 0)[0]
+                parts["sum"] = call(f"gather_{c}_{i}", kernel, [((m, t), F32)], *before, got)[0]
 
         def pieces(c):
-            if c == last - 1 and t % 256 == 0:
-                return [slice(0, t // 2), slice(t // 2, t)]
             return [slice(0, t)]
 
         def finish(c):
             parts[c] = []
             for i, cols in enumerate(pieces(c)):
-                parts[c].append(across(scores(f"scores_{c}_{i}", c, total[c], cols), chunks[c][0]))
+                parts[c].append(across(scores(f"scores_{c}_{i}", total[c], cols), chunks[c][0]))
 
         for i in range(min(3, n_proj - 1)):
             fetch(i, targets)
@@ -323,10 +299,7 @@
             start_hop(0, step + 1)
         for c in range(last - 1):
             gather(c)
-        value = None
-        for side in (0, 1):
-            before = [] if value is None else [value]
-            value = last_scores(side, total[last][side], moving[0, last + back_at][side], *before)
+        value = last_scores(total[last], moving[0, last + back_at])
         gather(last - 1)
 
         def close(sum_ref, value_ref, out_ref):

time: 53.4 us -> 53.1 us (level)
  starting transfers between devices: 23 us -> 22.4 us
  waiting for transfers between devices: 11.7 us -> 12.3 us
    ppermute x13 -> x12, waiting for transfers between devices: 10.6 us -> 11.4 us  [along(): return lax.ppermute(x, ('rows', 'proj'), swaps)]
    ppermute x13 -> x12, starting transfers between devices: 16.7 us -> 16.2 us  [along(): return lax.ppermute(x, ('rows', 'proj'), swaps)]
    pallas_call x34 -> x32, Pallas kernels: 17.4 us -> 17.2 us  [__call__(): pl.pallas_call(ordered, name=name, out_shape=tuple((pltpu.VMEM(shape, dty...]
    ppermute x7 -> x6, starting transfers between devices: 6.35 us -> 6.18 us  [across(): return lax.ppermute(x, 'proj', [(i, i ^ d) for i in range(n_proj)])]
  transfers between devices with their start and end apart: 20 -> 18, of which waited for: 7 -> 7; matrix products, arithmetic and copies ran while one was open for 0% -> 0% of each run, Pallas kernels for 33% -> 32%
where the time goes in v5:
time: 53.1 us; the launch traced here: 53 us
  starting transfers between devices  22.4 us (42%)
  Pallas kernels  17.2 us (32%)
  waiting for transfers between devices  12.3 us (23%)
  local copies, waits for them, and re-layouts  0.77 us (1%)
    pallas_call x32, Pallas kernels, __call__(): pl.pallas_call(ordered, name=name, out_shape=tuple((pltpu.VMEM(shape, dty...  17.2 us
    ppermute x12, starting transfers between devices, along(): return lax.ppermute(x, ('rows', 'proj'), swaps)  16.2 us
    ppermute x12, waiting for transfers between devices, along(): return lax.ppermute(x, ('rows', 'proj'), swaps)  11.4 us
    ppermute x6, starting transfers between devices, across(): return lax.ppermute(x, 'proj', [(i, i ^ d) for i in range(n_proj)])  6.18 us
  transfers between devices with their start and end apart: 18, of which 7 were waited for; matrix products, arithmetic and copies ran while one was open for 0% of the time, Pallas kernels for 32%

profile of v5, /device:TPU:0, one launch (start us, length us, event | category | flops | bytes accessed | tf_op | source)
XLA Modules:
  0.0 53.0 jit_solution(2956450656906082376)
XLA Ops:
  0.0 0.5 collective-permute-start
  0.5 2.6 %collective-permute-start.2 = (bf16[64,2048]{1,0:T(8,128)(2,1)}, bf16[64,2048]{1,0:T(8,128)(2,1)S(1)}, u32[]{:S(2)}, u32[]{:S(2)}) collective-permute-start(bf16[64,2048]{1,0:T(8,128)(2,1)} %refs_0_.2), channel_id=1, source_target_pairs={{0,3},{1,2},{2,1},{3,0},{4,7},{5,6},{6,5},{7,4},{8,11},{9,10},{10,... | collective-permute-start | bytes 786440 | tf_op jit(solution)/shard_map/ppermute | solution.py:67
  3.1 0.0 collective-permute-done.refs_0_
  3.1 2.5 %read_condition_0.1 = (bf16[64,1024]{1,0:T(8,128)(2,1)S(1)}, bf16[2048,1024]{1,0:T(8,128)(2,1)S(1)}) custom-call(bf16[64,2048]{1,0:T(8,128)(2,1)S(1)} %collective-permute-done.refs_0_, bf16[2048,2048]{1,0:T(8,128)(2,1)} %refs_1_.3), custom_call_target="tpu_custom_call" | custom-call | tf_op jit(solution)/shard_map/read_condition_0/pallas_call | solution.py:33
  5.6 2.2 %collective-permute-start.1 = (bf16[64,1024]{1,0:T(8,128)(2,1)S(1)}, bf16[64,1024]{1,0:T(8,128)(2,1)S(1)}, u32[]{:S(2)}, u32[]{:S(2)}) collective-permute-start(bf16[64,1024]{1,0:T(8,128)(2,1)S(1)} %get-tuple-element.9.refs_2_.refs_0_), channel_id=1, source_target_pairs={{0,4},{1,5},{2,6},{3,7},{4,0},{5,1},{6,2},{7,3},{8,12},{9,13},{10,... | collective-permute-start | bytes 393224 | tf_op jit(solution)/shard_map/ppermute | solution.py:64
  7.8 2.5 %read_condition_1.1 = (bf16[64,1024]{1,0:T(8,128)(2,1)S(1)}, bf16[2048,1024]{1,0:T(8,128)(2,1)S(1)}) custom-call(bf16[64,2048]{1,0:T(8,128)(2,1)S(1)} %collective-permute-done.refs_0_, bf16[2048,2048]{1,0:T(8,128)(2,1)} %refs_1_.3, bf16[64,1024]{1,0:T(8,128)(2,1)S(1)} %get-tuple-element.9.refs_2_.refs_0_), custom_call_target="tpu_custom_call" | custom-call | tf_op jit(solution)/shard_map/read_condition_1/pallas_call | solution.py:33
  10.3 0.1 collective-permute-start.3
  10.4 1.6 %condition_1.1.refs_0_.refs_1_ = bf16[64,2048]{1,0:T(8,128)(2,1)S(1)} custom-call(bf16[64,2048]{1,0:T(8,128)(2,1)S(1)} %collective-permute-done.2.refs_0_, bf16[2048,1024]{1,0:T(8,128)(2,1)S(1)} %get-tuple-element.10.refs_1_, bf16[2048,1024]{1,0:T(8,128)(2,1)S(1)} %get-tuple-element.11.refs_2_, bf16[64,1024]{1,0:T(8,128)(2,1)S(1)} %get-tuple-element.12.refs_3_.refs_1_), custom_call_target="tpu_custom_call" | custom-call | flops 2000000000 | tf_op jit(solution)/shard_map/condition_1/pallas_call | solution.py:33
  12.0 0.0 copy-start
  12.0 2.1 %collective-permute-start.5 = (bf16[64,2048]{1,0:T(8,128)(2,1)S(1)}, bf16[64,2048]{1,0:T(8,128)(2,1)S(1)}, u32[]{:S(2)}, u32[]{:S(2)}) collective-permute-start(bf16[64,2048]{1,0:T(8,128)(2,1)S(1)} %pass_1.1.refs_2_), channel_id=1, source_target_pairs={{0,4},{1,5},{2,6},{3,7},{4,0},{5,1},{6,2},{7,3},{8,12},{9,13},{10,... | collective-permute-start | bytes 786440 | tf_op jit(solution)/shard_map/ppermute | solution.py:64
  14.0 0.0 collective-permute-done.1.refs_1_
  14.1 1.3 %collective-permute-done.3.refs_2_ = bf16[64,1024]{1,0:T(8,128)(2,1)S(1)} collective-permute-done((bf16[64,1024]{1,0:T(8,128)(2,1)S(1)}, bf16[64,1024]{1,0:T(8,128)(2,1)S(1)}, u32[]{:S(2)}, u32[]{:S(2)}) %collective-permute-start.3) | collective-permute-done | bytes 131104 | tf_op jit(solution)/shard_map/ppermute | solution.py:64
  15.4 0.1 absorb_0b.1.refs_3_.refs_0_
  15.5 0.1 collective-permute-start.4
  15.6 1.6 %condition_3.1.refs_3_.refs_0_ = bf16[64,2048]{1,0:T(8,128)(2,1)S(1)} custom-call(bf16[64,2048]{1,0:T(8,128)(2,1)S(1)} %copy-done, bf16[2048,1024]{1,0:T(8,128)(2,1)S(1)} %get-tuple-element.10.refs_1_, bf16[2048,1024]{1,0:T(8,128)(2,1)S(1)} %get-tuple-element.11.refs_2_, bf16[64,2048]{1,0:T(8,128)(2,1)S(1)} %absorb_0b.1.refs_3_.refs_0_), custom_call_target="tpu_custom_call" | custom-call | flops 2000000000 | tf_op jit(solution)/shard_map/condition_3/pallas_call | solution.py:33
  17.2 0.0 slice-start
  17.2 1.6 %condition_2.1.refs_0_.refs_1_ = bf16[64,2048]{1,0:T(8,128)(2,1)S(1)} custom-call(bf16[64,2048]{1,0:T(8,128)(2,1)S(1)} %collective-permute-done.6.refs_0_, bf16[2048,1024]{1,0:T(8,128)(2,1)S(1)} %get-tuple-element.10.refs_1_, bf16[2048,1024]{1,0:T(8,128)(2,1)S(1)} %get-tuple-element.11.refs_2_, bf16[64,2048]{1,0:T(8,128)(2,1)S(1)} %condition_3.1.refs_3_.refs_0_), custom_call_target="tpu_custom_call" | custom-call | flops 2000000000 | tf_op jit(solution)/shard_map/condition_2/pallas_call | solution.py:33
  18.7 0.0 slice-start.1
  18.8 3.1 %collective-permute-start.9 = (bf16[64,2048]{1,0:T(8,128)(2,1)S(1)}, bf16[64,2048]{1,0:T(8,128)(2,1)S(1)}, u32[]{:S(2)}, u32[]{:S(2)}) collective-permute-start(bf16[64,2048]{1,0:T(8,128)(2,1)S(1)} %pass_2.1.refs_2_), channel_id=1, source_target_pairs={{0,4},{1,5},{2,6},{3,7},{4,0},{5,1},{6,2},{7,3},{8,12},{9,13},{10,... | collective-permute-start | bytes 786440 | tf_op jit(solution)/shard_map/ppermute | solution.py:64
  21.9 0.1 absorb_1.1.refs_1_.refs_0_
  22.0 0.1 collective-permute-start.8
  22.1 1.7 %transposed_train.1.refs_2_.refs_1_ = bf16[2048,1536]{1,0:T(8,128)(2,1)S(1)} custom-call(bf16[1536,2048]{1,0:T(8,128)(2,1)S(1)} %bitcast.1, bf16[64,2048]{1,0:T(8,128)(2,1)S(1)} %absorb_1.1.refs_1_.refs_0_), custom_call_target="tpu_custom_call" | custom-call | flops 2000000000 | tf_op jit(solution)/shard_map/transposed_train/pallas_call | solution.py:33
  23.8 0.1 total_0.1.refs_1_.refs_2_.refs_0_
  23.9 2.6 %collective-permute-start.7 = (bf16[64,2048]{1,0:T(8,128)(2,1)S(1)}, bf16[64,2048]{1,0:T(8,128)(2,1)S(1)}, u32[]{:S(2)}, u32[]{:S(2)}) collective-permute-start(bf16[64,2048]{1,0:T(8,128)(2,1)S(1)} %merge_3.1.refs_2_), channel_id=1, source_target_pairs={{0,4},{1,5},{2,6},{3,7},{4,0},{5,1},{6,2},{7,3},{8,12},{9,13},{10,... | collective-permute-start | bytes 786440 | tf_op jit(solution)/shard_map/ppermute | solution.py:64
  26.4 1.6 %collective-permute-done.9.refs_1_ = bf16[64,2048]{1,0:T(8,128)(2,1)S(1)} collective-permute-done((bf16[64,2048]{1,0:T(8,128)(2,1)S(1)}, bf16[64,2048]{1,0:T(8,128)(2,1)S(1)}, u32[]{:S(2)}, u32[]{:S(2)}) %collective-permute-start.9) | collective-permute-done | bytes 262176 | tf_op jit(solution)/shard_map/ppermute | solution.py:64
  28.0 0.1 absorb_2.1.refs_2_.refs_0_
  28.1 0.1 collective-permute-start.11
  28.2 0.1 total_1.1.refs_0_.refs_1_
  28.3 2.7 %collective-permute-start.14 = (bf16[64,2048]{1,0:T(8,128)(2,1)S(1)}, bf16[64,2048]{1,0:T(8,128)(2,1)S(1)}, u32[]{:S(2)}, u32[]{:S(2)}) collective-permute-start(bf16[64,2048]{1,0:T(8,128)(2,1)S(1)} %back_4.1.refs_2_), channel_id=1, source_target_pairs={{0,4},{1,5},{2,6},{3,7},{4,0},{5,1},{6,2},{7,3},{8,12},{9,13},{10,... | collective-permute-start | bytes 786440 | tf_op jit(solution)/shard_map/ppermute | solution.py:64
  31.0 2.6 %collective-permute-done.7.refs_1_ = bf16[64,2048]{1,0:T(8,128)(2,1)S(1)} collective-permute-done((bf16[64,2048]{1,0:T(8,128)(2,1)S(1)}, bf16[64,2048]{1,0:T(8,128)(2,1)S(1)}, u32[]{:S(2)}, u32[]{:S(2)}) %collective-permute-start.7) | collective-permute-done | bytes 262176 | tf_op jit(solution)/shard_map/ppermute | solution.py:64
  33.7 0.1 absorb_3.1.refs_2_.refs_0_
  33.7 0.1 collective-permute-start.13
  33.9 1.2 %scores_0_0.1.refs_2_ = bf16[64,1536]{1,0:T(8,128)(2,1)S(1)} custom-call(bf16[64,2048]{1,0:T(8,128)(2,1)S(1)} %adopt_0.1.refs_0_.refs_2_, bf16[2048,1536]{1,0:T(8,128)(2,1)S(1)} %transposed_train.1.refs_2_.refs_1_, bf16[64,2048]{1,0:T(8,128)(2,1)S(1)} %adopt_0.1.refs_0_.refs_2_), custom_call_target="tpu_custom_call" | custom-call | tf_op jit(solution)/shard_map/scores_0_0/pallas_call | solution.py:33
  35.1 0.6 %collective-permute-start.10 = (bf16[64,1536]{1,0:T(8,128)(2,1)S(1)}, bf16[64,1536]{1,0:T(8,128)(2,1)S(1)}, u32[]{:S(2)}, u32[]{:S(2)}) collective-permute-start(bf16[64,1536]{1,0:T(8,128)(2,1)S(1)} %scores_0_0.1.refs_2_), channel_id=1, source_target_pairs={{0,1},{1,0},{2,3},{3,2},{4,5},{5,4},{6,7},{7,6},{8,9},{9,8},{10,11... | collective-permute-start | bytes 589832 | tf_op jit(solution)/shard_map/ppermute | solution.py:67
  35.6 0.1 total_2.1.refs_0_.refs_1_
  35.7 1.6 %collective-permute-start.12 = (bf16[64,2048]{1,0:T(8,128)(2,1)S(1)}, bf16[64,2048]{1,0:T(8,128)(2,1)S(1)}, u32[]{:S(2)}, u32[]{:S(2)}) collective-permute-start(bf16[64,2048]{1,0:T(8,128)(2,1)S(1)} %back_5.1.refs_2_), channel_id=1, source_target_pairs={{0,4},{1,5},{2,6},{3,7},{4,0},{5,1},{6,2},{7,3},{8,12},{9,13},{10,... | collective-permute-start | bytes 786440 | tf_op jit(solution)/shard_map/ppermute | solution.py:64
  37.4 1.5 %collective-permute-done.14.refs_1_ = bf16[64,2048]{1,0:T(8,128)(2,1)S(1)} collective-permute-done((bf16[64,2048]{1,0:T(8,128)(2,1)S(1)}, bf16[64,2048]{1,0:T(8,128)(2,1)S(1)}, u32[]{:S(2)}, u32[]{:S(2)}) %collective-permute-start.14) | collective-permute-done | bytes 262176 | tf_op jit(solution)/shard_map/ppermute | solution.py:64
  38.8 1.2 %scores_1_0.1.refs_2_ = bf16[64,1536]{1,0:T(8,128)(2,1)S(1)} custom-call(bf16[64,2048]{1,0:T(8,128)(2,1)S(1)} %adopt_1.1.refs_0_.refs_2_, bf16[2048,1536]{1,0:T(8,128)(2,1)S(1)} %transposed_train.1.refs_2_.refs_1_, bf16[64,2048]{1,0:T(8,128)(2,1)S(1)} %adopt_1.1.refs_0_.refs_2_), custom_call_target="tpu_custom_call" | custom-call | tf_op jit(solution)/shard_map/scores_1_0/pallas_call | solution.py:33
  40.0 0.6 %collective-permute-start.15 = (bf16[64,1536]{1,0:T(8,128)(2,1)S(1)}, bf16[64,1536]{1,0:T(8,128)(2,1)S(1)}, u32[]{:S(2)}, u32[]{:S(2)}) collective-permute-start(bf16[64,1536]{1,0:T(8,128)(2,1)S(1)} %scores_1_0.1.refs_2_), channel_id=1, source_target_pairs={{0,3},{1,2},{2,1},{3,0},{4,7},{5,6},{6,5},{7,4},{8,11},{9,10},{10,... | collective-permute-start | bytes 589832 | tf_op jit(solution)/shard_map/ppermute | solution.py:67
  40.6 0.1 total_3.1.refs_0_.refs_1_
  40.7 1.6 %collective-permute-start.17 = (bf16[64,2048]{1,0:T(8,128)(2,1)S(1)}, bf16[64,2048]{1,0:T(8,128)(2,1)S(1)}, u32[]{:S(2)}, u32[]{:S(2)}) collective-permute-start(bf16[64,2048]{1,0:T(8,128)(2,1)S(1)} %back_6.1.refs_2_), channel_id=1, source_target_pairs={{0,4},{1,5},{2,6},{3,7},{4,0},{5,1},{6,2},{7,3},{8,12},{9,13},{10,... | collective-permute-start | bytes 786440 | tf_op jit(solution)/shard_map/ppermute | solution.py:64
  42.4 2.0 %collective-permute-done.12.refs_1_ = bf16[64,2048]{1,0:T(8,128)(2,1)S(1)} collective-permute-done((bf16[64,2048]{1,0:T(8,128)(2,1)S(1)}, bf16[64,2048]{1,0:T(8,128)(2,1)S(1)}, u32[]{:S(2)}, u32[]{:S(2)}) %collective-permute-start.12) | collective-permute-done | bytes 262176 | tf_op jit(solution)/shard_map/ppermute | solution.py:64
  44.4 1.2 %scores_2_0.1.refs_1_ = bf16[64,1536]{1,0:T(8,128)(2,1)S(1)} custom-call(bf16[64,2048]{1,0:T(8,128)(2,1)S(1)} %adopt_2.1.refs_0_.refs_2_, bf16[2048,1536]{1,0:T(8,128)(2,1)S(1)} %transposed_train.1.refs_2_.refs_1_, bf16[64,2048]{1,0:T(8,128)(2,1)S(1)} %adopt_2.1.refs_0_.refs_2_), custom_call_target="tpu_custom_call" | custom-call | tf_op jit(solution)/shard_map/scores_2_0/pallas_call | solution.py:33
  45.6 2.0 %collective-permute-start.16 = (bf16[64,1536]{1,0:T(8,128)(2,1)S(1)}, bf16[64,1536]{1,0:T(8,128)(2,1)S(1)}, u32[]{:S(2)}, u32[]{:S(2)}) collective-permute-start(bf16[64,1536]{1,0:T(8,128)(2,1)S(1)} %scores_2_0.1.refs_1_), channel_id=1, source_target_pairs={{0,2},{1,3},{2,0},{3,1},{4,6},{5,7},{6,4},{7,5},{8,10},{9,11},{10,... | collective-permute-start | bytes 589832 | tf_op jit(solution)/shard_map/ppermute | solution.py:67
  47.7 2.3 %collective-permute-done.17.refs_1_ = bf16[64,2048]{1,0:T(8,128)(2,1)S(1)} collective-permute-done((bf16[64,2048]{1,0:T(8,128)(2,1)S(1)}, bf16[64,2048]{1,0:T(8,128)(2,1)S(1)}, u32[]{:S(2)}, u32[]{:S(2)}) %collective-permute-start.17) | collective-permute-done | bytes 262176 | tf_op jit(solution)/shard_map/ppermute | solution.py:64
  50.0 1.2 %last_scores.1.refs_2_.refs_1_ = f32[64,1536]{1,0:T(8,128)S(1)} custom-call(bf16[64,2048]{1,0:T(8,128)(2,1)S(1)} %total_3.1.refs_0_.refs_1_, bf16[64,2048]{1,0:T(8,128)(2,1)S(1)} %collective-permute-done.17.refs_1_, bf16[2048,1536]{1,0:T(8,128)(2,1)S(1)} %transposed_train.1.refs_2_.refs_1_, f32[64,1536]{1,0:T(8,128)S(1)} %gather_1_0.1.refs_3_.refs_0_), custom_call_target="tpu_custom_call" | custom-call | tf_op jit(solution)/shard_map/last_scores/pallas_call | solution.py:33
  51.2 0.9 %collective-permute-done.16.refs_1_ = bf16[64,1536]{1,0:T(8,128)(2,1)S(1)} collective-permute-done((bf16[64,1536]{1,0:T(8,128)(2,1)S(1)}, bf16[64,1536]{1,0:T(8,128)(2,1)S(1)}, u32[]{:S(2)}, u32[]{:S(2)}) %collective-permute-start.16) | collective-permute-done | bytes 196640 | tf_op jit(solution)/shard_map/ppermute | solution.py:67
  52.2 0.7 %copy.4 = f32[64,1536]{1,0:T(8,128)} copy(f32[64,1536]{1,0:T(8,128)S(1)} %close.1) | data formatting | bytes 786432
  (28 shorter events, 0.5 us)
Async XLA Ops:
  0.0 3.1 %collective-permute-start = (bf16[64,2048]{1,0:T(8,128)(2,1)}, bf16[64,2048]{1,0:T(8,128)(2,1)S(1)}, u32[]{:S(2)}, u32[]{:S(2)}) collective-permute-start(bf16[64,2048]{1,0:T(8,128)(2,1)} %refs_0_.2), channel_id=1, source_target_pairs={{0,1},{1,0},{2,3},{3,2},{4,5},{5,4},{6,7},{7,6},{8,9},{9,8},{10,11... | collective-permute-start | bytes 786440 | tf_op jit(solution)/shard_map/ppermute | solution.py:67
  0.5 9.9 %collective-permute-start.2 = (bf16[64,2048]{1,0:T(8,128)(2,1)}, bf16[64,2048]{1,0:T(8,128)(2,1)S(1)}, u32[]{:S(2)}, u32[]{:S(2)}) collective-permute-start(bf16[64,2048]{1,0:T(8,128)(2,1)} %refs_0_.2), channel_id=1, source_target_pairs={{0,3},{1,2},{2,1},{3,0},{4,7},{5,6},{6,5},{7,4},{8,11},{9,10},{10,... | collective-permute-start | bytes 786440 | tf_op jit(solution)/shard_map/ppermute | solution.py:67
  3.1 14.1 %collective-permute-start.6 = (bf16[64,2048]{1,0:T(8,128)(2,1)}, bf16[64,2048]{1,0:T(8,128)(2,1)S(1)}, u32[]{:S(2)}, u32[]{:S(2)}) collective-permute-start(bf16[64,2048]{1,0:T(8,128)(2,1)} %refs_0_.2), channel_id=1, source_target_pairs={{0,2},{1,3},{2,0},{3,1},{4,6},{5,7},{6,4},{7,5},{8,10},{9,11},{10,... | collective-permute-start | bytes 786440 | tf_op jit(solution)/shard_map/ppermute | solution.py:67
  5.6 8.5 %collective-permute-start.1 = (bf16[64,1024]{1,0:T(8,128)(2,1)S(1)}, bf16[64,1024]{1,0:T(8,128)(2,1)S(1)}, u32[]{:S(2)}, u32[]{:S(2)}) collective-permute-start(bf16[64,1024]{1,0:T(8,128)(2,1)S(1)} %get-tuple-element.9.refs_2_.refs_0_), channel_id=1, source_target_pairs={{0,4},{1,5},{2,6},{3,7},{4,0},{5,1},{6,2},{7,3},{8,12},{9,13},{10,... | collective-permute-start | bytes 393224 | tf_op jit(solution)/shard_map/ppermute | solution.py:64
  10.3 5.2 %collective-permute-start.3 = (bf16[64,1024]{1,0:T(8,128)(2,1)S(1)}, bf16[64,1024]{1,0:T(8,128)(2,1)S(1)}, u32[]{:S(2)}, u32[]{:S(2)}) collective-permute-start(bf16[64,1024]{1,0:T(8,128)(2,1)S(1)} %get-tuple-element.12.refs_3_.refs_1_), channel_id=1, source_target_pairs={{0,4},{1,5},{2,6},{3,7},{4,0},{5,1},{6,2},{7,3},{8,12},{9,13},{10,... | collective-permute-start | bytes 393224 | tf_op jit(solution)/shard_map/ppermute | solution.py:64
  12.0 3.6 %copy-start = (bf16[64,2048]{1,0:T(8,128)(2,1)S(1)}, bf16[64,2048]{1,0:T(8,128)(2,1)}, u32[]{:S(2)}) copy-start(bf16[64,2048]{1,0:T(8,128)(2,1)} %refs_0_.2) | copy-start | bytes 786436
  12.0 9.9 %collective-permute-start.5 = (bf16[64,2048]{1,0:T(8,128)(2,1)S(1)}, bf16[64,2048]{1,0:T(8,128)(2,1)S(1)}, u32[]{:S(2)}, u32[]{:S(2)}) collective-permute-start(bf16[64,2048]{1,0:T(8,128)(2,1)S(1)} %pass_1.1.refs_2_), channel_id=1, source_target_pairs={{0,4},{1,5},{2,6},{3,7},{4,0},{5,1},{6,2},{7,3},{8,12},{9,13},{10,... | collective-permute-start | bytes 786440 | tf_op jit(solution)/shard_map/ppermute | solution.py:64
  15.5 8.3 %collective-permute-start.4 = (bf16[64,2048]{1,0:T(8,128)(2,1)S(1)}, bf16[64,2048]{1,0:T(8,128)(2,1)S(1)}, u32[]{:S(2)}, u32[]{:S(2)}) collective-permute-start(bf16[64,2048]{1,0:T(8,128)(2,1)S(1)} %absorb_0b.1.refs_3_.refs_0_), channel_id=1, source_target_pairs={{0,1},{1,0},{2,3},{3,2},{4,8},{5,9},{6,10},{7,11},{8,4},{9,5},{10,... | collective-permute-start | bytes 786440 | tf_op jit(solution)/shard_map/ppermute | solution.py:64
  17.2 4.9 %slice-start = ((s8[6291456]{0:T(1024)(128)(4,1)}), s8[4194304]{0:T(1024)(128)(4,1)S(1)}, s32[]{:S(2)}) async-start(s8[6291456]{0:T(1024)(128)(4,1)} %bitcast), calls=%async_computation | async-start | bytes 8388608
  18.7 3.3 %slice-start.1 = ((s8[6291456]{0:T(1024)(128)(4,1)}), s8[2097152]{0:T(1024)(128)(4,1)S(1)}, s32[]{:S(2)}) async-start(s8[6291456]{0:T(1024)(128)(4,1)} %bitcast), calls=%async_computation.1 | async-start | bytes 4194304
  18.8 9.2 %collective-permute-start.9 = (bf16[64,2048]{1,0:T(8,128)(2,1)S(1)}, bf16[64,2048]{1,0:T(8,128)(2,1)S(1)}, u32[]{:S(2)}, u32[]{:S(2)}) collective-permute-start(bf16[64,2048]{1,0:T(8,128)(2,1)S(1)} %pass_2.1.refs_2_), channel_id=1, source_target_pairs={{0,4},{1,5},{2,6},{3,7},{4,0},{5,1},{6,2},{7,3},{8,12},{9,13},{10,... | collective-permute-start | bytes 786440 | tf_op jit(solution)/shard_map/ppermute | solution.py:64
  22.0 6.2 %collective-permute-start.8 = (bf16[64,2048]{1,0:T(8,128)(2,1)S(1)}, bf16[64,2048]{1,0:T(8,128)(2,1)S(1)}, u32[]{:S(2)}, u32[]{:S(2)}) collective-permute-start(bf16[64,2048]{1,0:T(8,128)(2,1)S(1)} %absorb_1.1.refs_1_.refs_0_), channel_id=1, source_target_pairs={{0,1},{1,0},{2,3},{3,2},{4,8},{5,9},{6,10},{7,11},{8,4},{9,5},{10,... | collective-permute-start | bytes 786440 | tf_op jit(solution)/shard_map/ppermute | solution.py:64
  23.9 9.8 %collective-permute-start.7 = (bf16[64,2048]{1,0:T(8,128)(2,1)S(1)}, bf16[64,2048]{1,0:T(8,128)(2,1)S(1)}, u32[]{:S(2)}, u32[]{:S(2)}) collective-permute-start(bf16[64,2048]{1,0:T(8,128)(2,1)S(1)} %merge_3.1.refs_2_), channel_id=1, source_target_pairs={{0,4},{1,5},{2,6},{3,7},{4,0},{5,1},{6,2},{7,3},{8,12},{9,13},{10,... | collective-permute-start | bytes 786440 | tf_op jit(solution)/shard_map/ppermute | solution.py:64
  28.1 7.5 %collective-permute-start.11 = (bf16[64,2048]{1,0:T(8,128)(2,1)S(1)}, bf16[64,2048]{1,0:T(8,128)(2,1)S(1)}, u32[]{:S(2)}, u32[]{:S(2)}) collective-permute-start(bf16[64,2048]{1,0:T(8,128)(2,1)S(1)} %absorb_2.1.refs_2_.refs_0_), channel_id=1, source_target_pairs={{0,1},{1,0},{2,3},{3,2},{4,8},{5,9},{6,10},{7,11},{8,4},{9,5},{10,... | collective-permute-start | bytes 786440 | tf_op jit(solution)/shard_map/ppermute | solution.py:64
  28.3 10.5 %collective-permute-start.14 = (bf16[64,2048]{1,0:T(8,128)(2,1)S(1)}, bf16[64,2048]{1,0:T(8,128)(2,1)S(1)}, u32[]{:S(2)}, u32[]{:S(2)}) collective-permute-start(bf16[64,2048]{1,0:T(8,128)(2,1)S(1)} %back_4.1.refs_2_), channel_id=1, source_target_pairs={{0,4},{1,5},{2,6},{3,7},{4,0},{5,1},{6,2},{7,3},{8,12},{9,13},{10,... | collective-permute-start | bytes 786440 | tf_op jit(solution)/shard_map/ppermute | solution.py:64
  33.7 6.9 %collective-permute-start.13 = (bf16[64,2048]{1,0:T(8,128)(2,1)S(1)}, bf16[64,2048]{1,0:T(8,128)(2,1)S(1)}, u32[]{:S(2)}, u32[]{:S(2)}) collective-permute-start(bf16[64,2048]{1,0:T(8,128)(2,1)S(1)} %absorb_3.1.refs_2_.refs_0_), channel_id=1, source_target_pairs={{0,1},{1,0},{2,3},{3,2},{4,8},{5,9},{6,10},{7,11},{8,4},{9,5},{10,... | collective-permute-start | bytes 786440 | tf_op jit(solution)/shard_map/ppermute | solution.py:64
  35.1 12.6 %collective-permute-start.10 = (bf16[64,1536]{1,0:T(8,128)(2,1)S(1)}, bf16[64,1536]{1,0:T(8,128)(2,1)S(1)}, u32[]{:S(2)}, u32[]{:S(2)}) collective-permute-start(bf16[64,1536]{1,0:T(8,128)(2,1)S(1)} %scores_0_0.1.refs_2_), channel_id=1, source_target_pairs={{0,1},{1,0},{2,3},{3,2},{4,5},{5,4},{6,7},{7,6},{8,9},{9,8},{10,11... | collective-permute-start | bytes 589832 | tf_op jit(solution)/shard_map/ppermute | solution.py:67
  35.7 8.7 %collective-permute-start.12 = (bf16[64,2048]{1,0:T(8,128)(2,1)S(1)}, bf16[64,2048]{1,0:T(8,128)(2,1)S(1)}, u32[]{:S(2)}, u32[]{:S(2)}) collective-permute-start(bf16[64,2048]{1,0:T(8,128)(2,1)S(1)} %back_5.1.refs_2_), channel_id=1, source_target_pairs={{0,4},{1,5},{2,6},{3,7},{4,0},{5,1},{6,2},{7,3},{8,12},{9,13},{10,... | collective-permute-start | bytes 786440 | tf_op jit(solution)/shard_map/ppermute | solution.py:64
  40.0 7.6 %collective-permute-start.15 = (bf16[64,1536]{1,0:T(8,128)(2,1)S(1)}, bf16[64,1536]{1,0:T(8,128)(2,1)S(1)}, u32[]{:S(2)}, u32[]{:S(2)}) collective-permute-start(bf16[64,1536]{1,0:T(8,128)(2,1)S(1)} %scores_1_0.1.refs_2_), channel_id=1, source_target_pairs={{0,3},{1,2},{2,1},{3,0},{4,7},{5,6},{6,5},{7,4},{8,11},{9,10},{10,... | collective-permute-start | bytes 589832 | tf_op jit(solution)/shard_map/ppermute | solution.py:67
  40.7 9.3 %collective-permute-start.17 = (bf16[64,2048]{1,0:T(8,128)(2,1)S(1)}, bf16[64,2048]{1,0:T(8,128)(2,1)S(1)}, u32[]{:S(2)}, u32[]{:S(2)}) collective-permute-start(bf16[64,2048]{1,0:T(8,128)(2,1)S(1)} %back_6.1.refs_2_), channel_id=1, source_target_pairs={{0,4},{1,5},{2,6},{3,7},{4,0},{5,1},{6,2},{7,3},{8,12},{9,13},{10,... | collective-permute-start | bytes 786440 | tf_op jit(solution)/shard_map/ppermute | solution.py:64
  45.6 6.5 %collective-permute-start.16 = (bf16[64,1536]{1,0:T(8,128)(2,1)S(1)}, bf16[64,1536]{1,0:T(8,128)(2,1)S(1)}, u32[]{:S(2)}, u32[]{:S(2)}) collective-permute-start(bf16[64,1536]{1,0:T(8,128)(2,1)S(1)} %scores_2_0.1.refs_1_), channel_id=1, source_target_pairs={{0,2},{1,3},{2,0},{3,1},{4,6},{5,7},{6,4},{7,5},{8,10},{9,11},{10,... | collective-permute-start | bytes 589832 | tf_op jit(solution)/shard_map/ppermute | solution.py:67
